TPU v7x, 128 devices: a whole 4x4x4 slice. The times are simulated.
128 devices in a mesh: gx: 8 (over y, core), gy: 16 (over x, z).
Axes of the slice: x: 4, y: 4, z: 4, core: 2. Of those that a mesh axis runs over, the one named last changes fastest.
Arguments:
- eps_field: bfloat16 [48, 512, 2048], P(None, 'gx', 'gy'), may hold values from 1 to 10
- charge: float32 [48, 512, 2048], P(None, 'gx', 'gy'), may hold values from -6 to 6
- potential_start: float32 [48, 512, 2048], P(None, 'gx', 'gy'), may hold values from -3 to 3
- colloid_vel: float32 [3, 4096], P(None, ('gx', 'gy')), may hold values from -0.3 to 0.3
- colloid_spin: float32 [3, 4096], P(None, ('gx', 'gy')), may hold values from -0.06 to 0.06
- link_dir: int32 [8, 16, 32768], P('gx', 'gy'), may hold values from 0 to 17
- link_colloid: int32 [8, 16, 32768], P('gx', 'gy'), may hold values from -1 to 4095, as said below
- link_site: int32 [8, 16, 32768], P('gx', 'gy'), may hold values from 0 to 8191
- link_depth: int32 [8, 16, 32768], P('gx', 'gy'), may hold values from 0 to 47
- link_pop: float32 [8, 16, 32768], P('gx', 'gy'), may hold values from -0.1 to 0.1
- link_rb: float32 [3, 8, 16, 32768], P(None, 'gx', 'gy'), may hold values from -9 to 9
Outputs:
- potential: float32 [48, 512, 2048], P(None, 'gx', 'gy')
- force_torque: float32 [6, 4096], P(None, ('gx', 'gy'))
- link_out: float32 [8, 16, 32768], P('gx', 'gy')
Inputs may be any that keep to these rules, and one draw needn't show every extreme that they name: `link_colloid`: an empty slot holds -1 and the live slots of a tile come first; at least 16384 slots of every tile are live and every slot of at least one tile. The tile with index i along gx and j along gy owns the colloids (i n + j) * 32 up to (i n + j + 1) * 32 - 1, where n is the number of tiles along gy; a live slot names a colloid owned by its own tile or by one of the eight tiles beside it, wrapping around.
All inputs are finite; a program needn't handle non-finite values.
Results may differ from a plain program's by a relative error of at most 0.0003.
Values may be sent and summed in bfloat16 or wider, within the bound.
A program may use at most 128 MiB of HBM per device.

v0:
```python
import math

import jax
import jax.numpy as jnp
import numpy as np
from jax import lax
from jax.sharding import PartitionSpec as P

SWEEPS = 6
RADIUS = 8


velocity_table = np.array(
    [
        [1, 0, 0],
        [-1, 0, 0],
        [0, 1, 0],
        [0, -1, 0],
        [0, 0, 1],
        [0, 0, -1],
        [1, 1, 0],
        [1, -1, 0],
        [-1, 1, 0],
        [-1, -1, 0],
        [1, 0, 1],
        [1, 0, -1],
        [-1, 0, 1],
        [-1, 0, -1],
        [0, 1, 1],
        [0, 1, -1],
        [0, -1, 1],
        [0, -1, -1],
    ],
    dtype=np.float32,
).T
weight_table = np.array([1.0 / 18.0] * 6 + [1.0 / 36.0] * 12, dtype=np.float32)
OVER_RELAX = 1.6
BLOCK_LINKS = 8192


def padded_2(block, sides, width):
    for axis, dim in sides:
        count = lax.axis_size(axis)
        forward = [(i, i + 1) for i in range(count - 1)]
        forward.append((count - 1, 0))
        backward = [(target, source) for source, target in forward]
        low = lax.ppermute(
            lax.slice_in_dim(block, block.shape[dim] - width, None, axis=dim), axis, forward
        )
        high = lax.ppermute(lax.slice_in_dim(block, 0, width, axis=dim), axis, backward)
        block = jnp.concatenate([low, block, high], axis=dim)
    return block


def lattice_lookup(directions):
    onehot = (directions[None, :] == jnp.arange(18, dtype=jnp.int32)[:, None]).astype(jnp.float32)
    velocity = jnp.dot(
        jnp.asarray(velocity_table).astype(jnp.float32), onehot, precision=lax.Precision.HIGHEST
    )
    weight = jnp.dot(
        jnp.asarray(weight_table).astype(jnp.float32)[None, :],
        onehot,
        precision=lax.Precision.HIGHEST,
    )[0]
    return (velocity, weight)


def cross_product(first, second):
    return jnp.stack(
        [
            first[1] * second[2] - first[2] * second[1],
            first[2] * second[0] - first[0] * second[2],
            first[0] * second[1] - first[1] * second[0],
        ]
    )


def link_terms(pops, velocity, weight, valid, offsets, at_links, pressure):
    boundary = at_links[0:3] + cross_product(at_links[3:6], offsets)
    along = jnp.sum(velocity * boundary, axis=0)
    transfer = (2.0 * pops - 6.0 * weight * along + weight * pressure) * valid
    force = velocity * transfer[None, :]
    torque = cross_product(offsets, force)
    return jnp.concatenate([force, torque], axis=0)


def reflected(pops, velocity, weight, valid, offsets, at_links):
    boundary = at_links[0:3] + cross_product(at_links[3:6], offsets)
    along = jnp.sum(velocity * boundary, axis=0)
    return pops - 6.0 * weight * along * valid


def owner_update(motion, sums):
    mass = 4.0 / 3.0 * math.pi * RADIUS**3
    inertia = 0.4 * mass * RADIUS**2
    new_motion = jnp.concatenate(
        [motion[0:3] + sums[0:3] / mass, motion[3:6] + sums[3:6] / inertia], axis=0
    )
    report = jnp.concatenate([sums[0:3], sums[3:6] / RADIUS], axis=0)
    return (new_motion, report)


def relax_colour(phi_pad, eps_pad, charge, colour_mask):
    eps_slab = jnp.pad(eps_pad, ((1, 1), (0, 0), (0, 0)), mode="edge")
    padded = jnp.pad(phi_pad, ((1, 1), (0, 0), (0, 0)))
    eps_centre = eps_slab[1:-1, 1:-1, 1:-1]
    centre = padded[1:-1, 1:-1, 1:-1]
    eps_sides = [
        eps_slab[:-2, 1:-1, 1:-1],
        eps_slab[2:, 1:-1, 1:-1],
        eps_slab[1:-1, :-2, 1:-1],
        eps_slab[1:-1, 2:, 1:-1],
        eps_slab[1:-1, 1:-1, :-2],
        eps_slab[1:-1, 1:-1, 2:],
    ]
    phi_sides = [
        padded[:-2, 1:-1, 1:-1],
        padded[2:, 1:-1, 1:-1],
        padded[1:-1, :-2, 1:-1],
        padded[1:-1, 2:, 1:-1],
        padded[1:-1, 1:-1, :-2],
        padded[1:-1, 1:-1, 2:],
    ]
    numerator = charge
    denominator = jnp.zeros_like(charge)
    for eps_side, phi_side in zip(eps_sides, phi_sides):
        face = 0.5 * (eps_centre + eps_side)
        numerator = numerator + face * phi_side
        denominator = denominator + face
    target = numerator / denominator
    return jnp.where(colour_mask, centre + OVER_RELAX * (target - centre), centre)


def parity_of(shape):
    return (
        lax.broadcasted_iota(jnp.int32, shape, 0)
        + lax.broadcasted_iota(jnp.int32, shape, 1)
        + lax.broadcasted_iota(jnp.int32, shape, 2)
    ) % 2


def slot_table(slots, width):
    return (slots[None, :] == jnp.arange(width, dtype=jnp.int32)[:, None]).astype(jnp.float32)


def into_blocks(values, block_size):
    lead = values.shape[0]
    count = values.shape[1] // block_size
    return values.reshape(lead, count, block_size).transpose(1, 0, 2)


def near_sums(table_rows, slots, pops, velocity, weight, valid, offsets, pressure, block_size):
    width = table_rows.shape[0]
    table_cols = table_rows.T

    def add_block(total, inputs):
        slot_b, pops_b, vel_b, weight_b, valid_b, off_b, press_b = inputs
        onehot = slot_table(slot_b, width)
        at_links = jnp.dot(table_cols, onehot, precision=lax.Precision.HIGHEST)
        terms = link_terms(pops_b, vel_b, weight_b, valid_b, off_b, at_links, press_b)
        partial_value = lax.dot_general(
            terms, onehot, (((1,), (1,)), ((), ())), precision=lax.Precision.HIGHEST
        )
        return (total + partial_value, jnp.zeros((), jnp.float32))

    inputs = (
        slots.reshape(-1, block_size),
        pops.reshape(-1, block_size),
        into_blocks(velocity, block_size),
        weight.reshape(-1, block_size),
        valid.reshape(-1, block_size),
        into_blocks(offsets, block_size),
        pressure.reshape(-1, block_size),
    )
    total = lax.scan(add_block, jnp.zeros((6, width), jnp.float32), inputs)[0]
    return total.T


def near_reflect(table_rows, slots, pops, velocity, weight, valid, offsets, block_size):
    width = table_rows.shape[0]
    table_cols = table_rows.T

    def one_block(inputs):
        slot_b, pops_b, vel_b, weight_b, valid_b, off_b = inputs
        onehot = slot_table(slot_b, width)
        at_links = jnp.dot(table_cols, onehot, precision=lax.Precision.HIGHEST)
        return reflected(pops_b, vel_b, weight_b, valid_b, off_b, at_links)

    inputs = (
        slots.reshape(-1, block_size),
        pops.reshape(-1, block_size),
        into_blocks(velocity, block_size),
        weight.reshape(-1, block_size),
        valid.reshape(-1, block_size),
        into_blocks(offsets, block_size),
    )
    return lax.map(one_block, inputs).reshape(-1)


def shards(
    eps_field,
    charge,
    potential_start,
    colloid_vel,
    colloid_spin,
    link_dir,
    link_colloid,
    link_site,
    link_depth,
    link_pop,
    link_rb,
):
    potential = potential_start
    parity = parity_of(charge.shape)
    eps_pad = padded_2(eps_field, (("gx", 1), ("gy", 2)), 1).astype(jnp.float32)
    for sweep_index in range(SWEEPS):
        for colour in (0, 1):
            phi_pad = padded_2(potential, (("gx", 1), ("gy", 2)), 1)
            potential = relax_colour(phi_pad, eps_pad, charge, parity == colour)
    per_tile = colloid_vel.shape[1]
    lateral = charge.shape[1] * charge.shape[2]
    motion = jnp.concatenate([colloid_vel, colloid_spin], axis=0)
    motion_rows = motion.T
    directions = link_dir.reshape(-1)
    colloid_ids = link_colloid.reshape(-1)
    sites = link_depth.reshape(-1) * lateral + link_site.reshape(-1)
    pops = link_pop.reshape(-1)
    offsets = link_rb.reshape(3, -1)
    link_count = pops.shape[0]
    block_size = min(link_count, BLOCK_LINKS)
    velocity, weight = lattice_lookup(directions)
    valid_mask = colloid_ids >= 0
    valid = valid_mask.astype(jnp.float32)
    phi_here = jnp.take(potential.reshape(-1), sites)
    pressure = (
        0.5 * jnp.take(eps_field.reshape(-1), sites).astype(jnp.float32) * phi_here * phi_here
    )
    count_x = lax.axis_size("gx")
    count_y = lax.axis_size("gy")
    home_x = lax.axis_index("gx")
    home_y = lax.axis_index("gy")
    owner_tile = colloid_ids // per_tile
    near_x = (owner_tile // count_y - home_x + 1) % count_x
    near_y = (owner_tile % count_y - home_y + 1) % count_y
    slots = jnp.where(valid_mask, (near_x * 3 + near_y) * per_tile + colloid_ids % per_tile, -1)
    beside_all = padded_2(motion_rows.reshape(1, 1, per_tile, 6), (("gx", 0), ("gy", 1)), 1)
    partial_value = near_sums(
        beside_all.reshape(9 * per_tile, 6),
        slots,
        pops,
        velocity,
        weight,
        valid,
        offsets,
        pressure,
        block_size,
    )
    blocks = partial_value.reshape(3, 3, per_tile, 6)
    framed = padded_2(blocks, (("gx", 0), ("gy", 1)), 1)
    sums_rows = (
        blocks[1, 1]
        + framed[0, 0]
        + framed[0, 2]
        + framed[0, 4]
        + framed[2, 0]
        + framed[2, 4]
        + framed[4, 0]
        + framed[4, 2]
        + framed[4, 4]
    )
    new_motion, report = owner_update(motion, sums_rows.T)
    around_new = padded_2(new_motion.T.reshape(1, 1, per_tile, 6), (("gx", 0), ("gy", 1)), 1)
    table_new = around_new.reshape(9 * per_tile, 6)
    link_out = near_reflect(
        table_new, slots, pops, velocity, weight, valid, offsets, block_size
    ).reshape(link_pop.shape)
    return (potential, report, link_out)


def solution(mesh):
    placed = (
        P(None, "gx", "gy"),
        P(None, "gx", "gy"),
        P(None, "gx", "gy"),
        P(None, ("gx", "gy")),
        P(None, ("gx", "gy")),
        P("gx", "gy", None),
        P("gx", "gy", None),
        P("gx", "gy", None),
        P("gx", "gy", None),
        P("gx", "gy", None),
        P(None, "gx", "gy", None),
    )
    return jax.shard_map(
        shards,
        mesh=mesh,
        in_specs=placed,
        out_specs=(P(None, "gx", "gy"), P(None, ("gx", "gy")), P("gx", "gy", None)),
        check_vma=False,
    )
```

profile of v0, /device:TPU:0, one launch (start us, length us, event | category | flops | bytes accessed | tf_op | source)
XLA Modules:
  0.0 932.0 jit_solution(11790147928939617633)
XLA Ops:
  31.5 5.7 collective-permute-start.7
  42.0 6.0 select_maximum_fusion.44
  47.9 25.6 %add_select_fusion.11 = (f32[48,64,128]{2,1,0:T(8,128)}, f32[48,64,128]{2,1,0:T(8,128)}, f32[48,64,128]{2,1,0:T(8,128)}, f32[48,64,128]{2,1,0:T(8,128)}, f32[48,...) fusion(f32[48,64,128]{2,1,0:T(8,128)} %param.19, f32[48,66,1]{2,1,0:T(8,128)} %copy.63, ...), kind=kLoop, calls=%fused_computation.112 | loop fusion | flops 22806528 | bytes 32361504 | tf_op jit(solution)/shard_map/jit(_where)/select_n | solution.py:131
  87.3 5.9 collective-permute-start.11
  101.8 8.1 add_select_fusion.10
  135.3 8.1 add_select_fusion.9
  169.0 8.1 add_select_fusion.8
  188.5 5.6 collective-permute-start.23
  202.7 8.1 add_select_fusion.7
  236.2 8.1 add_select_fusion.6
  269.9 8.1 add_select_fusion.5
  291.0 5.8 collective-permute-start.35
  307.2 8.1 add_select_fusion.4
  344.1 8.1 add_select_fusion.3
  363.6 5.6 collective-permute-start.43
  379.7 8.1 add_select_fusion.2
  399.6 5.8 collective-permute-start.47
  405.8 201.3 %gather_fusion = bf16[32768]{0:T(1024)(128)(2,1)S(1)} fusion(bf16[393216]{0:T(1024)(128)(2,1)S(1)} %bitcast.143, s32[32768]{0:T(1024)S(1)} %broadcast_clamp_fusion), kind=kCustom, calls=%fused_computation | custom fusion | bytes 262144 | tf_op jit(solution)/shard_map/jit(_take)/gather | solution.py:236
  623.6 8.1 add_select_fusion.1
  666.0 8.1 add_select_fusion
  674.2 180.8 %gather_fusion.1 = f32[32768]{0:T(1024)S(1)} fusion(f32[393216]{0:T(1024)S(1)} %bitcast.142, s32[32768]{0:T(1024)} %copy-done.74), kind=kCustom, calls=%fused_computation.1 | custom fusion | bytes 393216 | tf_op jit(solution)/shard_map/jit(_take)/gather | solution.py:234
  856.1 35.1 %while.22 = (s32[]{:T(128)}, f32[6,288]{1,0:T(8,128)S(1)}, f32[4,3,8192]{2,1,0:T(4,128)S(1)}, f32[4,8192]{1,0:T(4,128)S(1)}, f32[4,8192]{1,0:T(4,128)S(1)}, /*in...) while((s32[]{:T(128)}, f32[6,288]{1,0:T(8,128)S(1)}, ...), condition=%wide.region_2.3_spmd.clone, body=%wide.region_0.2_spmd.clone.sunk | while | flops 344952192 | bytes 1888719 | solution.py:175
  907.4 5.7 collective-permute-start.63
  914.8 16.1 %while.21 = (s32[]{:T(128)}, f32[4,8192]{1,0:T(4,128)S(1)}, f32[4,8192]{1,0:T(4,128)S(1)}, f32[4,8192]{1,0:T(4,128)S(1)}, f32[4,3,8192]{2,1,0:T(4,128)S(1)}, /*i...) while((s32[]{:T(128)}, f32[4,8192]{1,0:T(4,128)S(1)}, ...), condition=%wide.region_5.6_spmd, body=%wide.region_3.5_spmd.sunk | while | flops 172449792 | bytes 1153969 | solution.py:197
  (517 shorter events, 385.6 us)
Async XLA Ops:
  10.6 9.9 %collective-permute-start.2 = (bf16[48,66,1]{1,0,2:T(8,128)(2,1)S(1)}, bf16[48,66,1]{1,0,2:T(8,128)(2,1)S(1)}, u32[]{:S(2)}, u32[]{:S(2)}) collective-permute-start(bf16[48,66,1]{1,0,2:T(8,128)(2,1)S(1)} %copy.56), channel_id=1, source_target_pairs={{0,1},{1,2},{2,3},{3,4},{4,5},{5,6},{6,7},{7,8},{8,9},{9,10},{10,1... | collective-permute-start | bytes 19016 | tf_op jit(solution)/shard_map/ppermute | solution.py:47
  13.1 7.9 collective-permute-start.3
  17.5 9.2 collective-permute-start.4
  17.7 9.0 collective-permute-start.5
  31.5 8.6 collective-permute-start.7
  85.2 8.0 collective-permute-start.10
  87.3 7.8 collective-permute-start.11
  253.6 7.8 collective-permute-start.30
  281.1 353.7 %collective-permute-start.52 = (f32[1,1,32,6]{2,3,1,0:T(8,128)S(1)}, f32[1,1,32,6]{2,3,1,0:T(8,128)}, u32[]{:S(2)}, u32[]{:S(2)}) collective-permute-start(f32[1,1,32,6]{2,3,1,0:T(8,128)S(1)} %maximum_bitcast_fusion), channel_id=1, source_target_pairs={{0,16},{16,32},{32,48},{48,64},{64,80},{80,96},{96,112},{112,0},{1... | collective-permute-start | bytes 2312 | tf_op jit(solution)/shard_map/ppermute | solution.py:47
  281.2 353.6 %collective-permute-start.53 = (f32[1,1,32,6]{2,3,1,0:T(8,128)S(1)}, f32[1,1,32,6]{2,3,1,0:T(8,128)}, u32[]{:S(2)}, u32[]{:S(2)}) collective-permute-start(f32[1,1,32,6]{2,3,1,0:T(8,128)S(1)} %maximum_bitcast_fusion), channel_id=1, source_target_pairs={{16,0},{32,16},{48,32},{64,48},{80,64},{96,80},{112,96},{0,112},{1... | collective-permute-start | bytes 2312 | tf_op jit(solution)/shard_map/ppermute | solution.py:50
  288.9 9.7 %collective-permute-start.34 = (f32[48,66,1]{1,0,2:T(8,128)S(1)}, f32[48,66,1]{1,0,2:T(8,128)S(1)}, u32[]{:S(2)}, u32[]{:S(2)}) collective-permute-start(f32[48,66,1]{1,0,2:T(8,128)S(1)} %copy.102), channel_id=1, source_target_pairs={{0,1},{1,2},{2,3},{3,4},{4,5},{5,6},{6,7},{7,8},{8,9},{9,10},{10,1... | collective-permute-start | bytes 38024 | tf_op jit(solution)/shard_map/ppermute | solution.py:47
  291.0 9.5 %collective-permute-start.35 = (f32[48,66,1]{1,0,2:T(8,128)S(1)}, f32[48,66,1]{1,0,2:T(8,128)S(1)}, u32[]{:S(2)}, u32[]{:S(2)}) collective-permute-start(f32[48,66,1]{1,0,2:T(8,128)S(1)} %copy.103), channel_id=1, source_target_pairs={{1,0},{2,1},{3,2},{4,3},{5,4},{6,5},{7,6},{8,7},{9,8},{10,9},{11,1... | collective-permute-start | bytes 38024 | tf_op jit(solution)/shard_map/ppermute | solution.py:50
  327.1 8.4 collective-permute-start.38
  329.2 8.2 collective-permute-start.39
  361.5 9.6 %collective-permute-start.42 = (f32[48,66,1]{1,0,2:T(8,128)S(1)}, f32[48,66,1]{1,0,2:T(8,128)S(1)}, u32[]{:S(2)}, u32[]{:S(2)}) collective-permute-start(f32[48,66,1]{1,0,2:T(8,128)S(1)} %copy.114), channel_id=1, source_target_pairs={{0,1},{1,2},{2,3},{3,4},{4,5},{5,6},{6,7},{7,8},{8,9},{9,10},{10,1... | collective-permute-start | bytes 38024 | tf_op jit(solution)/shard_map/ppermute | solution.py:47
  363.6 9.4 %collective-permute-start.43 = (f32[48,66,1]{1,0,2:T(8,128)S(1)}, f32[48,66,1]{1,0,2:T(8,128)S(1)}, u32[]{:S(2)}, u32[]{:S(2)}) collective-permute-start(f32[48,66,1]{1,0,2:T(8,128)S(1)} %copy.115), channel_id=1, source_target_pairs={{1,0},{2,1},{3,2},{4,3},{5,4},{6,5},{7,6},{8,7},{9,8},{10,9},{11,1... | collective-permute-start | bytes 38024 | tf_op jit(solution)/shard_map/ppermute | solution.py:50
  397.4 216.7 %collective-permute-start.46 = (f32[48,66,1]{1,0,2:T(8,128)S(1)}, f32[48,66,1]{1,0,2:T(8,128)S(1)}, u32[]{:S(2)}, u32[]{:S(2)}) collective-permute-start(f32[48,66,1]{1,0,2:T(8,128)S(1)} %copy.120), channel_id=1, source_target_pairs={{0,1},{1,2},{2,3},{3,4},{4,5},{5,6},{6,7},{7,8},{8,9},{9,10},{10,1... | collective-permute-start | bytes 38024 | tf_op jit(solution)/shard_map/ppermute | solution.py:47
  399.6 216.5 %collective-permute-start.47 = (f32[48,66,1]{1,0,2:T(8,128)S(1)}, f32[48,66,1]{1,0,2:T(8,128)}, u32[]{:S(2)}, u32[]{:S(2)}) collective-permute-start(f32[48,66,1]{1,0,2:T(8,128)S(1)} %copy.121), channel_id=1, source_target_pairs={{1,0},{2,1},{3,2},{4,3},{5,4},{6,5},{7,6},{8,7},{9,8},{10,9},{11,1... | collective-permute-start | bytes 38024 | tf_op jit(solution)/shard_map/ppermute | solution.py:50
  631.8 9.0 collective-permute-start.48
  631.9 9.0 collective-permute-start.49
  635.5 19.1 %collective-permute-start.54 = (f32[3,1,32,6]{2,3,1,0:T(8,128)S(1)}, f32[3,1,32,6]{2,3,1,0:T(8,128)S(1)}, u32[]{:S(2)}, u32[]{:S(2)}) collective-permute-start(f32[3,1,32,6]{2,3,1,0:T(8,128)S(1)} %pad_maximum_fusion.113), channel_id=1, source_target_pairs={{0,1},{1,2},{2,3},{3,4},{4,5},{5,6},{6,7},{7,8},{8,9},{9,10},{10,1... | collective-permute-start | bytes 6920 | tf_op jit(solution)/shard_map/ppermute | solution.py:47
  635.5 19.1 %collective-permute-start.55 = (f32[3,1,32,6]{2,3,1,0:T(8,128)S(1)}, f32[3,1,32,6]{2,3,1,0:T(8,128)S(1)}, u32[]{:S(2)}, u32[]{:S(2)}) collective-permute-start(f32[3,1,32,6]{2,3,1,0:T(8,128)S(1)} %pad_maximum_fusion.113), channel_id=1, source_target_pairs={{1,0},{2,1},{3,2},{4,3},{5,4},{6,5},{7,6},{8,7},{9,8},{10,9},{11,1... | collective-permute-start | bytes 6920 | tf_op jit(solution)/shard_map/ppermute | solution.py:50
  646.5 9.5 %collective-permute-start.50 = (f32[48,66,1]{1,0,2:T(8,128)}, f32[48,66,1]{1,0,2:T(8,128)}, u32[]{:S(2)}, u32[]{:S(2)}) collective-permute-start(f32[48,66,1]{1,0,2:T(8,128)} %copy.126), channel_id=1, source_target_pairs={{0,1},{1,2},{2,3},{3,4},{4,5},{5,6},{6,7},{7,8},{8,9},{9,10},{10,1... | collective-permute-start | bytes 38024 | tf_op jit(solution)/shard_map/ppermute | solution.py:47
  649.2 9.5 %collective-permute-start.51 = (f32[48,66,1]{1,0,2:T(8,128)}, f32[48,66,1]{1,0,2:T(8,128)}, u32[]{:S(2)}, u32[]{:S(2)}) collective-permute-start(f32[48,66,1]{1,0,2:T(8,128)} %copy.127), channel_id=1, source_target_pairs={{1,0},{2,1},{3,2},{4,3},{5,4},{6,5},{7,6},{8,7},{9,8},{10,9},{11,1... | collective-permute-start | bytes 38024 | tf_op jit(solution)/shard_map/ppermute | solution.py:50
  (135 other events, 1730.6 us)
where the time goes:
time: 940 us; the launch traced here: 932 us
  local copies, waits for them, and re-layouts  529 us (56%)
  other arithmetic  196 us (21%)
  starting transfers between devices  138 us (15%)
  matrix products  46.9 us (5%)
  waiting for transfers between devices  19.2 us (2%)
    gather x2, local copies, waits for them, and re-layouts, shards(): jnp.take(eps_field.reshape(-1), sites).astype(jnp.float32)  202 us
    gather x2, local copies, waits for them, and re-layouts, shards(): phi_here = jnp.take(potential.reshape(-1), sites)  181 us
    ppermute x32, starting transfers between devices, padded_2(): lax.ppermute(lax.slice_in_dim(block, 0, width, axis=dim), axis, backward)  135 us
    select_n x12, other arithmetic, relax_colour(): jnp.where(colour_mask, centre + OVER_RELAX * (target - centre), centre)  115 us
    concatenate x29, other arithmetic, padded_2(): block = jnp.concatenate([low, block, high], axis=dim)  64.5 us
    slice x41, local copies, waits for them, and re-layouts, padded_2(): lax.slice_in_dim(block, block.shape[dim] - width, None, axis=dim)  59.1 us
    ppermute x13, local copies, waits for them, and re-layouts, padded_2(): lax.ppermute(lax.slice_in_dim(block, 0, width, axis=dim), axis, backward)  25.4 us
    slice x15, local copies, waits for them, and re-layouts, padded_2(): lax.slice_in_dim(block, 0, width, axis=dim)  24.7 us
  transfers between devices with their start and end apart: 64, of which 15 were waited for; matrix products, arithmetic and copies ran while one was open for 38% of the time, Pallas kernels for 0%

commit v1 on v0

v1 whole, which is shorter than its diff:
```python
import math

import jax
import jax.numpy as jnp
import numpy as np
from jax import lax
from jax.experimental import pallas as pl
from jax.experimental.pallas import tpu as pltpu
from jax.sharding import PartitionSpec as P

TILES_X, TILES_Y = 8, 16
NC_DEV = 32
LINKS = 32768
RADIUS = 8
SWEEPS=6
OVER_RELAX=1.6
NZ, TX, TY = 48, 64, 128
HALF = NZ//2
ROWS = 112
TOP = 24
LANES = 256
DEPTH = 2*SWEEPS

def parity_mask(colour, shape):
    s = lax.broadcasted_iota(jnp.int32, shape, 0) + lax.broadcasted_iota(jnp.int32, shape, 1)
    return (s + colour) % 2 == 0

def relax_kernel(eps_ref, charge_ref, phi_ref, pot_ref, q_ref, p_refs, e_refs, c_refs, coef_refs):
    even = parity_mask(0, (8, LANES))
    lane = lax.broadcasted_iota(jnp.int32, (8, LANES), 1)
    inside = (lane < TY + 16) | (lane >= LANES - 16)
    zero = jnp.zeros((8, LANES), jnp.float32)
    for ref in (*p_refs, *e_refs):
        for g in (0, ROWS - 8):
            def clear(m, _):
                ref[m, g:g + 8, :] = zero
                return 0
            lax.fori_loop(0, HALF + 2, clear, 0)
    for ref in p_refs:
        for g in range(0, ROWS, 8):
            ref[0, g:g + 8, :] = zero
            ref[HALF + 1, g:g + 8, :] = zero

    def compact(m, _):
        for r in range(0, ROWS - 16, 16):
            a = eps_ref[2 * m, r:r + 16, :].astype(jnp.float32)
            b = eps_ref[2 * m + 1, r:r + 16, :].astype(jnp.float32)
            for h in (0, 8):
                a1, b1 = a[h:h + 8], b[h:h + 8]
                e_refs[0][m + 1, r + 8 + h:r + 16 + h, :] = jnp.where(even, a1, b1)
                e_refs[1][m + 1, r + 8 + h:r + 16 + h, :] = jnp.where(even, b1, a1)
        for r in range(0, ROWS - 16, 8):
            a = phi_ref[2 * m, r:r + 8, :]
            b = phi_ref[2 * m + 1, r:r + 8, :]
            p_refs[0][m + 1, r + 8:r + 16, :] = jnp.where(even, a, b)
            p_refs[1][m + 1, r + 8:r + 16, :] = jnp.where(even, b, a)
        return 0
    lax.fori_loop(0, HALF, compact, 0)
    for g in range(8, ROWS - 8, 8):
        for c in (0, 1):
            e_refs[1 - c][0, g:g + 8, :] = e_refs[c][1, g:g + 8, :]
            e_refs[1 - c][HALF + 1, g:g + 8, :] = e_refs[c][HALF, g:g + 8, :]

    def sides(ref, m, g, low):
        here = ref[m + 1, g:g + 8, :]
        return (
            here,
            jnp.where(low, ref[m, g:g + 8, :], ref[m + 2, g:g + 8, :]),
            ref[m + 1, g - 1:g + 7, :],
            ref[m + 1, g + 1:g + 9, :],
            pltpu.roll(here, 1, 1),
            pltpu.roll(here, LANES - 1, 1),
        )

    for c in (0, 1):
        low = even if c == 0 else ~even
        def coefs(m, _):
            for g in range(8, ROWS - 8, 8):
                centre = e_refs[c][m + 1, g:g + 8, :]
                faces = [0.5 * (centre + side) for side in sides(e_refs[1 - c], m, g, low)]
                total = faces[0]
                for face in faces[1:]:
                    total = total + face
                scale = jnp.where(inside & (total > 0.0), OVER_RELAX / total, 0.0)
                ch = jnp.where(low, charge_ref[2 * m, g - 8:g, :], charge_ref[2 * m + 1, g - 8:g, :])
                c_refs[c][m, g - 8:g, :] = scale * ch
                for i in range(6):
                    coef_refs[c][i, m, g - 8:g, :] = scale * faces[i]
            return 0
        lax.fori_loop(0, HALF, coefs, 0)

    for step in range(DEPTH):
        c = step % 2
        low = even if c == 0 else ~even
        reach = -(-(DEPTH - 1 - step) // 8) * 8
        def half(m, _):
            for g in range(TOP - reach, TOP + TX + reach, 8):
                value = c_refs[c][m, g - 8:g, :] - (OVER_RELAX - 1.0) * p_refs[c][m + 1, g:g + 8, :]
                for i, side in enumerate(sides(p_refs[1 - c], m, g, low)):
                    value = value + coef_refs[c][i, m, g - 8:g, :] * side
                p_refs[c][m + 1, g:g + 8, :] = value
            return 0
        lax.fori_loop(0, HALF, half, 0)

    evn = parity_mask(0, (8, TY))
    def out(m, _):
        for g in range(0, TX, 8):
            a = p_refs[0][m + 1, TOP + g:TOP + g + 8, 0:TY]
            b = p_refs[1][m + 1, TOP + g:TOP + g + 8, 0:TY]
            ea = e_refs[0][m + 1, TOP + g:TOP + g + 8, 0:TY]
            eb = e_refs[1][m + 1, TOP + g:TOP + g + 8, 0:TY]
            lo, hi = jnp.where(evn, a, b), jnp.where(evn, b, a)
            elo, ehi = jnp.where(evn, ea, eb), jnp.where(evn, eb, ea)
            pot_ref[2 * m, g:g + 8, :] = lo
            pot_ref[2 * m + 1, g:g + 8, :] = hi
            q_ref[2 * m, g:g + 8, :] = 0.5 * elo * lo * lo
            q_ref[2 * m + 1, g:g + 8, :] = 0.5 * ehi * hi * hi
        return 0
    lax.fori_loop(0, HALF, out, 0)

def relax(eps_p, charge_p, phi_p):
    vm = lambda *s: pltpu.VMEM(s, jnp.float32)
    return pl.pallas_call(
        relax_kernel,
        out_shape=(jax.ShapeDtypeStruct((NZ, TX, TY), jnp.float32),) * 2,
        in_specs=[pl.BlockSpec(memory_space=pltpu.VMEM)] * 3,
        out_specs=(pl.BlockSpec(memory_space=pltpu.VMEM),) * 2,
        scratch_shapes=[
            [vm(HALF + 2, ROWS, LANES)] * 2,
            [vm(HALF + 2, ROWS, LANES)] * 2,
            [vm(HALF, ROWS - 16, LANES)] * 2,
            [vm(6, HALF, ROWS - 16, LANES)] * 2,
        ],
        name="relax",
        compiler_params=pltpu.CompilerParams(vmem_limit_bytes=62 * 2**20),
    )(eps_p, charge_p, phi_p)


CHUNK = 4096
SLOTS = 9 * NC_DEV
SLOTS_PAD = 384
VELOCITY = np.array(
    [[1, 0, 0], [-1, 0, 0], [0, 1, 0], [0, -1, 0], [0, 0, 1], [0, 0, -1], [1, 1, 0], [1, -1, 0], [-1, 1, 0],
     [-1, -1, 0], [1, 0, 1], [1, 0, -1], [-1, 0, 1], [-1, 0, -1], [0, 1, 1], [0, 1, -1], [0, -1, 1], [0, -1, -1]],
    dtype=np.float32,
).T
WEIGHT = np.array([1.0 / 18.0] * 6 + [1.0 / 36.0] * 12, dtype=np.float32)


def lattice_table():
    rows = np.zeros((4, 8, 128), np.float32)
    rows[0:3, :, 0:18] = VELOCITY[:, None, :]
    rows[3, :, 0:18] = WEIGHT[None, :]
    return jnp.asarray(rows.reshape(32, 128))


def split(values):
    high = values.astype(jnp.bfloat16).astype(jnp.float32)
    return jnp.concatenate([high, values - high], axis=0).astype(jnp.bfloat16)


def cross(first, second):
    return (
        first[1] * second[2] - first[2] * second[1],
        first[2] * second[0] - first[0] * second[2],
        first[0] * second[1] - first[1] * second[0],
    )


def decode(lat_ref, direction):
    return [jnp.take_along_axis(lat_ref[8 * i:8 * i + 8, :], direction, axis=1) for i in range(4)]


def motions_at(table, slot_ref, base, onehot_ref, at_ref):
    ids = lax.broadcasted_iota(jnp.int32, (SLOTS, 128), 0)
    for pair in range(4):
        halves = [ids == slot_ref[pl.ds(base + 2 * pair + h, 1), :] for h in (0, 1)]
        onehot = jnp.concatenate([half.astype(jnp.float32) for half in halves], axis=1).astype(jnp.bfloat16)
        if onehot_ref is not None:
            onehot_ref[:, 256 * pair:256 * pair + 256] = onehot
        found = jnp.dot(table, onehot, preferred_element_type=jnp.float32)
        found = found[0:8] + found[8:16]
        at_ref[16 * pair:16 * pair + 8, :] = found[:, 0:128]
        at_ref[16 * pair + 8:16 * pair + 16, :] = found[:, 128:256]
    return [at_ref[pl.ds(i, 8, stride=8), :] for i in range(6)]


def along_link(motion, velocity, offsets):
    spin = cross(motion[3:6], offsets)
    return sum(velocity[i] * (motion[i] + spin[i]) for i in range(3))


def links_kernel(row_ref, site_ref, dir_ref, ids_ref, pop_ref, rb_ref, q_ref, table_ref, lat_ref, slot_ref, sums_ref, onehot_ref, at_ref, term_ref):
    home_x = lax.axis_index("gx")
    home_y = lax.axis_index("gy")
    lane = lax.broadcasted_iota(jnp.int32, (8, 128), 1)
    sub = lax.broadcasted_iota(jnp.int32, (8, 128), 0)

    @pl.when(pl.program_id(0) == 0)
    def _():
        sums_ref[...] = jnp.zeros_like(sums_ref)
        term_ref[...] = jnp.zeros_like(term_ref)

    table = split(table_ref[...])[:, 0:SLOTS]

    def group(b, _):
        base = pl.multiple_of(b * 8, 8)
        rows = pl.ds(base, 8)
        ids = ids_ref[rows, :]
        owner = ids >> 5
        near_x = ((owner >> 4) - home_x + 1) & (TILES_X - 1)
        near_y = ((owner & (TILES_Y - 1)) - home_y + 1) & (TILES_Y - 1)
        slot_ref[rows, :] = jnp.where(ids >= 0, (near_x * 3 + near_y) * NC_DEV + (ids & (NC_DEV - 1)), -1)
        column = site_ref[rows, :] & 127
        pressure = jnp.zeros((8, 128), jnp.float32)
        for j in range(128):
            at = lambda s: jnp.broadcast_to(q_ref[pl.ds(row_ref[b * 1024 + s * 128 + j], 1), :], (8, 128))
            picked = at(0)
            for s in range(1, 8):
                picked = jnp.where(sub == s, at(s), picked)
            pressure = jnp.where(lane == j, jnp.take_along_axis(picked, column, axis=1), pressure)
        *velocity, weight = decode(lat_ref, dir_ref[rows, :])
        offsets = [rb_ref[i, rows, :] for i in range(3)]
        motion = motions_at(table, slot_ref, base, onehot_ref, at_ref)
        along = along_link(motion, velocity, offsets)
        transfer = 2.0 * pop_ref[rows, :] - 6.0 * weight * along + weight * pressure
        transfer = jnp.where(ids >= 0, transfer, 0.0)
        force = [v * transfer for v in velocity]
        for i, term in enumerate((*force, *cross(offsets, force))):
            term_ref[pl.ds(i, 8, stride=8), :] = term
        total = jnp.zeros((16, SLOTS), jnp.float32)
        for pair in range(4):
            terms = jnp.concatenate([term_ref[16 * pair:16 * pair + 8, :], term_ref[16 * pair + 8:16 * pair + 16, :]], axis=1)
            total = total + lax.dot_general(
                split(terms), onehot_ref[:, 256 * pair:256 * pair + 256], (((1,), (1,)), ((), ())),
                preferred_element_type=jnp.float32,
            )
        sums_ref[:, 0:SLOTS] += total[0:8] + total[8:16]
        return 0

    lax.fori_loop(0, CHUNK // 1024, group, 0)


def link_spec(lead=None):
    if lead is None:
        return pl.BlockSpec((CHUNK // 128, 128), lambda i: (i, 0))
    return pl.BlockSpec((lead, CHUNK // 128, 128), lambda i: (0, i, 0))


def whole(*shape):
    return pl.BlockSpec(shape, lambda i: (0,) * len(shape))


def link_sums(row, site, direction, ids, pop, rb, q, table):
    return pl.pallas_call(
        links_kernel,
        grid=(LINKS // CHUNK,),
        in_specs=[
            pl.BlockSpec((CHUNK,), lambda i: (i,), memory_space=pltpu.SMEM),
            link_spec(), link_spec(), link_spec(), link_spec(), link_spec(3),
            whole(NZ * TX, TY), whole(8, SLOTS_PAD), whole(32, 128),
        ],
        out_specs=(link_spec(), whole(8, SLOTS_PAD)),
        out_shape=(jax.ShapeDtypeStruct((LINKS // 128, 128), jnp.int32), jax.ShapeDtypeStruct((8, SLOTS_PAD), jnp.float32)),
        scratch_shapes=[pltpu.VMEM((SLOTS, 1024), jnp.bfloat16), pltpu.VMEM((64, 128), jnp.float32), pltpu.VMEM((64, 128), jnp.float32)],
        name="link_sums",
        compiler_params=pltpu.CompilerParams(vmem_limit_bytes=40 * 2**20),
    )(row, site, direction, ids, pop, rb, q, table, lattice_table())


def reflect_kernel(dir_ref, slot_ref, pop_ref, rb_ref, table_ref, lat_ref, out_ref, at_ref):
    table = split(table_ref[...])[:, 0:SLOTS]

    def group(b, _):
        base = pl.multiple_of(b * 8, 8)
        rows = pl.ds(base, 8)
        *velocity, weight = decode(lat_ref, dir_ref[rows, :])
        offsets = [rb_ref[i, rows, :] for i in range(3)]
        motion = motions_at(table, slot_ref, base, None, at_ref)
        along = jnp.where(slot_ref[rows, :] >= 0, along_link(motion, velocity, offsets), 0.0)
        out_ref[rows, :] = pop_ref[rows, :] - 6.0 * weight * along
        return 0

    lax.fori_loop(0, CHUNK // 1024, group, 0)


def reflect(direction, slot, pop, rb, table):
    return pl.pallas_call(
        reflect_kernel,
        grid=(LINKS // CHUNK,),
        in_specs=[link_spec(), link_spec(), link_spec(), link_spec(3), whole(8, SLOTS_PAD), whole(32, 128)],
        out_specs=link_spec(),
        out_shape=jax.ShapeDtypeStruct((LINKS // 128, 128), jnp.float32),
        scratch_shapes=[pltpu.VMEM((64, 128), jnp.float32)],
        name="reflect",
        compiler_params=pltpu.CompilerParams(vmem_limit_bytes=40 * 2**20),
    )(direction, slot, pop, rb, table, lattice_table())


def beside():
    x, y = lax.axis_index("gx"), lax.axis_index("gy")
    for t in range(9):
        if t != 4:
            yield t, (lax.rem(x + t // 3 - 1 + TILES_X, TILES_X), lax.rem(y + t % 3 - 1 + TILES_Y, TILES_Y))


def greet():
    barrier = pltpu.get_barrier_semaphore()
    for _, device in beside():
        pl.semaphore_signal(barrier, inc=1, device_id=device, device_id_type=pl.DeviceIdType.MESH)
    pl.semaphore_wait(barrier, 8)


def post(source, got_ref, send_sem, recv_sem):
    copies = []
    for t, device in beside():
        copy = pltpu.make_async_remote_copy(
            src_ref=source(t), dst_ref=got_ref.at[8 - t], send_sem=send_sem.at[t], recv_sem=recv_sem.at[8 - t],
            device_id=device, device_id_type=pl.DeviceIdType.MESH,
        )
        copy.start()
        copies.append(copy)
    return copies


def write_table(table_ref, block):
    for tile in range(3):
        total = jnp.zeros((8, 128), jnp.float32)
        for i in range(4):
            if 4 * tile + i < 9:
                value = block(4 * tile + i)
                total = total + (pltpu.roll(value, NC_DEV * i, 1) if i else value)
        table_ref[:, 128 * tile:128 * tile + 128] = total


def share_kernel(motion_ref, table_ref, got_ref, send_sem, recv_sem):
    greet()
    copies = post(lambda t: motion_ref, got_ref, send_sem, recv_sem)
    for copy in copies:
        copy.wait()
    write_table(table_ref, lambda t: motion_ref[...] if t == 4 else got_ref[t])


def update_kernel(sums_ref, motion_ref, report_ref, table_ref, part_ref, got_ref, new_ref, back_ref, send_sem, recv_sem, send2_sem, recv2_sem):
    greet()
    lane = lax.broadcasted_iota(jnp.int32, (8, 128), 1)
    row = lax.broadcasted_iota(jnp.int32, (8, 128), 0)
    for t in range(9):
        value = sums_ref[:, 128 * (t // 4):128 * (t // 4) + 128]
        if t % 4:
            value = pltpu.roll(value, 128 - NC_DEV * (t % 4), 1)
        part_ref[t] = jnp.where(lane < NC_DEV, value, 0.0)
    copies = post(lambda t: part_ref.at[t], got_ref, send_sem, recv_sem)
    total = part_ref[4]
    for copy in copies:
        copy.wait()
    for t in range(9):
        if t != 4:
            total = total + got_ref[t]
    mass = 4.0 / 3.0 * math.pi * RADIUS**3
    inertia = 0.4 * mass * RADIUS**2
    report_ref[...] = jnp.where(row < 3, total, total / RADIUS)
    new_ref[...] = motion_ref[...] + jnp.where(row < 3, total / mass, total / inertia)
    copies = post(lambda t: new_ref, back_ref, send2_sem, recv2_sem)
    for copy in copies:
        copy.wait()
    write_table(table_ref, lambda t: new_ref[...] if t == 4 else back_ref[t])


VM = pl.BlockSpec(memory_space=pltpu.VMEM)


def share_motion(motion):
    return pl.pallas_call(
        share_kernel,
        out_shape=jax.ShapeDtypeStruct((8, SLOTS_PAD), jnp.float32),
        in_specs=[VM],
        out_specs=VM,
        scratch_shapes=[pltpu.VMEM((9, 8, 128), jnp.float32), pltpu.SemaphoreType.DMA((9,)), pltpu.SemaphoreType.DMA((9,))],
        name="share_motion",
        compiler_params=pltpu.CompilerParams(collective_id=0, has_side_effects=True),
    )(motion)


def update(sums, motion):
    return pl.pallas_call(
        update_kernel,
        out_shape=(jax.ShapeDtypeStruct((8, 128), jnp.float32), jax.ShapeDtypeStruct((8, SLOTS_PAD), jnp.float32)),
        in_specs=[VM, VM],
        out_specs=(VM, VM),
        scratch_shapes=[
            pltpu.VMEM((9, 8, 128), jnp.float32), pltpu.VMEM((9, 8, 128), jnp.float32),
            pltpu.VMEM((8, 128), jnp.float32), pltpu.VMEM((9, 8, 128), jnp.float32),
            pltpu.SemaphoreType.DMA((9,)), pltpu.SemaphoreType.DMA((9,)), pltpu.SemaphoreType.DMA((9,)), pltpu.SemaphoreType.DMA((9,)),
        ],
        name="update",
        compiler_params=pltpu.CompilerParams(collective_id=1, has_side_effects=True),
    )(sums, motion)


def neighbours(axis, value_low, value_high):
    count = lax.axis_size(axis)
    forward = [(i, (i + 1) % count) for i in range(count)]
    backward = [(target, source) for source, target in forward]
    return lax.ppermute(value_low, axis, forward), lax.ppermute(value_high, axis, backward)


def framed(block):
    low, high = neighbours("gx", block[:, TX - 16:], block[:, :16])
    block = jnp.concatenate([low, block, high], axis=1)
    low, high = neighbours("gy", block[:, :, TY - 16:], block[:, :, :16])
    gap = jnp.zeros((NZ, TX + 32, LANES - TY - 32), block.dtype)
    return jnp.concatenate([block, high, gap, low], axis=2)


def shards(
    eps_field, charge, potential_start, colloid_vel, colloid_spin, link_dir, link_colloid, link_site, link_depth,
    link_pop, link_rb,
):
    flat = lambda a: a.reshape(LINKS // 128, 128)
    motion = jnp.pad(jnp.concatenate([colloid_vel, colloid_spin], axis=0), ((0, 2), (0, 128 - NC_DEV)))
    table = share_motion(motion)
    potential, q = relax(framed(eps_field), framed(charge), framed(potential_start))
    row = link_depth.reshape(-1) * TX + (link_site.reshape(-1) >> 7)
    rb = link_rb.reshape(3, LINKS // 128, 128)
    slot, sums = link_sums(
        row, flat(link_site), flat(link_dir), flat(link_colloid), flat(link_pop), rb, q.reshape(NZ * TX, TY), table
    )
    report, table = update(sums, motion)
    link_out = reflect(flat(link_dir), slot, flat(link_pop), rb, table).reshape(link_pop.shape)
    return potential, report[0:6, 0:NC_DEV], link_out


def solution(mesh):
    tile = P(None, "gx", "gy")
    owned = P(None, ("gx", "gy"))
    link = P("gx", "gy", None)
    return jax.shard_map(
        shards,
        mesh=mesh,
        in_specs=(tile, tile, tile, owned, owned, link, link, link, link, link, P(None, "gx", "gy", None)),
        out_specs=(tile, owned, link),
        check_vma=False,
    )
```

time: 940 us -> 216 us (0.23)
  local copies, waits for them, and re-layouts: 529 us -> 48.4 us
  other arithmetic: 196 us -> 12.8 us
  Pallas kernels: 0 us -> 126 us
  starting transfers between devices: 138 us -> 23.4 us
  matrix products: 46.9 us -> 0 us
  waiting for transfers between devices: 19.2 us -> 3.08 us
    gather x4 -> x0, local copies, waits for them, and re-layouts: 383 us -> none  [the longest x2 202 us: shards(): jnp.take(eps_field.reshape(-1), sites).astype(jnp.float32)]
    pallas_call x0 -> x5, Pallas kernels: none -> 126 us  [the longest x1 49.6 us: relax(): pl.pallas_call(relax_kernel, out_shape=(jax.ShapeDtypeStruct((NZ, TX, TY)...]
    select_n x14 -> x0, other arithmetic: 116 us -> none  [the longest x12 115 us: relax_colour(): jnp.where(colour_mask, centre + OVER_RELAX * (target - centre), centre)]
    ppermute x64 -> x12, starting transfers between devices: 138 us -> 23.4 us  [the longest x6 22.8 us: neighbours(): lax.ppermute(value_high, axis, backward)]
    slice x57 -> x12, local copies, waits for them, and re-layouts: 84.7 us -> 23 us  [the longest x9 18.7 us: framed(): low, high = neighbours('gy', block[:, :, TY - 16:], block[:, :, :16])]
    concatenate x30 -> x3, other arithmetic: 65.1 us -> 12.6 us  [the longest x2 12 us: framed(): return jnp.concatenate([block, high, gap, low], axis=2)]
    dot_general x14 -> x0, matrix products: 46.9 us -> none  [the longest x4 17.1 us: add_block(): lax.dot_general(terms, onehot, (((1,), (1,)), ((), ())), precision=lax.Pr...]
    ppermute x26 -> x6, local copies, waits for them, and re-layouts: 49.4 us -> 15.3 us  [the longest x3 7.66 us: neighbours(): lax.ppermute(value_low, axis, forward)]
  transfers between devices with their start and end apart: 64 -> 12, of which waited for: 15 -> 2; matrix products, arithmetic and copies ran while one was open for 38% -> 20% of each run, Pallas kernels for 0% -> 6%
where the time goes in v1:
time: 216 us; the launch traced here: 214 us
  Pallas kernels  126 us (58%)
  local copies, waits for them, and re-layouts  48.4 us (22%)
  starting transfers between devices  23.4 us (11%)
  other arithmetic  12.8 us (6%)
  waiting for transfers between devices  3.08 us (1%)
    pallas_call x1, Pallas kernels, relax(): pl.pallas_call(relax_kernel, out_shape=(jax.ShapeDtypeStruct((NZ, TX, TY)...  49.6 us
    pallas_call x1, Pallas kernels, link_sums(): pl.pallas_call(links_kernel, grid=(LINKS // CHUNK,), in_specs=[pl.BlockSp...  38 us
    ppermute x6, starting transfers between devices, neighbours(): lax.ppermute(value_high, axis, backward)  22.8 us
    slice x9, local copies, waits for them, and re-layouts, framed(): low, high = neighbours('gy', block[:, :, TY - 16:], block[:, :, :16])  18.7 us
    pallas_call x1, Pallas kernels, update(): pl.pallas_call(update_kernel, out_shape=(jax.ShapeDtypeStruct((8, 128), j...  17.3 us
    pallas_call x1, Pallas kernels, share_motion(): pl.pallas_call(share_kernel, out_shape=jax.ShapeDtypeStruct((8, SLOTS_PAD...  12.2 us
    concatenate x2, other arithmetic, framed(): return jnp.concatenate([block, high, gap, low], axis=2)  12 us
    unnamed x41, local copies, waits for them, and re-layouts  8.89 us
  transfers between devices with their start and end apart: 12, of which 2 were waited for; matrix products, arithmetic and copies ran while one was open for 20% of the time, Pallas kernels for 6%

profile of v1, /device:TPU:0, one launch (start us, length us, event | category | flops | bytes accessed | tf_op | source)
XLA Modules:
  0.0 214.4 jit_solution(9081922148896153626)
XLA Ops:
  0.7 2.3 %fusion.3 = (f32[48,16,128]{2,1,0:T(8,128)}, f32[48,16,128]{2,1,0:T(8,128)}) fusion(f32[48,64,128]{2,1,0:T(8,128)} %param.14), kind=kLoop, calls=%fused_computation.19 | loop fusion | bytes 1572864 | tf_op jit(solution)/shard_map/slice | solution.py:409
  2.9 3.0 %collective-permute-start.5 = (f32[48,16,128]{2,1,0:T(8,128)}, f32[48,16,128]{2,1,0:T(8,128)S(1)}, u32[]{:S(2)}, u32[]{:S(2)}) collective-permute-start(f32[48,16,128]{2,1,0:T(8,128)} %get-tuple-element.21), channel_id=1, source_target_pairs={{16,0},{32,16},{48,32},{64,48},{80,64},{96,80},{112,96},{0,112},{1... | collective-permute-start | bytes 1179656 | tf_op jit(solution)/shard_map/ppermute | solution.py:405
  8.5 2.4 %collective-permute-start.1 = (bf16[48,16,128]{2,1,0:T(8,128)(2,1)S(1)}, bf16[48,16,128]{2,1,0:T(8,128)(2,1)S(1)}, u32[]{:S(2)}, u32[]{:S(2)}) collective-permute-start(bf16[48,16,128]{2,1,0:T(8,128)(2,1)S(1)} %get-tuple-element.25), channel_id=1, source_target_pairs={{16,0},{32,16},{48,32},{64,48},{80,64},{96,80},{112,96},{0,112},{1... | collective-permute-start | bytes 589832 | tf_op jit(solution)/shard_map/ppermute | solution.py:405
  10.9 2.7 %collective-permute-done = bf16[48,16,128]{2,1,0:T(8,128)(2,1)S(1)} collective-permute-done((bf16[48,16,128]{2,1,0:T(8,128)(2,1)S(1)}, bf16[48,16,128]{2,1,0:T(8,128)(2,1)S(1)}, u32[]{:S(2)}, u32[]{:S(2)}) %collective-permute-start) | collective-permute-done | bytes 196640 | tf_op jit(solution)/shard_map/ppermute | solution.py:405
  16.3 6.3 %collective-permute-start.2 = (bf16[48,96,16]{1,2,0:T(8,128)(2,1)}, bf16[48,96,16]{1,2,0:T(8,128)(2,1)S(1)}, u32[]{:S(2)}, u32[]{:S(2)}) collective-permute-start(bf16[48,96,16]{1,2,0:T(8,128)(2,1)} %copy.16), channel_id=1, source_target_pairs={{1,0},{2,1},{3,2},{4,3},{5,4},{6,5},{7,6},{8,7},{9,8},{10,9},{11,1... | collective-permute-start | bytes 442376 | tf_op jit(solution)/shard_map/ppermute | solution.py:405
  23.9 12.2 %share_motion.1.table_ref = f32[8,384]{1,0:T(8,128)} custom-call(f32[8,128]{1,0:T(8,128)} %select_maximum_fusion.motion_ref), custom_call_target="tpu_custom_call" | custom-call | tf_op jit(solution)/shard_map/share_motion/pallas_call | solution.py:374
  42.6 3.0 %fusion.1 = (f32[48,96,16]{2,1,0:T(8,128)}, f32[48,96,16]{2,1,0:T(8,128)}) fusion(f32[48,96,128]{2,1,0:T(8,128)S(1)} %constant_dynamic-update-slice_fusion.3), kind=kLoop, calls=%fused_computation.17 | loop fusion | bytes 1179648 | tf_op jit(solution)/shard_map/slice | solution.py:411
  45.7 2.3 %copy.20 = f32[48,96,16]{1,2,0:T(8,128)S(1)} copy(f32[48,96,16]{2,1,0:T(8,128)} %get-tuple-element.17) | data formatting | bytes 589824 | tf_op jit(solution)/shard_map/slice | solution.py:411
  48.0 4.8 %collective-permute-start.6 = (f32[48,96,16]{1,2,0:T(8,128)S(1)}, f32[48,96,16]{1,2,0:T(8,128)}, u32[]{:S(2)}, u32[]{:S(2)}) collective-permute-start(f32[48,96,16]{1,2,0:T(8,128)S(1)} %copy.20), channel_id=1, source_target_pairs={{1,0},{2,1},{3,2},{4,3},{5,4},{6,5},{7,6},{8,7},{9,8},{10,9},{11,1... | collective-permute-start | bytes 884744 | tf_op jit(solution)/shard_map/ppermute | solution.py:405
  52.8 3.1 %copy.21 = f32[48,96,16]{1,2,0:T(8,128)} copy(f32[48,96,16]{2,1,0:T(8,128)} %get-tuple-element.18) | data formatting | bytes 589824 | tf_op jit(solution)/shard_map/slice | solution.py:411
  58.5 3.0 %fusion = (f32[48,96,16]{2,1,0:T(8,128)}, f32[48,96,16]{2,1,0:T(8,128)}) fusion(f32[48,96,128]{2,1,0:T(8,128)S(1)} %constant_dynamic-update-slice_fusion.6), kind=kLoop, calls=%fused_computation.16 | loop fusion | bytes 1179648 | tf_op jit(solution)/shard_map/slice | solution.py:411
  61.5 2.3 %copy.24 = f32[48,96,16]{1,2,0:T(8,128)S(1)} copy(f32[48,96,16]{2,1,0:T(8,128)} %get-tuple-element.15) | data formatting | bytes 589824 | tf_op jit(solution)/shard_map/slice | solution.py:411
  63.8 5.4 %collective-permute-start.10 = (f32[48,96,16]{1,2,0:T(8,128)S(1)}, f32[48,96,16]{1,2,0:T(8,128)}, u32[]{:S(2)}, u32[]{:S(2)}) collective-permute-start(f32[48,96,16]{1,2,0:T(8,128)S(1)} %copy.24), channel_id=1, source_target_pairs={{1,0},{2,1},{3,2},{4,3},{5,4},{6,5},{7,6},{8,7},{9,8},{10,9},{11,1... | collective-permute-start | bytes 884744 | tf_op jit(solution)/shard_map/ppermute | solution.py:405
  69.2 3.1 %copy.25 = f32[48,96,16]{1,2,0:T(8,128)} copy(f32[48,96,16]{2,1,0:T(8,128)} %get-tuple-element.16) | data formatting | bytes 589824 | tf_op jit(solution)/shard_map/slice | solution.py:411
  72.3 4.3 %pad_maximum_fusion.2.eps_ref = bf16[48,96,256]{2,1,0:T(8,128)(2,1)} fusion(bf16[48,96,16]{2,1,0:T(8,128)(2,1)} %copy.19, bf16[48,96,16]{2,1,0:T(8,128)(2,1)} %copy.18, bf16[48,96,128]{2,1,0:T(8,128)(2,1)} %copy-done.11, bf16[256]{0:T(256)(128)(2,1)S(1)} %pad.17.clone), kind=kLoop, calls=%fused_computation.2 | loop fusion | flops 9437184 | bytes 3834368 | tf_op jit(solution)/shard_map/concatenate | solution.py:413
  76.6 3.1 %copy.22 = f32[48,96,16]{2,1,0:T(8,128)} copy(f32[48,96,16]{1,2,0:T(8,128)} %collective-permute-done.6) | data formatting | bytes 589824 | tf_op jit(solution)/shard_map/ppermute | solution.py:405
  79.7 3.1 %copy.23 = f32[48,96,16]{2,1,0:T(8,128)} copy(f32[48,96,16]{1,2,0:T(8,128)} %collective-permute-done.7) | data formatting | bytes 589824 | tf_op jit(solution)/shard_map/ppermute | solution.py:405
  82.8 3.1 %copy.26 = f32[48,96,16]{2,1,0:T(8,128)} copy(f32[48,96,16]{1,2,0:T(8,128)} %collective-permute-done.10) | data formatting | bytes 589824 | tf_op jit(solution)/shard_map/ppermute | solution.py:405
  86.0 3.1 %copy.27 = f32[48,96,16]{2,1,0:T(8,128)} copy(f32[48,96,16]{1,2,0:T(8,128)} %collective-permute-done.11) | data formatting | bytes 589824 | tf_op jit(solution)/shard_map/ppermute | solution.py:405
  89.1 7.7 %pad_maximum_fusion.1 = (f32[48,96,256]{2,1,0:T(8,128)}, f32[48,96,256]{2,1,0:T(8,128)}) fusion(f32[48,96,16]{2,1,0:T(8,128)} %copy.27, f32[48,96,16]{2,1,0:T(8,128)} %copy.26, f32[48,96,128]{2,1,0:T(8,128)} %copy-done.10, f32[256]{0:T(256)S(1)} %pad.13.clone, f32[48,96,16]{2,1,0:T(8,128)} %copy.23, f32[48,96,16]{2,1,0:T(8,128)} %copy.22, ...), kind=kLoop, calls=%fused_computation.1 | loop fusion | flops 7077888 | bytes 15336448 | tf_op jit(solution)/shard_map/concatenate | solution.py:413
  96.8 49.6 %relax.1 = (f32[48,64,128]{2,1,0:T(8,128)}, f32[48,64,128]{2,1,0:T(8,128)}) custom-call(bf16[48,96,256]{2,1,0:T(8,128)(2,1)} %pad_maximum_fusion.2.eps_ref, f32[48,96,256]{2,1,0:T(8,128)} %get-tuple-element.28.charge_ref, f32[48,96,256]{2,1,0:T(8,128)} %get-tuple-element.27.phi_ref), custom_call_target="tpu_custom_call" | custom-call | tf_op jit(solution)/shard_map/relax/pallas_call | solution.py:123
  147.8 38.0 %link_sums.1 = (s32[256,128]{1,0:T(8,128)S(1)}, f32[8,384]{1,0:T(8,128)S(1)}) custom-call(s32[32768]{0:T(1024)S(1)} %bitcast.13, s32[256,128]{1,0:T(8,128)S(1)} %bitcast.12, s32[256,128]{1,0:T(8,128)S(1)} %bitcast.14, s32[256,128]{1,0:T(8,128)S(1)} %bitcast.18, f32[256,128]{1,0:T(8,128)S(1)} %bitcast.16, f32[3,256,128]{2,1,0:T(8,128)S(1)} %bitcast.10, ...), custom_call_target="tpu_custom_call" | custom-call | tf_op jit(solution)/shard_map/link_sums/pallas_call | solution.py:255
  186.4 17.3 %update.1 = (f32[8,128]{1,0:T(8,128)}, f32[8,384]{1,0:T(8,128)}) custom-call(f32[8,384]{1,0:T(8,128)} %copy-done.8, f32[8,128]{1,0:T(8,128)} %select_maximum_fusion.motion_ref), custom_call_target="tpu_custom_call" | custom-call | tf_op jit(solution)/shard_map/update/pallas_call | solution.py:386
  204.4 8.7 %reflect.1 = f32[256,128]{1,0:T(8,128)} custom-call(s32[256,128]{1,0:T(8,128)S(1)} %bitcast.15, s32[256,128]{1,0:T(8,128)S(1)} %get-tuple-element.13.slot_ref, f32[256,128]{1,0:T(8,128)S(1)} %bitcast.17, f32[3,256,128]{2,1,0:T(8,128)S(1)} %bitcast.11, f32[8,384]{1,0:T(8,128)S(1)} %copy-done.9, f32[32,128]{1,0:T(8,128)S(1)} %copy-done.6), custom_call_target="tpu_custom_call" | custom-call | tf_op jit(solution)/shard_map/reflect/pallas_call | solution.py:288
  (75 shorter events, 19.6 us)
Async XLA Ops:
  0.6 13.0 %copy-start.13 = (bf16[48,64,128]{2,1,0:T(8,128)(2,1)S(1)}, bf16[48,64,128]{2,1,0:T(8,128)(2,1)}, u32[]{:S(2)}) copy-start(bf16[48,64,128]{2,1,0:T(8,128)(2,1)} %param.13) | copy-start | bytes 2359300
  0.6 6.3 %copy-start.12 = (f32[48,64,128]{2,1,0:T(8,128)S(1)}, f32[48,64,128]{2,1,0:T(8,128)}, u32[]{:S(2)}) copy-start(f32[48,64,128]{2,1,0:T(8,128)} %param.15) | copy-start | bytes 4718596
  2.9 37.1 %collective-permute-start.4 = (f32[48,16,128]{2,1,0:T(8,128)}, f32[48,16,128]{2,1,0:T(8,128)}, u32[]{:S(2)}, u32[]{:S(2)}) collective-permute-start(f32[48,16,128]{2,1,0:T(8,128)} %get-tuple-element.22), channel_id=1, source_target_pairs={{0,16},{16,32},{32,48},{48,64},{64,80},{80,96},{96,112},{112,0},{1... | collective-permute-start | bytes 1179656 | tf_op jit(solution)/shard_map/ppermute | solution.py:405
  2.9 39.6 %collective-permute-start.5 = (f32[48,16,128]{2,1,0:T(8,128)}, f32[48,16,128]{2,1,0:T(8,128)S(1)}, u32[]{:S(2)}, u32[]{:S(2)}) collective-permute-start(f32[48,16,128]{2,1,0:T(8,128)} %get-tuple-element.21), channel_id=1, source_target_pairs={{16,0},{32,16},{48,32},{64,48},{80,64},{96,80},{112,96},{0,112},{1... | collective-permute-start | bytes 1179656 | tf_op jit(solution)/shard_map/ppermute | solution.py:405
  6.9 6.7 %collective-permute-start = (bf16[48,16,128]{2,1,0:T(8,128)(2,1)S(1)}, bf16[48,16,128]{2,1,0:T(8,128)(2,1)S(1)}, u32[]{:S(2)}, u32[]{:S(2)}) collective-permute-start(bf16[48,16,128]{2,1,0:T(8,128)(2,1)S(1)} %get-tuple-element.26), channel_id=1, source_target_pairs={{0,16},{16,32},{32,48},{48,64},{64,80},{80,96},{96,112},{112,0},{1... | collective-permute-start | bytes 589832 | tf_op jit(solution)/shard_map/ppermute | solution.py:405
  8.0 47.9 %collective-permute-start.8 = (f32[48,16,128]{2,1,0:T(8,128)}, f32[48,16,128]{2,1,0:T(8,128)S(1)}, u32[]{:S(2)}, u32[]{:S(2)}) collective-permute-start(f32[48,16,128]{2,1,0:T(8,128)} %get-tuple-element.20), channel_id=1, source_target_pairs={{0,16},{16,32},{32,48},{48,64},{64,80},{80,96},{96,112},{112,0},{1... | collective-permute-start | bytes 1179656 | tf_op jit(solution)/shard_map/ppermute | solution.py:405
  8.5 5.6 %collective-permute-start.1 = (bf16[48,16,128]{2,1,0:T(8,128)(2,1)S(1)}, bf16[48,16,128]{2,1,0:T(8,128)(2,1)S(1)}, u32[]{:S(2)}, u32[]{:S(2)}) collective-permute-start(bf16[48,16,128]{2,1,0:T(8,128)(2,1)S(1)} %get-tuple-element.25), channel_id=1, source_target_pairs={{16,0},{32,16},{48,32},{64,48},{80,64},{96,80},{112,96},{0,112},{1... | collective-permute-start | bytes 589832 | tf_op jit(solution)/shard_map/ppermute | solution.py:405
  15.2 7.8 %copy-start.2 = (s32[1,1,32768]{2,1,0:T(1,128)S(1)}, s32[1,1,32768]{2,1,0:T(1,128)}, u32[]{:S(2)}) copy-start(s32[1,1,32768]{2,1,0:T(1,128)} %param.20) | copy-start | bytes 393220
  15.2 7.8 %copy-start.14 = (s32[1,1,32768]{2,1,0:T(1,128)S(1)}, s32[1,1,32768]{2,1,0:T(1,128)}, u32[]{:S(2)}) copy-start(s32[1,1,32768]{2,1,0:T(1,128)} %param.21) | copy-start | bytes 393220
  15.2 8.0 %copy-start.15 = (f32[3,32]{1,0:T(4,128)S(1)}, f32[3,32]{1,0:T(4,128)}, u32[]{:S(2)}) copy-start(f32[3,32]{1,0:T(4,128)} %param.17) | copy-start | bytes 1156
  15.2 8.0 %copy-start.16 = (f32[3,32]{1,0:T(4,128)S(1)}, f32[3,32]{1,0:T(4,128)}, u32[]{:S(2)}) copy-start(f32[3,32]{1,0:T(4,128)} %param.16) | copy-start | bytes 1156
  16.3 20.0 %collective-permute-start.2 = (bf16[48,96,16]{1,2,0:T(8,128)(2,1)}, bf16[48,96,16]{1,2,0:T(8,128)(2,1)S(1)}, u32[]{:S(2)}, u32[]{:S(2)}) collective-permute-start(bf16[48,96,16]{1,2,0:T(8,128)(2,1)} %copy.16), channel_id=1, source_target_pairs={{1,0},{2,1},{3,2},{4,3},{5,4},{6,5},{7,6},{8,7},{9,8},{10,9},{11,1... | collective-permute-start | bytes 442376 | tf_op jit(solution)/shard_map/ppermute | solution.py:405
  23.0 15.6 %collective-permute-start.3 = (bf16[48,96,16]{1,2,0:T(8,128)(2,1)S(1)}, bf16[48,96,16]{1,2,0:T(8,128)(2,1)S(1)}, u32[]{:S(2)}, u32[]{:S(2)}) collective-permute-start(bf16[48,96,16]{1,2,0:T(8,128)(2,1)S(1)} %copy.17), channel_id=1, source_target_pairs={{0,1},{1,2},{2,3},{3,4},{4,5},{5,6},{6,7},{7,8},{8,9},{9,10},{10,1... | collective-permute-start | bytes 442376 | tf_op jit(solution)/shard_map/ppermute | solution.py:405
  36.3 21.1 %collective-permute-start.9 = (f32[48,16,128]{2,1,0:T(8,128)}, f32[48,16,128]{2,1,0:T(8,128)}, u32[]{:S(2)}, u32[]{:S(2)}) collective-permute-start(f32[48,16,128]{2,1,0:T(8,128)} %get-tuple-element.19), channel_id=1, source_target_pairs={{16,0},{32,16},{48,32},{64,48},{80,64},{96,80},{112,96},{0,112},{1... | collective-permute-start | bytes 1179656 | tf_op jit(solution)/shard_map/ppermute | solution.py:405
  48.0 28.7 %collective-permute-start.6 = (f32[48,96,16]{1,2,0:T(8,128)S(1)}, f32[48,96,16]{1,2,0:T(8,128)}, u32[]{:S(2)}, u32[]{:S(2)}) collective-permute-start(f32[48,96,16]{1,2,0:T(8,128)S(1)} %copy.20), channel_id=1, source_target_pairs={{1,0},{2,1},{3,2},{4,3},{5,4},{6,5},{7,6},{8,7},{9,8},{10,9},{11,1... | collective-permute-start | bytes 884744 | tf_op jit(solution)/shard_map/ppermute | solution.py:405
  55.8 23.9 %collective-permute-start.7 = (f32[48,96,16]{1,2,0:T(8,128)}, f32[48,96,16]{1,2,0:T(8,128)}, u32[]{:S(2)}, u32[]{:S(2)}) collective-permute-start(f32[48,96,16]{1,2,0:T(8,128)} %copy.21), channel_id=1, source_target_pairs={{0,1},{1,2},{2,3},{3,4},{4,5},{5,6},{6,7},{7,8},{8,9},{9,10},{10,1... | collective-permute-start | bytes 884744 | tf_op jit(solution)/shard_map/ppermute | solution.py:405
  63.8 19.0 %collective-permute-start.10 = (f32[48,96,16]{1,2,0:T(8,128)S(1)}, f32[48,96,16]{1,2,0:T(8,128)}, u32[]{:S(2)}, u32[]{:S(2)}) collective-permute-start(f32[48,96,16]{1,2,0:T(8,128)S(1)} %copy.24), channel_id=1, source_target_pairs={{1,0},{2,1},{3,2},{4,3},{5,4},{6,5},{7,6},{8,7},{9,8},{10,9},{11,1... | collective-permute-start | bytes 884744 | tf_op jit(solution)/shard_map/ppermute | solution.py:405
  72.3 13.6 %collective-permute-start.11 = (f32[48,96,16]{1,2,0:T(8,128)}, f32[48,96,16]{1,2,0:T(8,128)}, u32[]{:S(2)}, u32[]{:S(2)}) collective-permute-start(f32[48,96,16]{1,2,0:T(8,128)} %copy.25), channel_id=1, source_target_pairs={{0,1},{1,2},{2,3},{3,4},{4,5},{5,6},{6,7},{7,8},{8,9},{9,10},{10,1... | collective-permute-start | bytes 884744 | tf_op jit(solution)/shard_map/ppermute | solution.py:405
  96.8 49.6 %copy-start.1 = (f32[3,1,1,32768]{3,2,1,0:T(1,128)S(1)}, f32[3,1,1,32768]{3,2,1,0:T(1,128)}, u32[]{:S(2)}) copy-start(f32[3,1,1,32768]{3,2,1,0:T(1,128)} %param.23) | copy-start | bytes 1179652
  96.8 49.6 %copy-start.3 = (s32[1,1,32768]{2,1,0:T(1,128)S(1)}, s32[1,1,32768]{2,1,0:T(1,128)}, u32[]{:S(2)}) copy-start(s32[1,1,32768]{2,1,0:T(1,128)} %param.18) | copy-start | bytes 393220
  96.8 49.6 %copy-start.4 = (f32[1,1,32768]{2,1,0:T(1,128)S(1)}, f32[1,1,32768]{2,1,0:T(1,128)}, u32[]{:S(2)}) copy-start(f32[1,1,32768]{2,1,0:T(1,128)} %param.22) | copy-start | bytes 393220
  96.8 49.6 %copy-start.5 = (s32[1,1,32768]{2,1,0:T(1,128)S(1)}, s32[1,1,32768]{2,1,0:T(1,128)}, u32[]{:S(2)}) copy-start(s32[1,1,32768]{2,1,0:T(1,128)} %param.19) | copy-start | bytes 393220
  96.8 49.6 %copy-start.6 = (f32[32,128]{1,0:T(8,128)S(1)}, f32[32,128]{1,0:T(8,128)}, u32[]{:S(2)}) copy-start(f32[32,128]{1,0:T(8,128)} %constant.12.clone.lat_ref) | copy-start | bytes 49156
  96.8 49.6 %copy-start.7 = (f32[8,384]{1,0:T(8,128)S(1)}, f32[8,384]{1,0:T(8,128)}, u32[]{:S(2)}) copy-start(f32[8,384]{1,0:T(8,128)} %share_motion.1.table_ref) | copy-start | bytes 36868
  (5 other events, 6.8 us)

commit v2 on v1

--- a/solution.py
+++ b/solution.py
@@ -12,105 +12,316 @@
 NC_DEV = 32
 LINKS = 32768
 RADIUS = 8
-SWEEPS=6
-OVER_RELAX=1.6
+SWEEPS = 6
+OVER_RELAX = 1.6
 NZ, TX, TY = 48, 64, 128
-HALF = NZ//2
-ROWS = 112
-TOP = 24
-LANES = 256
-DEPTH = 2*SWEEPS
-
-def parity_mask(colour, shape):
-    s = lax.broadcasted_iota(jnp.int32, shape, 0) + lax.broadcasted_iota(jnp.int32, shape, 1)
-    return (s + colour) % 2 == 0
-
-def relax_kernel(eps_ref, charge_ref, phi_ref, pot_ref, q_ref, p_refs, e_refs, c_refs, coef_refs):
-    even = parity_mask(0, (8, LANES))
-    lane = lax.broadcasted_iota(jnp.int32, (8, LANES), 1)
-    inside = (lane < TY + 16) | (lane >= LANES - 16)
-    zero = jnp.zeros((8, LANES), jnp.float32)
-    for ref in (*p_refs, *e_refs):
-        for g in (0, ROWS - 8):
-            def clear(m, _):
+HALF = NZ // 2
+GROUPS = HALF // 8
+ROWS = 96
+TOP = 16
+
+
+def beside():
+    x, y = lax.axis_index("gx"), lax.axis_index("gy")
+    for t in range(9):
+        if t != 4:
+            yield t, (lax.rem(x + t // 3 - 1 + TILES_X, TILES_X), lax.rem(y + t % 3 - 1 + TILES_Y, TILES_Y))
+
+
+def greet():
+    barrier = pltpu.get_barrier_semaphore()
+    for _, device in beside():
+        pl.semaphore_signal(barrier, inc=1, device_id=device, device_id_type=pl.DeviceIdType.MESH)
+    return lambda: pl.semaphore_wait(barrier, 8)
+
+
+class Mail:
+    def __init__(self, send_sem, recv_sem):
+        self.sems, self.count, self.copies, self.device = (send_sem, recv_sem), 0, [], dict(beside())
+
+    def send(self, t, source, target):
+        copy = pltpu.make_async_remote_copy(
+            src_ref=source, dst_ref=target, send_sem=self.sems[0].at[self.count], recv_sem=self.sems[1].at[self.count],
+            device_id=self.device[t], device_id_type=pl.DeviceIdType.MESH,
+        )
+        copy.start()
+        self.count += 1
+        self.copies.append(copy)
+
+    def wait(self):
+        for copy in self.copies:
+            copy.wait()
+        self.copies = []
+
+
+def write_table(table_ref, block):
+    for tile in range(3):
+        total = jnp.zeros((8, 128), jnp.float32)
+        for i in range(4):
+            if 4 * tile + i < 9:
+                value = block(4 * tile + i)
+                total = total + (pltpu.roll(value, NC_DEV * i, 1) if i else value)
+        table_ref[:, 128 * tile:128 * tile + 128] = total
+
+
+def relax_kernel(
+    eps_ref, charge_ref, phi_ref, motion_ref, pot_ref, q_ref, table_ref,
+    p_refs, e_refs, ps_refs, es_refs, gs_refs, c_refs, coef_refs, cs_refs, coefs_refs,
+    to_low, to_high, from_low, from_high, x_eps, x_charge, x_phi, to2_low, to2_high, from2_low, from2_high, x2_refs,
+    got_ref, send_sem, recv_sem,
+):
+    sub = lax.broadcasted_iota(jnp.int32, (8, 128), 0)
+    lane = lax.broadcasted_iota(jnp.int32, (8, 128), 1)
+    even = (sub + lane) % 2 == 0
+    odd = ~even
+    first = lane % 16 < 8
+    slot = lane // 16
+    zero = jnp.zeros((8, 128), jnp.float32)
+    blocks = range(8, ROWS - 8, 8)
+    greeted = greet()
+    mail = Mail(send_sem, recv_sem)
+
+    def pack(plane, low_ref, high_ref, at):
+        def group(g, _):
+            for r in range(0, TX, 16):
+                low, high = [zero, zero], [zero, zero]
+                for k in range(16):
+                    rows = plane(g, k, r)
+                    for h in (0, 1):
+                        value = rows[h]
+                        here = lane // 8 == k
+                        low[h] = jnp.where(here, pltpu.roll(value, 8 * k, 1) if k else value, low[h])
+                        high[h] = jnp.where(here, pltpu.roll(value, 8 * (k + 1), 1) if k < 15 else value, high[h])
+                for h in (0, 1):
+                    low_ref[at + g, r + 8 * h:r + 8 * h + 8, :] = low[h]
+                    high_ref[at + g, r + 8 * h:r + 8 * h + 8, :] = high[h]
+            return 0
+        lax.fori_loop(0, GROUPS, group, 0)
+
+    def send_sides(low_ref, high_ref, dst_low, dst_high, at):
+        span = pl.ds(at, GROUPS)
+        for t, rows, target in ((3, (0, TX), 8), (0, (0, 8), 72), (6, (TX - 8, 8), 0)):
+            mail.send(t, low_ref.at[span, pl.ds(*rows), :], dst_high.at[span, pl.ds(target, rows[1]), :])
+            mail.send(t + 2, high_ref.at[span, pl.ds(*rows), :], dst_low.at[span, pl.ds(target, rows[1]), :])
+
+    def natural(ref):
+        def plane(g, k, r):
+            value = ref[16 * g + k, r:r + 16, :].astype(jnp.float32)
+            return value[0:8], value[8:16]
+        return plane
+
+    pack(natural(phi_ref), to_low, to_high, 0)
+    greeted()
+    send_sides(to_low, to_high, from_low, from_high, 0)
+    for ref, target, rows in ((phi_ref, x_phi, 8), (eps_ref, x_eps, 16), (charge_ref, x_charge, 8)):
+        mail.send(1, ref.at[:, pl.ds(0, rows), :], target.at[1])
+        mail.send(7, ref.at[:, pl.ds(TX - rows, rows), :], target.at[0])
+    pack(natural(eps_ref), to_low, to_high, GROUPS)
+    send_sides(to_low, to_high, from_low, from_high, GROUPS)
+    pack(natural(charge_ref), to_low, to_high, 2 * GROUPS)
+    send_sides(to_low, to_high, from_low, from_high, 2 * GROUPS)
+    for t, _ in beside():
+        mail.send(t, motion_ref, got_ref.at[8 - t])
+
+    def clear(m, _):
+        for ref in (*p_refs, *e_refs):
+            for g in (0, ROWS - 8):
                 ref[m, g:g + 8, :] = zero
-                return 0
-            lax.fori_loop(0, HALF + 2, clear, 0)
+        return 0
+    lax.fori_loop(0, HALF + 2, clear, 0)
     for ref in p_refs:
-        for g in range(0, ROWS, 8):
+        for g in blocks:
             ref[0, g:g + 8, :] = zero
             ref[HALF + 1, g:g + 8, :] = zero
+    for ref in (*ps_refs, *es_refs):
+        for g in (0, ROWS - 8):
+            for m in range(GROUPS + 2):
+                ref[m, g:g + 8, :] = zero
+    for ref in ps_refs:
+        for g in blocks:
+            ref[0, g:g + 8, :] = zero
+            ref[GROUPS + 1, g:g + 8, :] = zero
+
+    def two(refs, m, rows, a, b):
+        refs[0][m, rows, :] = jnp.where(even, a, b)
+        refs[1][m, rows, :] = jnp.where(even, b, a)
 
     def compact(m, _):
-        for r in range(0, ROWS - 16, 16):
+        for r in range(0, TX, 16):
             a = eps_ref[2 * m, r:r + 16, :].astype(jnp.float32)
             b = eps_ref[2 * m + 1, r:r + 16, :].astype(jnp.float32)
             for h in (0, 8):
-                a1, b1 = a[h:h + 8], b[h:h + 8]
-                e_refs[0][m + 1, r + 8 + h:r + 16 + h, :] = jnp.where(even, a1, b1)
-                e_refs[1][m + 1, r + 8 + h:r + 16 + h, :] = jnp.where(even, b1, a1)
-        for r in range(0, ROWS - 16, 8):
-            a = phi_ref[2 * m, r:r + 8, :]
-            b = phi_ref[2 * m + 1, r:r + 8, :]
-            p_refs[0][m + 1, r + 8:r + 16, :] = jnp.where(even, a, b)
-            p_refs[1][m + 1, r + 8:r + 16, :] = jnp.where(even, b, a)
+                two(e_refs, m + 1, slice(TOP + r + h, TOP + r + h + 8), a[h:h + 8], b[h:h + 8])
+        for r in range(0, TX, 8):
+            two(p_refs, m + 1, slice(TOP + r, TOP + r + 8), phi_ref[2 * m, r:r + 8, :], phi_ref[2 * m + 1, r:r + 8, :])
         return 0
     lax.fori_loop(0, HALF, compact, 0)
-    for g in range(8, ROWS - 8, 8):
+
+    mail.wait()
+    write_table(table_ref, lambda t: motion_ref[...] if t == 4 else got_ref[t])
+
+    def edges(m, _):
+        for side, g in ((0, 8), (1, TOP + TX)):
+            rows = slice(8, 16) if side == 0 else slice(0, 8)
+            a = x_eps[side, 2 * m].astype(jnp.float32)[rows]
+            b = x_eps[side, 2 * m + 1].astype(jnp.float32)[rows]
+            two(e_refs, m + 1, slice(g, g + 8), a, b)
+            two(p_refs, m + 1, slice(g, g + 8), x_phi[side, 2 * m], x_phi[side, 2 * m + 1])
+        return 0
+    lax.fori_loop(0, HALF, edges, 0)
+
+    def unpacked(low_ref, high_ref, at, r):
+        low, high = low_ref[at, r:r + 8, :], high_ref[at, r:r + 8, :]
+        return jnp.where(first, low, pltpu.roll(high, 8, 1)), jnp.where(first, pltpu.roll(low, 120, 1), high)
+
+    def strips(g, _):
+        for r in range(0, TX + 16, 8):
+            rows = slice(8 + r, 16 + r)
+            two(ps_refs, g + 1, rows, *unpacked(from_low, from_high, g, r))
+            two(es_refs, g + 1, rows, *unpacked(from_low, from_high, GROUPS + g, r))
+            two(gs_refs, g, slice(r, r + 8), *unpacked(from_low, from_high, 2 * GROUPS + g, r))
+        return 0
+    lax.fori_loop(0, GROUPS, strips, 0)
+    for g in blocks:
+        rows = slice(g, g + 8)
         for c in (0, 1):
-            e_refs[1 - c][0, g:g + 8, :] = e_refs[c][1, g:g + 8, :]
-            e_refs[1 - c][HALF + 1, g:g + 8, :] = e_refs[c][HALF, g:g + 8, :]
-
-    def sides(ref, m, g, low):
-        here = ref[m + 1, g:g + 8, :]
+            e_refs[1 - c][0, rows, :] = e_refs[c][1, rows, :]
+            e_refs[1 - c][HALF + 1, rows, :] = e_refs[c][HALF, rows, :]
+            es_refs[1 - c][0, rows, :] = pltpu.roll(es_refs[c][1, rows, :], 112, 1)
+            es_refs[1 - c][GROUPS + 1, rows, :] = pltpu.roll(es_refs[c][GROUPS, rows, :], 16, 1)
+
+    def main_sides(ref, strip_ref, m, g, low):
+        rows = slice(g, g + 8)
+        here = ref[m + 1, rows, :]
+        seam = pltpu.roll(strip_ref[m // 8 + 1, rows, :], 120 - 16 * (m % 8), 1)
         return (
             here,
-            jnp.where(low, ref[m, g:g + 8, :], ref[m + 2, g:g + 8, :]),
+            jnp.where(low, ref[m, rows, :], ref[m + 2, rows, :]),
             ref[m + 1, g - 1:g + 7, :],
             ref[m + 1, g + 1:g + 9, :],
-            pltpu.roll(here, 1, 1),
-            pltpu.roll(here, LANES - 1, 1),
+            pltpu.roll(jnp.where(lane == 127, seam, here), 1, 1),
+            pltpu.roll(jnp.where(lane == 0, seam, here), 127, 1),
         )
 
+    def strip_sides(ref, strip_ref, n, g, low):
+        rows = slice(g, g + 8)
+        here = strip_ref[n + 1, rows, :]
+        seam = zero
+        for k in range(8):
+            seam = jnp.where(slot == k, pltpu.roll(ref[8 * n + k + 1, rows, :], 16 * k + 8, 1), seam)
+        below = pltpu.roll(jnp.where(slot == 7, strip_ref[n, rows, :], here), 16, 1)
+        above = pltpu.roll(jnp.where(slot == 0, strip_ref[n + 2, rows, :], here), 112, 1)
+        return (
+            here,
+            jnp.where(low, below, above),
+            strip_ref[n + 1, g - 1:g + 7, :],
+            strip_ref[n + 1, g + 1:g + 9, :],
+            pltpu.roll(jnp.where(lane % 16 == 7, seam, here), 1, 1),
+            pltpu.roll(jnp.where(lane % 16 == 8, seam, here), 127, 1),
+        )
+
+    def weights(centre, sides, charge, c_ref, coef_ref, m, g):
+        faces = [0.5 * (centre + side) for side in sides]
+        total = faces[0]
+        for face in faces[1:]:
+            total = total + face
+        scale = OVER_RELAX / total
+        c_ref[m, g - 8:g, :] = scale * charge
+        for i in range(6):
+            coef_ref[i, m, g - 8:g, :] = scale * faces[i]
+
     for c in (0, 1):
-        low = even if c == 0 else ~even
-        def coefs(m, _):
-            for g in range(8, ROWS - 8, 8):
-                centre = e_refs[c][m + 1, g:g + 8, :]
-                faces = [0.5 * (centre + side) for side in sides(e_refs[1 - c], m, g, low)]
-                total = faces[0]
-                for face in faces[1:]:
-                    total = total + face
-                scale = jnp.where(inside & (total > 0.0), OVER_RELAX / total, 0.0)
-                ch = jnp.where(low, charge_ref[2 * m, g - 8:g, :], charge_ref[2 * m + 1, g - 8:g, :])
-                c_refs[c][m, g - 8:g, :] = scale * ch
-                for i in range(6):
-                    coef_refs[c][i, m, g - 8:g, :] = scale * faces[i]
+        low = odd if c else even
+
+        def main_weights(m, _):
+            for g in blocks:
+                if g == 8:
+                    a, b = x_charge[0, 2 * m], x_charge[0, 2 * m + 1]
+                elif g == TOP + TX:
+                    a, b = x_charge[1, 2 * m], x_charge[1, 2 * m + 1]
+                else:
+                    a, b = charge_ref[2 * m, g - TOP:g - TOP + 8, :], charge_ref[2 * m + 1, g - TOP:g - TOP + 8, :]
+                sides = main_sides(e_refs[1 - c], es_refs[1 - c], m, g, low)
+                weights(e_refs[c][m + 1, g:g + 8, :], sides, jnp.where(low, a, b), c_refs[c], coef_refs[c], m, g)
             return 0
-        lax.fori_loop(0, HALF, coefs, 0)
-
-    for step in range(DEPTH):
-        c = step % 2
-        low = even if c == 0 else ~even
-        reach = -(-(DEPTH - 1 - step) // 8) * 8
-        def half(m, _):
-            for g in range(TOP - reach, TOP + TX + reach, 8):
-                value = c_refs[c][m, g - 8:g, :] - (OVER_RELAX - 1.0) * p_refs[c][m + 1, g:g + 8, :]
-                for i, side in enumerate(sides(p_refs[1 - c], m, g, low)):
-                    value = value + coef_refs[c][i, m, g - 8:g, :] * side
-                p_refs[c][m + 1, g:g + 8, :] = value
+        lax.fori_loop(0, HALF, main_weights, 0)
+
+        def strip_weights(n, _):
+            for g in blocks:
+                sides = strip_sides(e_refs[1 - c], es_refs[1 - c], n, g, low)
+                weights(es_refs[c][n + 1, g:g + 8, :], sides, gs_refs[c][n, g - 8:g, :], cs_refs[c], coefs_refs[c], n, g)
             return 0
-        lax.fori_loop(0, HALF, half, 0)
-
-    evn = parity_mask(0, (8, TY))
+        lax.fori_loop(0, GROUPS, strip_weights, 0)
+
+    def updated(own, sides, c_ref, coef_ref, m, g):
+        value = c_ref[m, g - 8:g, :] - (OVER_RELAX - 1.0) * own
+        for i, side in enumerate(sides):
+            value = value + coef_ref[i, m, g - 8:g, :] * side
+        return value
+
+    def step(c, inner):
+        low = odd if c else even
+
+        def main_step(m, _):
+            for g in blocks[1:-1] if inner else blocks:
+                sides = main_sides(p_refs[1 - c], ps_refs[1 - c], m, g, low)
+                p_refs[c][m + 1, g:g + 8, :] = updated(p_refs[c][m + 1, g:g + 8, :], sides, c_refs[c], coef_refs[c], m, g)
+            return 0
+        lax.fori_loop(0, HALF, main_step, 0)
+        if inner:
+            return
+
+        def strip_step(n, _):
+            for g in blocks:
+                sides = strip_sides(p_refs[1 - c], ps_refs[1 - c], n, g, low)
+                ps_refs[c][n + 1, g:g + 8, :] = updated(ps_refs[c][n + 1, g:g + 8, :], sides, cs_refs[c], coefs_refs[c], n, g)
+            return 0
+        lax.fori_loop(0, GROUPS, strip_step, 0)
+
+    def three(i, _):
+        step(0, False)
+        step(1, False)
+        return 0
+    lax.fori_loop(0, 3, three, 0)
+    step(0, False)
+    step(1, True)
+
+    def coloured(g, k, r):
+        value = p_refs[k % 2][8 * g + k // 2 + 1, TOP + r:TOP + r + 16, :]
+        return value[0:8], value[8:16]
+
+    for c in (0, 1):
+        mail.send(1, p_refs[c].at[pl.ds(1, HALF), pl.ds(TOP, 8), :], x2_refs[c].at[1])
+        mail.send(7, p_refs[c].at[pl.ds(1, HALF), pl.ds(TOP + TX - 8, 8), :], x2_refs[c].at[0])
+    pack(coloured, to2_low, to2_high, 0)
+    send_sides(to2_low, to2_high, from2_low, from2_high, 0)
+    mail.wait()
+
+    def edges2(m, _):
+        for c in (0, 1):
+            p_refs[c][m + 1, 8:16, :] = x2_refs[c][0, m]
+            p_refs[c][m + 1, TOP + TX:TOP + TX + 8, :] = x2_refs[c][1, m]
+        return 0
+    lax.fori_loop(0, HALF, edges2, 0)
+
+    def strips2(g, _):
+        for r in range(0, TX + 16, 8):
+            a, b = unpacked(from2_low, from2_high, g, r)
+            ps_refs[0][g + 1, 8 + r:16 + r, :] = a
+            ps_refs[1][g + 1, 8 + r:16 + r, :] = b
+        return 0
+    lax.fori_loop(0, GROUPS, strips2, 0)
+    step(0, False)
+    step(1, False)
+    step(0, False)
+    step(1, True)
+
     def out(m, _):
         for g in range(0, TX, 8):
-            a = p_refs[0][m + 1, TOP + g:TOP + g + 8, 0:TY]
-            b = p_refs[1][m + 1, TOP + g:TOP + g + 8, 0:TY]
-            ea = e_refs[0][m + 1, TOP + g:TOP + g + 8, 0:TY]
-            eb = e_refs[1][m + 1, TOP + g:TOP + g + 8, 0:TY]
-            lo, hi = jnp.where(evn, a, b), jnp.where(evn, b, a)
-            elo, ehi = jnp.where(evn, ea, eb), jnp.where(evn, eb, ea)
+            a, b = [ref[m + 1, TOP + g:TOP + g + 8, :] for ref in p_refs]
+            ea, eb = [ref[m + 1, TOP + g:TOP + g + 8, :] for ref in e_refs]
+            lo, hi = jnp.where(even, a, b), jnp.where(even, b, a)
+            elo, ehi = jnp.where(even, ea, eb), jnp.where(even, eb, ea)
             pot_ref[2 * m, g:g + 8, :] = lo
             pot_ref[2 * m + 1, g:g + 8, :] = hi
             q_ref[2 * m, g:g + 8, :] = 0.5 * elo * lo * lo
@@ -118,22 +329,41 @@
         return 0
     lax.fori_loop(0, HALF, out, 0)
 
-def relax(eps_p, charge_p, phi_p):
+
+def relax(eps, charge, phi, motion):
     vm = lambda *s: pltpu.VMEM(s, jnp.float32)
+    spec = pl.BlockSpec(memory_space=pltpu.VMEM)
     return pl.pallas_call(
         relax_kernel,
-        out_shape=(jax.ShapeDtypeStruct((NZ, TX, TY), jnp.float32),) * 2,
-        in_specs=[pl.BlockSpec(memory_space=pltpu.VMEM)] * 3,
-        out_specs=(pl.BlockSpec(memory_space=pltpu.VMEM),) * 2,
+        out_shape=(
+            jax.ShapeDtypeStruct((NZ, TX, TY), jnp.float32),
+            jax.ShapeDtypeStruct((NZ, TX, TY), jnp.float32),
+            jax.ShapeDtypeStruct((8, SLOTS_PAD), jnp.float32),
+        ),
+        in_specs=[spec] * 4,
+        out_specs=(spec,) * 3,
         scratch_shapes=[
-            [vm(HALF + 2, ROWS, LANES)] * 2,
-            [vm(HALF + 2, ROWS, LANES)] * 2,
-            [vm(HALF, ROWS - 16, LANES)] * 2,
-            [vm(6, HALF, ROWS - 16, LANES)] * 2,
+            [vm(HALF + 2, ROWS, 128)] * 2,
+            [vm(HALF + 2, ROWS, 128)] * 2,
+            [vm(GROUPS + 2, ROWS, 128)] * 2,
+            [vm(GROUPS + 2, ROWS, 128)] * 2,
+            [vm(GROUPS, ROWS - 16, 128)] * 2,
+            [vm(HALF, ROWS - 16, 128)] * 2,
+            [vm(6, HALF, ROWS - 16, 128)] * 2,
+            [vm(GROUPS, ROWS - 16, 128)] * 2,
+            [vm(6, GROUPS, ROWS - 16, 128)] * 2,
+            vm(3 * GROUPS, TX, 128), vm(3 * GROUPS, TX, 128),
+            vm(3 * GROUPS, TX + 16, 128), vm(3 * GROUPS, TX + 16, 128),
+            pltpu.VMEM((2, NZ, 16, 128), jnp.bfloat16), vm(2, NZ, 8, 128), vm(2, NZ, 8, 128),
+            vm(GROUPS, TX, 128), vm(GROUPS, TX, 128),
+            vm(GROUPS, TX + 16, 128), vm(GROUPS, TX + 16, 128),
+            [vm(2, HALF, 8, 128)] * 2,
+            vm(9, 8, 128),
+            pltpu.SemaphoreType.DMA((42,)), pltpu.SemaphoreType.DMA((42,)),
         ],
         name="relax",
-        compiler_params=pltpu.CompilerParams(vmem_limit_bytes=62 * 2**20),
-    )(eps_p, charge_p, phi_p)
+        compiler_params=pltpu.CompilerParams(vmem_limit_bytes=58 * 2**20, collective_id=0, has_side_effects=True),
+    )(eps, charge, phi, motion)
 
 
 CHUNK = 4096
@@ -297,52 +527,9 @@
     )(direction, slot, pop, rb, table, lattice_table())
 
 
-def beside():
-    x, y = lax.axis_index("gx"), lax.axis_index("gy")
-    for t in range(9):
-        if t != 4:
-            yield t, (lax.rem(x + t // 3 - 1 + TILES_X, TILES_X), lax.rem(y + t % 3 - 1 + TILES_Y, TILES_Y))
-
-
-def greet():
-    barrier = pltpu.get_barrier_semaphore()
-    for _, device in beside():
-        pl.semaphore_signal(barrier, inc=1, device_id=device, device_id_type=pl.DeviceIdType.MESH)
-    pl.semaphore_wait(barrier, 8)
-
-
-def post(source, got_ref, send_sem, recv_sem):
-    copies = []
-    for t, device in beside():
-        copy = pltpu.make_async_remote_copy(
-            src_ref=source(t), dst_ref=got_ref.at[8 - t], send_sem=send_sem.at[t], recv_sem=recv_sem.at[8 - t],
-            device_id=device, device_id_type=pl.DeviceIdType.MESH,
-        )
-        copy.start()
-        copies.append(copy)
-    return copies
-
-
-def write_table(table_ref, block):
-    for tile in range(3):
-        total = jnp.zeros((8, 128), jnp.float32)
-        for i in range(4):
-            if 4 * tile + i < 9:
-                value = block(4 * tile + i)
-                total = total + (pltpu.roll(value, NC_DEV * i, 1) if i else value)
-        table_ref[:, 128 * tile:128 * tile + 128] = total
-
-
-def share_kernel(motion_ref, table_ref, got_ref, send_sem, recv_sem):
-    greet()
-    copies = post(lambda t: motion_ref, got_ref, send_sem, recv_sem)
-    for copy in copies:
-        copy.wait()
-    write_table(table_ref, lambda t: motion_ref[...] if t == 4 else got_ref[t])
-
-
-def update_kernel(sums_ref, motion_ref, report_ref, table_ref, part_ref, got_ref, new_ref, back_ref, send_sem, recv_sem, send2_sem, recv2_sem):
-    greet()
+def update_kernel(sums_ref, motion_ref, report_ref, table_ref, part_ref, got_ref, new_ref, back_ref, send_sem, recv_sem):
+    greeted = greet()
+    mail = Mail(send_sem, recv_sem)
     lane = lax.broadcasted_iota(jnp.int32, (8, 128), 1)
     row = lax.broadcasted_iota(jnp.int32, (8, 128), 0)
     for t in range(9):
@@ -350,10 +537,11 @@
         if t % 4:
             value = pltpu.roll(value, 128 - NC_DEV * (t % 4), 1)
         part_ref[t] = jnp.where(lane < NC_DEV, value, 0.0)
-    copies = post(lambda t: part_ref.at[t], got_ref, send_sem, recv_sem)
+    greeted()
+    for t, _ in beside():
+        mail.send(t, part_ref.at[t], got_ref.at[8 - t])
     total = part_ref[4]
-    for copy in copies:
-        copy.wait()
+    mail.wait()
     for t in range(9):
         if t != 4:
             total = total + got_ref[t]
@@ -361,25 +549,13 @@
     inertia = 0.4 * mass * RADIUS**2
     report_ref[...] = jnp.where(row < 3, total, total / RADIUS)
     new_ref[...] = motion_ref[...] + jnp.where(row < 3, total / mass, total / inertia)
-    copies = post(lambda t: new_ref, back_ref, send2_sem, recv2_sem)
-    for copy in copies:
-        copy.wait()
+    for t, _ in beside():
+        mail.send(t, new_ref, back_ref.at[8 - t])
+    mail.wait()
     write_table(table_ref, lambda t: new_ref[...] if t == 4 else back_ref[t])
 
 
 VM = pl.BlockSpec(memory_space=pltpu.VMEM)
-
-
-def share_motion(motion):
-    return pl.pallas_call(
-        share_kernel,
-        out_shape=jax.ShapeDtypeStruct((8, SLOTS_PAD), jnp.float32),
-        in_specs=[VM],
-        out_specs=VM,
-        scratch_shapes=[pltpu.VMEM((9, 8, 128), jnp.float32), pltpu.SemaphoreType.DMA((9,)), pltpu.SemaphoreType.DMA((9,))],
-        name="share_motion",
-        compiler_params=pltpu.CompilerParams(collective_id=0, has_side_effects=True),
-    )(motion)
 
 
 def update(sums, motion):
@@ -391,26 +567,11 @@
         scratch_shapes=[
             pltpu.VMEM((9, 8, 128), jnp.float32), pltpu.VMEM((9, 8, 128), jnp.float32),
             pltpu.VMEM((8, 128), jnp.float32), pltpu.VMEM((9, 8, 128), jnp.float32),
-            pltpu.SemaphoreType.DMA((9,)), pltpu.SemaphoreType.DMA((9,)), pltpu.SemaphoreType.DMA((9,)), pltpu.SemaphoreType.DMA((9,)),
+            pltpu.SemaphoreType.DMA((16,)), pltpu.SemaphoreType.DMA((16,)),
         ],
         name="update",
         compiler_params=pltpu.CompilerParams(collective_id=1, has_side_effects=True),
     )(sums, motion)
-
-
-def neighbours(axis, value_low, value_high):
-    count = lax.axis_size(axis)
-    forward = [(i, (i + 1) % count) for i in range(count)]
-    backward = [(target, source) for source, target in forward]
-    return lax.ppermute(value_low, axis, forward), lax.ppermute(value_high, axis, backward)
-
-
-def framed(block):
-    low, high = neighbours("gx", block[:, TX - 16:], block[:, :16])
-    block = jnp.concatenate([low, block, high], axis=1)
-    low, high = neighbours("gy", block[:, :, TY - 16:], block[:, :, :16])
-    gap = jnp.zeros((NZ, TX + 32, LANES - TY - 32), block.dtype)
-    return jnp.concatenate([block, high, gap, low], axis=2)
 
 
 def shards(
@@ -419,8 +580,7 @@
 ):
     flat = lambda a: a.reshape(LINKS // 128, 128)
     motion = jnp.pad(jnp.concatenate([colloid_vel, colloid_spin], axis=0), ((0, 2), (0, 128 - NC_DEV)))
-    table = share_motion(motion)
-    potential, q = relax(framed(eps_field), framed(charge), framed(potential_start))
+    potential, q, table = relax(eps_field, charge, potential_start, motion)
     row = link_depth.reshape(-1) * TX + (link_site.reshape(-1) >> 7)
     rb = link_rb.reshape(3, LINKS // 128, 128)
     slot, sums = link_sums(

time: 216 us -> 169 us (0.78)
  local copies, waits for them, and re-layouts: 48.4 us -> 5.21 us
  Pallas kernels: 126 us -> 160 us
  starting transfers between devices: 23.4 us -> 0 us
  other arithmetic: 12.8 us -> 1.51 us
  waiting for transfers between devices: 3.08 us -> 0 us
    pallas_call x1, Pallas kernels: 49.6 us -> 99.7 us  [relax(): pl.pallas_call(relax_kernel, out_shape=(jax.ShapeDtypeStruct((NZ, TX, TY)...]
    ppermute x12 -> x0, starting transfers between devices: 23.4 us -> none  [the longest x6 22.8 us: neighbours(): lax.ppermute(value_high, axis, backward)]
    slice x12 -> x0, local copies, waits for them, and re-layouts: 23 us -> none  [the longest x9 18.7 us: framed(): low, high = neighbours('gy', block[:, :, TY - 16:], block[:, :, :16])]
    ppermute x6 -> x0, local copies, waits for them, and re-layouts: 15.3 us -> none  [the longest x3 7.66 us: neighbours(): lax.ppermute(value_low, axis, forward)]
    pallas_call x1 -> x0, Pallas kernels: 12.2 us -> none  [share_motion(): pl.pallas_call(share_kernel, out_shape=jax.ShapeDtypeStruct((8, SLOTS_PAD...]
    concatenate x2 -> x0, other arithmetic: 12 us -> none  [framed(): return jnp.concatenate([block, high, gap, low], axis=2)]
    unnamed x41 -> x28, local copies, waits for them, and re-layouts: 8.89 us -> 5.21 us
    pallas_call x1, Pallas kernels: 17.3 us -> 13.7 us  [update(): pl.pallas_call(update_kernel, out_shape=(jax.ShapeDtypeStruct((8, 128), j...]
  transfers between devices with their start and end apart: 12 -> 0, of which waited for: 2 -> 0; matrix products, arithmetic and copies ran while one was open for 20% -> 0% of each run, Pallas kernels for 6% -> 0%
where the time goes in v2:
time: 169 us; the launch traced here: 167 us
  Pallas kernels  160 us (95%)
  local copies, waits for them, and re-layouts  5.21 us (3%)
    pallas_call x1, Pallas kernels, relax(): pl.pallas_call(relax_kernel, out_shape=(jax.ShapeDtypeStruct((NZ, TX, TY)...  99.7 us
    pallas_call x1, Pallas kernels, link_sums(): pl.pallas_call(links_kernel, grid=(LINKS // CHUNK,), in_specs=[pl.BlockSp...  38 us
    pallas_call x1, Pallas kernels, update(): pl.pallas_call(update_kernel, out_shape=(jax.ShapeDtypeStruct((8, 128), j...  13.7 us
    pallas_call x1, Pallas kernels, reflect(): pl.pallas_call(reflect_kernel, grid=(LINKS // CHUNK,), in_specs=[link_spe...  8.68 us
    unnamed x28, local copies, waits for them, and re-layouts  5.21 us

profile of v2, /device:TPU:0, one launch (start us, length us, event | category | flops | bytes accessed | tf_op | source)
XLA Modules:
  0.0 167.4 jit_solution(10938756037376704082)
XLA Ops:
  0.6 1.3 select_maximum_fusion.motion_ref
  1.9 0.0 copy-start.4
  2.0 0.0 copy-start.5
  2.0 0.0 copy-start.6
  2.0 99.7 %relax.1 = (f32[48,64,128]{2,1,0:T(8,128)}, f32[48,64,128]{2,1,0:T(8,128)}, f32[8,384]{1,0:T(8,128)}) custom-call(bf16[48,64,128]{2,1,0:T(8,128)(2,1)} %eps_ref.1, f32[48,64,128]{2,1,0:T(8,128)} %charge_ref.1, f32[48,64,128]{2,1,0:T(8,128)} %phi_ref.1, f32[8,128]{1,0:T(8,128)} %select_maximum_fusion.motion_ref), custom_call_target="tpu_custom_call" | custom-call | tf_op jit(solution)/shard_map/relax/pallas_call | solution.py:336
  101.6 0.0 copy-done.2
  101.7 0.0 copy-done.11
  101.7 0.2 shift-right-arithmetic_add_fusion
  101.9 0.0 copy-done.1
  101.9 0.0 copy-done.3
  101.9 0.0 copy-done.4
  101.9 0.0 copy-done.5
  101.9 0.0 copy-done.6
  101.9 0.0 copy-start
  101.9 1.4 copy-done
  103.3 0.7 copy-done.9
  104.0 38.0 %link_sums.1 = (s32[256,128]{1,0:T(8,128)S(1)}, f32[8,384]{1,0:T(8,128)S(1)}) custom-call(s32[32768]{0:T(1024)S(1)} %bitcast.13, s32[256,128]{1,0:T(8,128)S(1)} %bitcast.12, s32[256,128]{1,0:T(8,128)S(1)} %bitcast.14, s32[256,128]{1,0:T(8,128)S(1)} %bitcast.18, f32[256,128]{1,0:T(8,128)S(1)} %bitcast.16, f32[3,256,128]{2,1,0:T(8,128)S(1)} %bitcast.10, ...), custom_call_target="tpu_custom_call" | custom-call | tf_op jit(solution)/shard_map/link_sums/pallas_call | solution.py:485
  142.0 0.6 copy-done.7
  142.6 13.7 %update.1 = (f32[8,128]{1,0:T(8,128)}, f32[8,384]{1,0:T(8,128)}) custom-call(f32[8,384]{1,0:T(8,128)} %copy-done.7, f32[8,128]{1,0:T(8,128)} %select_maximum_fusion.motion_ref), custom_call_target="tpu_custom_call" | custom-call | tf_op jit(solution)/shard_map/update/pallas_call | solution.py:562
  156.3 0.7 copy-done.8
  157.0 8.7 %reflect.1 = f32[256,128]{1,0:T(8,128)} custom-call(s32[256,128]{1,0:T(8,128)S(1)} %bitcast.15, s32[256,128]{1,0:T(8,128)S(1)} %get-tuple-element.15.slot_ref, f32[256,128]{1,0:T(8,128)S(1)} %bitcast.17, f32[3,256,128]{2,1,0:T(8,128)S(1)} %bitcast.11, f32[8,384]{1,0:T(8,128)S(1)} %copy-done.8, f32[32,128]{1,0:T(8,128)S(1)} %copy-done.6), custom_call_target="tpu_custom_call" | custom-call | tf_op jit(solution)/shard_map/reflect/pallas_call | solution.py:518
  165.7 1.1 copy.18
  166.8 0.0 copy-done.12
  166.9 0.6 copy.19
  (10 shorter events, 0.0 us)
Async XLA Ops:
  1.9 99.7 %copy-start.2 = (s32[1,1,32768]{2,1,0:T(1,128)S(1)}, s32[1,1,32768]{2,1,0:T(1,128)}, u32[]{:S(2)}) copy-start(s32[1,1,32768]{2,1,0:T(1,128)} %param.20) | copy-start | bytes 393220
  1.9 99.7 %copy-start.11 = (s32[1,1,32768]{2,1,0:T(1,128)S(1)}, s32[1,1,32768]{2,1,0:T(1,128)}, u32[]{:S(2)}) copy-start(s32[1,1,32768]{2,1,0:T(1,128)} %param.21) | copy-start | bytes 393220
  1.9 99.9 %copy-start.1 = (f32[3,1,1,32768]{3,2,1,0:T(1,128)S(1)}, f32[3,1,1,32768]{3,2,1,0:T(1,128)}, u32[]{:S(2)}) copy-start(f32[3,1,1,32768]{3,2,1,0:T(1,128)} %param.23) | copy-start | bytes 1179652
  1.9 100.0 %copy-start.3 = (s32[1,1,32768]{2,1,0:T(1,128)S(1)}, s32[1,1,32768]{2,1,0:T(1,128)}, u32[]{:S(2)}) copy-start(s32[1,1,32768]{2,1,0:T(1,128)} %param.18) | copy-start | bytes 393220
  1.9 100.0 %copy-start.4 = (f32[1,1,32768]{2,1,0:T(1,128)S(1)}, f32[1,1,32768]{2,1,0:T(1,128)}, u32[]{:S(2)}) copy-start(f32[1,1,32768]{2,1,0:T(1,128)} %param.22) | copy-start | bytes 393220
  2.0 100.0 %copy-start.5 = (s32[1,1,32768]{2,1,0:T(1,128)S(1)}, s32[1,1,32768]{2,1,0:T(1,128)}, u32[]{:S(2)}) copy-start(s32[1,1,32768]{2,1,0:T(1,128)} %param.19) | copy-start | bytes 393220
  2.0 100.0 %copy-start.6 = (f32[32,128]{1,0:T(8,128)S(1)}, f32[32,128]{1,0:T(8,128)}, u32[]{:S(2)}) copy-start(f32[32,128]{1,0:T(8,128)} %constant.9.clone.lat_ref) | copy-start | bytes 49156
  101.9 1.4 copy-start
  103.3 0.7 copy-start.9
  104.0 61.7 %copy-start.10 = (f32[48,64,128]{2,1,0:T(8,128)S(1)}, f32[48,64,128]{2,1,0:T(8,128)}, u32[]{:S(2)}) copy-start(f32[48,64,128]{2,1,0:T(8,128)} %get-tuple-element.20) | copy-start | bytes 4718596
  142.0 0.6 copy-start.7
  156.3 0.7 copy-start.8
  165.7 1.1 copy-start.12

commit v3 on v2

--- a/solution.py
+++ b/solution.py
@@ -19,6 +19,8 @@
 GROUPS = HALF // 8
 ROWS = 96
 TOP = 16
+UNROLL = 8
+WU = 4
 
 
 def beside():
@@ -66,7 +68,7 @@
 
 def relax_kernel(
     eps_ref, charge_ref, phi_ref, motion_ref, pot_ref, q_ref, table_ref,
-    p_refs, e_refs, ps_refs, es_refs, gs_refs, c_refs, coef_refs, cs_refs, coefs_refs,
+    p_refs, e_refs, ps_refs, es_refs, gs_refs, seam_refs, c_refs, coef_refs, cs_refs, coefs_refs,
     to_low, to_high, from_low, from_high, x_eps, x_charge, x_phi, to2_low, to2_high, from2_low, from2_high, x2_refs,
     got_ref, send_sem, recv_sem,
 ):
@@ -110,16 +112,21 @@
             return value[0:8], value[8:16]
         return plane
 
-    pack(natural(phi_ref), to_low, to_high, 0)
-    greeted()
-    send_sides(to_low, to_high, from_low, from_high, 0)
-    for ref, target, rows in ((phi_ref, x_phi, 8), (eps_ref, x_eps, 16), (charge_ref, x_charge, 8)):
+    def send_rows(ref, target, rows):
         mail.send(1, ref.at[:, pl.ds(0, rows), :], target.at[1])
         mail.send(7, ref.at[:, pl.ds(TX - rows, rows), :], target.at[0])
+
     pack(natural(eps_ref), to_low, to_high, GROUPS)
+    greeted()
     send_sides(to_low, to_high, from_low, from_high, GROUPS)
+    send_rows(eps_ref, x_eps, 16)
+    send_rows(charge_ref, x_charge, 8)
     pack(natural(charge_ref), to_low, to_high, 2 * GROUPS)
     send_sides(to_low, to_high, from_low, from_high, 2 * GROUPS)
+    early, mail.copies = mail.copies, []
+    send_rows(phi_ref, x_phi, 8)
+    pack(natural(phi_ref), to_low, to_high, 0)
+    send_sides(to_low, to_high, from_low, from_high, 0)
     for t, _ in beside():
         mail.send(t, motion_ref, got_ref.at[8 - t])
 
@@ -157,8 +164,8 @@
         return 0
     lax.fori_loop(0, HALF, compact, 0)
 
-    mail.wait()
-    write_table(table_ref, lambda t: motion_ref[...] if t == 4 else got_ref[t])
+    for copy in early:
+        copy.wait()
 
     def edges(m, _):
         for side, g in ((0, 8), (1, TOP + TX)):
@@ -166,7 +173,6 @@
             a = x_eps[side, 2 * m].astype(jnp.float32)[rows]
             b = x_eps[side, 2 * m + 1].astype(jnp.float32)[rows]
             two(e_refs, m + 1, slice(g, g + 8), a, b)
-            two(p_refs, m + 1, slice(g, g + 8), x_phi[side, 2 * m], x_phi[side, 2 * m + 1])
         return 0
     lax.fori_loop(0, HALF, edges, 0)
 
@@ -177,7 +183,6 @@
     def strips(g, _):
         for r in range(0, TX + 16, 8):
             rows = slice(8 + r, 16 + r)
-            two(ps_refs, g + 1, rows, *unpacked(from_low, from_high, g, r))
             two(es_refs, g + 1, rows, *unpacked(from_low, from_high, GROUPS + g, r))
             two(gs_refs, g, slice(r, r + 8), *unpacked(from_low, from_high, 2 * GROUPS + g, r))
         return 0
@@ -190,10 +195,22 @@
             es_refs[1 - c][0, rows, :] = pltpu.roll(es_refs[c][1, rows, :], 112, 1)
             es_refs[1 - c][GROUPS + 1, rows, :] = pltpu.roll(es_refs[c][GROUPS, rows, :], 16, 1)
 
-    def main_sides(ref, strip_ref, m, g, low):
+    def turn(seam_ref, n, g, value):
+        for k in range(8):
+            seam_ref[8 * n + k, g - 8:g, :] = pltpu.roll(value, 120 - 16 * k, 1)
+
+    def turn_all(strip_refs):
+        def one(n, _):
+            for g in blocks:
+                for c in (0, 1):
+                    turn(seam_refs[c], n, g, strip_refs[c][n + 1, g:g + 8, :])
+            return 0
+        lax.fori_loop(0, GROUPS, one, 0)
+
+    def main_sides(ref, seam_ref, m, g, low):
         rows = slice(g, g + 8)
         here = ref[m + 1, rows, :]
-        seam = pltpu.roll(strip_ref[m // 8 + 1, rows, :], 120 - 16 * (m % 8), 1)
+        seam = seam_ref[m, g - 8:g, :]
         return (
             here,
             jnp.where(low, ref[m, rows, :], ref[m + 2, rows, :]),
@@ -220,6 +237,8 @@
             pltpu.roll(jnp.where(lane % 16 == 8, seam, here), 127, 1),
         )
 
+    turn_all(es_refs)
+
     def weights(centre, sides, charge, c_ref, coef_ref, m, g):
         faces = [0.5 * (centre + side) for side in sides]
         total = faces[0]
@@ -233,18 +252,20 @@
     for c in (0, 1):
         low = odd if c else even
 
-        def main_weights(m, _):
-            for g in blocks:
-                if g == 8:
-                    a, b = x_charge[0, 2 * m], x_charge[0, 2 * m + 1]
-                elif g == TOP + TX:
-                    a, b = x_charge[1, 2 * m], x_charge[1, 2 * m + 1]
-                else:
-                    a, b = charge_ref[2 * m, g - TOP:g - TOP + 8, :], charge_ref[2 * m + 1, g - TOP:g - TOP + 8, :]
-                sides = main_sides(e_refs[1 - c], es_refs[1 - c], m, g, low)
-                weights(e_refs[c][m + 1, g:g + 8, :], sides, jnp.where(low, a, b), c_refs[c], coef_refs[c], m, g)
+        def main_weights(n, _):
+            for k in range(WU):
+                m = WU * n + k
+                for g in blocks:
+                    if g == 8:
+                        a, b = x_charge[0, 2 * m], x_charge[0, 2 * m + 1]
+                    elif g == TOP + TX:
+                        a, b = x_charge[1, 2 * m], x_charge[1, 2 * m + 1]
+                    else:
+                        a, b = charge_ref[2 * m, g - TOP:g - TOP + 8, :], charge_ref[2 * m + 1, g - TOP:g - TOP + 8, :]
+                    sides = main_sides(e_refs[1 - c], seam_refs[1 - c], m, g, low)
+                    weights(e_refs[c][m + 1, g:g + 8, :], sides, jnp.where(low, a, b), c_refs[c], coef_refs[c], m, g)
             return 0
-        lax.fori_loop(0, HALF, main_weights, 0)
+        lax.fori_loop(0, HALF // WU, main_weights, 0)
 
         def strip_weights(n, _):
             for g in blocks:
@@ -254,29 +275,52 @@
         lax.fori_loop(0, GROUPS, strip_weights, 0)
 
     def updated(own, sides, c_ref, coef_ref, m, g):
-        value = c_ref[m, g - 8:g, :] - (OVER_RELAX - 1.0) * own
-        for i, side in enumerate(sides):
-            value = value + coef_ref[i, m, g - 8:g, :] * side
-        return value
+        parts = [coef_ref[i, m, g - 8:g, :] * side for i, side in enumerate(sides)]
+        first_part = c_ref[m, g - 8:g, :] - (OVER_RELAX - 1.0) * own
+        return ((first_part + parts[0]) + (parts[1] + parts[2])) + (parts[3] + (parts[4] + parts[5]))
 
     def step(c, inner):
         low = odd if c else even
 
-        def main_step(m, _):
-            for g in blocks[1:-1] if inner else blocks:
-                sides = main_sides(p_refs[1 - c], ps_refs[1 - c], m, g, low)
-                p_refs[c][m + 1, g:g + 8, :] = updated(p_refs[c][m + 1, g:g + 8, :], sides, c_refs[c], coef_refs[c], m, g)
+        def main_step(n, _):
+            for k in range(UNROLL):
+                m = UNROLL * n + k
+                chosen = blocks[1:-1] if inner else blocks
+                values = []
+                for g in chosen:
+                    sides = main_sides(p_refs[1 - c], seam_refs[1 - c], m, g, low)
+                    values.append(updated(p_refs[c][m + 1, g:g + 8, :], sides, c_refs[c], coef_refs[c], m, g))
+                for g, value in zip(chosen, values):
+                    p_refs[c][m + 1, g:g + 8, :] = value
             return 0
-        lax.fori_loop(0, HALF, main_step, 0)
+        lax.fori_loop(0, HALF // UNROLL, main_step, 0)
         if inner:
             return
 
         def strip_step(n, _):
             for g in blocks:
                 sides = strip_sides(p_refs[1 - c], ps_refs[1 - c], n, g, low)
-                ps_refs[c][n + 1, g:g + 8, :] = updated(ps_refs[c][n + 1, g:g + 8, :], sides, cs_refs[c], coefs_refs[c], n, g)
+                value = updated(ps_refs[c][n + 1, g:g + 8, :], sides, cs_refs[c], coefs_refs[c], n, g)
+                ps_refs[c][n + 1, g:g + 8, :] = value
+                turn(seam_refs[c], n, g, value)
             return 0
         lax.fori_loop(0, GROUPS, strip_step, 0)
+
+    mail.wait()
+    write_table(table_ref, lambda t: motion_ref[...] if t == 4 else got_ref[t])
+
+    def edges1(m, _):
+        for side, g in ((0, 8), (1, TOP + TX)):
+            two(p_refs, m + 1, slice(g, g + 8), x_phi[side, 2 * m], x_phi[side, 2 * m + 1])
+        return 0
+    lax.fori_loop(0, HALF, edges1, 0)
+
+    def strips1(g, _):
+        for r in range(0, TX + 16, 8):
+            two(ps_refs, g + 1, slice(8 + r, 16 + r), *unpacked(from_low, from_high, g, r))
+        return 0
+    lax.fori_loop(0, GROUPS, strips1, 0)
+    turn_all(ps_refs)
 
     def three(i, _):
         step(0, False)
@@ -311,6 +355,7 @@
             ps_refs[1][g + 1, 8 + r:16 + r, :] = b
         return 0
     lax.fori_loop(0, GROUPS, strips2, 0)
+    turn_all(ps_refs)
     step(0, False)
     step(1, False)
     step(0, False)
@@ -348,6 +393,7 @@
             [vm(GROUPS + 2, ROWS, 128)] * 2,
             [vm(GROUPS + 2, ROWS, 128)] * 2,
             [vm(GROUPS, ROWS - 16, 128)] * 2,
+            [vm(HALF, ROWS - 16, 128)] * 2,
             [vm(HALF, ROWS - 16, 128)] * 2,
             [vm(6, HALF, ROWS - 16, 128)] * 2,
             [vm(GROUPS, ROWS - 16, 128)] * 2,

time: 169 us -> 128 us (0.76)
  Pallas kernels: 160 us -> 120 us
    pallas_call x1, Pallas kernels: 99.7 us -> 60.6 us  [relax(): pl.pallas_call(relax_kernel, out_shape=(jax.ShapeDtypeStruct((NZ, TX, TY)...]
where the time goes in v3:
time: 128 us; the launch traced here: 127 us
  Pallas kernels  120 us (94%)
  local copies, waits for them, and re-layouts  5.21 us (4%)
  other arithmetic  1.51 us (1%)
    pallas_call x1, Pallas kernels, relax(): pl.pallas_call(relax_kernel, out_shape=(jax.ShapeDtypeStruct((NZ, TX, TY)...  60.6 us
    pallas_call x1, Pallas kernels, link_sums(): pl.pallas_call(links_kernel, grid=(LINKS // CHUNK,), in_specs=[pl.BlockSp...  38 us
    pallas_call x1, Pallas kernels, update(): pl.pallas_call(update_kernel, out_shape=(jax.ShapeDtypeStruct((8, 128), j...  12.4 us
    pallas_call x1, Pallas kernels, reflect(): pl.pallas_call(reflect_kernel, grid=(LINKS // CHUNK,), in_specs=[link_spe...  8.68 us
    unnamed x28, local copies, waits for them, and re-layouts  5.21 us

profile of v3, /device:TPU:0, one launch (start us, length us, event | category | flops | bytes accessed | tf_op | source)
XLA Modules:
  0.0 127.1 jit_solution(11078643284721520119)
XLA Ops:
  0.6 1.3 %select_maximum_fusion.motion_ref = f32[8,128]{1,0:T(8,128)} fusion(f32[3,32]{1,0:T(4,128)} %param.17, f32[3,32]{1,0:T(4,128)} %param.16), kind=kLoop, calls=%fused_computation.1 | loop fusion | flops 8192 | bytes 4864 | tf_op jit(solution)/shard_map/concatenate | solution.py:628
  1.9 0.0 copy-start.4
  2.0 0.0 copy-start.5
  2.0 0.0 copy-start.6
  2.0 60.6 %relax.1 = (f32[48,64,128]{2,1,0:T(8,128)}, f32[48,64,128]{2,1,0:T(8,128)}, f32[8,384]{1,0:T(8,128)}) custom-call(bf16[48,64,128]{2,1,0:T(8,128)(2,1)} %eps_ref.1, f32[48,64,128]{2,1,0:T(8,128)} %charge_ref.1, f32[48,64,128]{2,1,0:T(8,128)} %phi_ref.1, f32[8,128]{1,0:T(8,128)} %select_maximum_fusion.motion_ref), custom_call_target="tpu_custom_call" | custom-call | tf_op jit(solution)/shard_map/relax/pallas_call | solution.py:381
  62.6 0.0 copy-done.2
  62.6 0.0 copy-done.11
  62.6 0.2 shift-right-arithmetic_add_fusion
  62.8 0.0 copy-done.1
  62.8 0.0 copy-done.3
  62.8 0.0 copy-done.4
  62.8 0.0 copy-done.5
  62.8 0.0 copy-done.6
  62.8 0.0 copy-start
  62.8 1.4 %copy-done = f32[48,64,128]{2,1,0:T(8,128)S(1)} copy-done((f32[48,64,128]{2,1,0:T(8,128)S(1)}, f32[48,64,128]{2,1,0:T(8,128)}, u32[]{:S(2)}) %copy-start) | copy-done | bytes 1572888
  64.2 0.7 copy-done.9
  65.0 38.0 %link_sums.1 = (s32[256,128]{1,0:T(8,128)S(1)}, f32[8,384]{1,0:T(8,128)S(1)}) custom-call(s32[32768]{0:T(1024)S(1)} %bitcast.13, s32[256,128]{1,0:T(8,128)S(1)} %bitcast.12, s32[256,128]{1,0:T(8,128)S(1)} %bitcast.14, s32[256,128]{1,0:T(8,128)S(1)} %bitcast.18, f32[256,128]{1,0:T(8,128)S(1)} %bitcast.16, f32[3,256,128]{2,1,0:T(8,128)S(1)} %bitcast.10, ...), custom_call_target="tpu_custom_call" | custom-call | tf_op jit(solution)/shard_map/link_sums/pallas_call | solution.py:531
  102.9 0.6 copy-done.7
  103.5 12.4 %update.1 = (f32[8,128]{1,0:T(8,128)}, f32[8,384]{1,0:T(8,128)}) custom-call(f32[8,384]{1,0:T(8,128)} %copy-done.7, f32[8,128]{1,0:T(8,128)} %select_maximum_fusion.motion_ref), custom_call_target="tpu_custom_call" | custom-call | tf_op jit(solution)/shard_map/update/pallas_call | solution.py:608
  116.0 0.7 copy-done.8
  116.7 8.7 %reflect.1 = f32[256,128]{1,0:T(8,128)} custom-call(s32[256,128]{1,0:T(8,128)S(1)} %bitcast.15, s32[256,128]{1,0:T(8,128)S(1)} %get-tuple-element.15.slot_ref, f32[256,128]{1,0:T(8,128)S(1)} %bitcast.17, f32[3,256,128]{2,1,0:T(8,128)S(1)} %bitcast.11, f32[8,384]{1,0:T(8,128)S(1)} %copy-done.8, f32[32,128]{1,0:T(8,128)S(1)} %copy-done.6), custom_call_target="tpu_custom_call" | custom-call | tf_op jit(solution)/shard_map/reflect/pallas_call | solution.py:564
  125.4 1.1 copy.18
  126.5 0.0 copy-done.12
  126.5 0.6 copy.19
  (10 shorter events, 0.0 us)
Async XLA Ops:
  1.9 60.6 %copy-start.2 = (s32[1,1,32768]{2,1,0:T(1,128)S(1)}, s32[1,1,32768]{2,1,0:T(1,128)}, u32[]{:S(2)}) copy-start(s32[1,1,32768]{2,1,0:T(1,128)} %param.20) | copy-start | bytes 393220
  1.9 60.6 %copy-start.11 = (s32[1,1,32768]{2,1,0:T(1,128)S(1)}, s32[1,1,32768]{2,1,0:T(1,128)}, u32[]{:S(2)}) copy-start(s32[1,1,32768]{2,1,0:T(1,128)} %param.21) | copy-start | bytes 393220
  1.9 60.9 %copy-start.1 = (f32[3,1,1,32768]{3,2,1,0:T(1,128)S(1)}, f32[3,1,1,32768]{3,2,1,0:T(1,128)}, u32[]{:S(2)}) copy-start(f32[3,1,1,32768]{3,2,1,0:T(1,128)} %param.23) | copy-start | bytes 1179652
  1.9 60.9 %copy-start.3 = (s32[1,1,32768]{2,1,0:T(1,128)S(1)}, s32[1,1,32768]{2,1,0:T(1,128)}, u32[]{:S(2)}) copy-start(s32[1,1,32768]{2,1,0:T(1,128)} %param.18) | copy-start | bytes 393220
  1.9 60.9 %copy-start.4 = (f32[1,1,32768]{2,1,0:T(1,128)S(1)}, f32[1,1,32768]{2,1,0:T(1,128)}, u32[]{:S(2)}) copy-start(f32[1,1,32768]{2,1,0:T(1,128)} %param.22) | copy-start | bytes 393220
  2.0 60.9 %copy-start.5 = (s32[1,1,32768]{2,1,0:T(1,128)S(1)}, s32[1,1,32768]{2,1,0:T(1,128)}, u32[]{:S(2)}) copy-start(s32[1,1,32768]{2,1,0:T(1,128)} %param.19) | copy-start | bytes 393220
  2.0 60.9 %copy-start.6 = (f32[32,128]{1,0:T(8,128)S(1)}, f32[32,128]{1,0:T(8,128)}, u32[]{:S(2)}) copy-start(f32[32,128]{1,0:T(8,128)} %constant.9.clone.lat_ref) | copy-start | bytes 49156
  62.8 1.4 %copy-start = (f32[48,64,128]{2,1,0:T(8,128)S(1)}, f32[48,64,128]{2,1,0:T(8,128)}, u32[]{:S(2)}) copy-start(f32[48,64,128]{2,1,0:T(8,128)} %get-tuple-element.11) | copy-start | bytes 4718596
  64.2 0.7 copy-start.9
  65.0 60.4 %copy-start.10 = (f32[48,64,128]{2,1,0:T(8,128)S(1)}, f32[48,64,128]{2,1,0:T(8,128)}, u32[]{:S(2)}) copy-start(f32[48,64,128]{2,1,0:T(8,128)} %get-tuple-element.20) | copy-start | bytes 4718596
  102.9 0.6 copy-start.7
  116.0 0.7 copy-start.8
  125.4 1.1 copy-start.12

commit v4 on v3

--- a/solution.py
+++ b/solution.py
@@ -412,7 +412,9 @@
     )(eps, charge, phi, motion)
 
 
-CHUNK = 4096
+CHUNK = 1024
+CHUNKS = LINKS // CHUNK
+RING = 2
 SLOTS = 9 * NC_DEV
 SLOTS_PAD = 384
 VELOCITY = np.array(
@@ -447,39 +449,39 @@
     return [jnp.take_along_axis(lat_ref[8 * i:8 * i + 8, :], direction, axis=1) for i in range(4)]
 
 
-def motions_at(table, slot_ref, base, onehot_ref, at_ref):
+def onehot_of(slot_ref, base, pair):
     ids = lax.broadcasted_iota(jnp.int32, (SLOTS, 128), 0)
-    for pair in range(4):
-        halves = [ids == slot_ref[pl.ds(base + 2 * pair + h, 1), :] for h in (0, 1)]
-        onehot = jnp.concatenate([half.astype(jnp.float32) for half in halves], axis=1).astype(jnp.bfloat16)
-        if onehot_ref is not None:
-            onehot_ref[:, 256 * pair:256 * pair + 256] = onehot
-        found = jnp.dot(table, onehot, preferred_element_type=jnp.float32)
-        found = found[0:8] + found[8:16]
-        at_ref[16 * pair:16 * pair + 8, :] = found[:, 0:128]
-        at_ref[16 * pair + 8:16 * pair + 16, :] = found[:, 128:256]
-    return [at_ref[pl.ds(i, 8, stride=8), :] for i in range(6)]
-
-
-def along_link(motion, velocity, offsets):
-    spin = cross(motion[3:6], offsets)
-    return sum(velocity[i] * (motion[i] + spin[i]) for i in range(3))
-
-
-def links_kernel(row_ref, site_ref, dir_ref, ids_ref, pop_ref, rb_ref, q_ref, table_ref, lat_ref, slot_ref, sums_ref, onehot_ref, at_ref, term_ref):
+    halves = [ids == slot_ref[pl.ds(base + 2 * pair + h, 1), :] for h in (0, 1)]
+    return jnp.concatenate([half.astype(jnp.float32) for half in halves], axis=1).astype(jnp.bfloat16)
+
+
+def found_at(table, onehot, pair, at_ref):
+    found = jnp.dot(table, onehot, preferred_element_type=jnp.float32)
+    found = found[0:8] + found[8:16]
+    at_ref[16 * pair:16 * pair + 8, :] = found[:, 0:128]
+    at_ref[16 * pair + 8:16 * pair + 16, :] = found[:, 128:256]
+
+
+def links_kernel(
+    row_ref, site_ref, dir_ref, ids_ref, pop_ref, rb_ref, q_ref, table_ref, lat_ref, slot_ref, gain_ref, sums_ref,
+    onehot_ref, at_ref, term_ref, index_refs, index_sem,
+):
     home_x = lax.axis_index("gx")
     home_y = lax.axis_index("gy")
     lane = lax.broadcasted_iota(jnp.int32, (8, 128), 1)
     sub = lax.broadcasted_iota(jnp.int32, (8, 128), 0)
 
-    @pl.when(pl.program_id(0) == 0)
-    def _():
-        sums_ref[...] = jnp.zeros_like(sums_ref)
-        term_ref[...] = jnp.zeros_like(term_ref)
-
+    def fetch(b, k):
+        rows = row_ref.at[pl.ds(pl.multiple_of(b * CHUNK, CHUNK), CHUNK)]
+        return pltpu.make_async_copy(rows, index_refs[k], index_sem.at[k])
+
+    for k in range(RING):
+        fetch(k, k).start()
+    sums_ref[...] = jnp.zeros_like(sums_ref)
+    term_ref[...] = jnp.zeros_like(term_ref)
     table = split(table_ref[...])[:, 0:SLOTS]
 
-    def group(b, _):
+    def group(b, k):
         base = pl.multiple_of(b * 8, 8)
         rows = pl.ds(base, 8)
         ids = ids_ref[rows, :]
@@ -489,21 +491,34 @@
         slot_ref[rows, :] = jnp.where(ids >= 0, (near_x * 3 + near_y) * NC_DEV + (ids & (NC_DEV - 1)), -1)
         column = site_ref[rows, :] & 127
         pressure = jnp.zeros((8, 128), jnp.float32)
+        fetch(b, k).wait()
         for j in range(128):
-            at = lambda s: jnp.broadcast_to(q_ref[pl.ds(row_ref[b * 1024 + s * 128 + j], 1), :], (8, 128))
+            at = lambda s: jnp.broadcast_to(q_ref[pl.ds(index_refs[k][s * 128 + j], 1), :], (8, 128))
             picked = at(0)
             for s in range(1, 8):
                 picked = jnp.where(sub == s, at(s), picked)
             pressure = jnp.where(lane == j, jnp.take_along_axis(picked, column, axis=1), pressure)
+
+        @pl.when(b + RING < CHUNKS)
+        def _():
+            fetch(b + RING, k).start()
+
         *velocity, weight = decode(lat_ref, dir_ref[rows, :])
         offsets = [rb_ref[i, rows, :] for i in range(3)]
-        motion = motions_at(table, slot_ref, base, onehot_ref, at_ref)
-        along = along_link(motion, velocity, offsets)
-        transfer = 2.0 * pop_ref[rows, :] - 6.0 * weight * along + weight * pressure
-        transfer = jnp.where(ids >= 0, transfer, 0.0)
-        force = [v * transfer for v in velocity]
-        for i, term in enumerate((*force, *cross(offsets, force))):
-            term_ref[pl.ds(i, 8, stride=8), :] = term
+        arms = (*velocity, *cross(offsets, velocity))
+        for pair in range(4):
+            onehot = onehot_of(slot_ref, base, pair)
+            onehot_ref[:, 256 * pair:256 * pair + 256] = onehot
+            found_at(table, onehot, pair, at_ref)
+        live = ids >= 0
+        scale = jnp.where(live, 6.0 * weight, 0.0)
+        source = jnp.where(live, 2.0 * pop_ref[rows, :] + weight * pressure, 0.0)
+        for i, arm in enumerate(arms):
+            gain = scale * arm
+            gain_ref[i, rows, :] = gain
+            source = source - gain * at_ref[pl.ds(i, 8, stride=8), :]
+        for i, arm in enumerate(arms):
+            term_ref[pl.ds(i, 8, stride=8), :] = arm * source
         total = jnp.zeros((16, SLOTS), jnp.float32)
         for pair in range(4):
             terms = jnp.concatenate([term_ref[16 * pair:16 * pair + 8, :], term_ref[16 * pair + 8:16 * pair + 16, :]], axis=1)
@@ -512,68 +527,41 @@
                 preferred_element_type=jnp.float32,
             )
         sums_ref[:, 0:SLOTS] += total[0:8] + total[8:16]
-        return 0
-
-    lax.fori_loop(0, CHUNK // 1024, group, 0)
-
-
-def link_spec(lead=None):
-    if lead is None:
-        return pl.BlockSpec((CHUNK // 128, 128), lambda i: (i, 0))
-    return pl.BlockSpec((lead, CHUNK // 128, 128), lambda i: (0, i, 0))
-
-
-def whole(*shape):
-    return pl.BlockSpec(shape, lambda i: (0,) * len(shape))
+
+    def ring(i, _):
+        for k in range(RING):
+            group(i * RING + k, k)
+        return 0
+
+    lax.fori_loop(0, CHUNKS // RING, ring, 0)
+
+
+VM = pl.BlockSpec(memory_space=pltpu.VMEM)
 
 
 def link_sums(row, site, direction, ids, pop, rb, q, table):
     return pl.pallas_call(
         links_kernel,
-        grid=(LINKS // CHUNK,),
-        in_specs=[
-            pl.BlockSpec((CHUNK,), lambda i: (i,), memory_space=pltpu.SMEM),
-            link_spec(), link_spec(), link_spec(), link_spec(), link_spec(3),
-            whole(NZ * TX, TY), whole(8, SLOTS_PAD), whole(32, 128),
+        in_specs=[pl.BlockSpec(memory_space=pl.ANY)] + [VM] * 8,
+        out_specs=(VM, VM, VM),
+        out_shape=(
+            jax.ShapeDtypeStruct((LINKS // 128, 128), jnp.int32),
+            jax.ShapeDtypeStruct((6, LINKS // 128, 128), jnp.float32),
+            jax.ShapeDtypeStruct((8, SLOTS_PAD), jnp.float32),
+        ),
+        scratch_shapes=[
+            pltpu.VMEM((SLOTS, CHUNK), jnp.bfloat16), pltpu.VMEM((64, 128), jnp.float32), pltpu.VMEM((64, 128), jnp.float32),
+            [pltpu.SMEM((CHUNK,), jnp.int32)] * RING, pltpu.SemaphoreType.DMA((RING,)),
         ],
-        out_specs=(link_spec(), whole(8, SLOTS_PAD)),
-        out_shape=(jax.ShapeDtypeStruct((LINKS // 128, 128), jnp.int32), jax.ShapeDtypeStruct((8, SLOTS_PAD), jnp.float32)),
-        scratch_shapes=[pltpu.VMEM((SLOTS, 1024), jnp.bfloat16), pltpu.VMEM((64, 128), jnp.float32), pltpu.VMEM((64, 128), jnp.float32)],
         name="link_sums",
         compiler_params=pltpu.CompilerParams(vmem_limit_bytes=40 * 2**20),
     )(row, site, direction, ids, pop, rb, q, table, lattice_table())
 
 
-def reflect_kernel(dir_ref, slot_ref, pop_ref, rb_ref, table_ref, lat_ref, out_ref, at_ref):
-    table = split(table_ref[...])[:, 0:SLOTS]
-
-    def group(b, _):
-        base = pl.multiple_of(b * 8, 8)
-        rows = pl.ds(base, 8)
-        *velocity, weight = decode(lat_ref, dir_ref[rows, :])
-        offsets = [rb_ref[i, rows, :] for i in range(3)]
-        motion = motions_at(table, slot_ref, base, None, at_ref)
-        along = jnp.where(slot_ref[rows, :] >= 0, along_link(motion, velocity, offsets), 0.0)
-        out_ref[rows, :] = pop_ref[rows, :] - 6.0 * weight * along
-        return 0
-
-    lax.fori_loop(0, CHUNK // 1024, group, 0)
-
-
-def reflect(direction, slot, pop, rb, table):
-    return pl.pallas_call(
-        reflect_kernel,
-        grid=(LINKS // CHUNK,),
-        in_specs=[link_spec(), link_spec(), link_spec(), link_spec(3), whole(8, SLOTS_PAD), whole(32, 128)],
-        out_specs=link_spec(),
-        out_shape=jax.ShapeDtypeStruct((LINKS // 128, 128), jnp.float32),
-        scratch_shapes=[pltpu.VMEM((64, 128), jnp.float32)],
-        name="reflect",
-        compiler_params=pltpu.CompilerParams(vmem_limit_bytes=40 * 2**20),
-    )(direction, slot, pop, rb, table, lattice_table())
-
-
-def update_kernel(sums_ref, motion_ref, report_ref, table_ref, part_ref, got_ref, new_ref, back_ref, send_sem, recv_sem):
+def update_kernel(
+    sums_ref, motion_ref, slot_ref, pop_ref, gain_ref, report_ref, out_ref,
+    part_ref, got_ref, new_ref, back_ref, table_ref, onehot_ref, at_ref, send_sem, recv_sem,
+):
     greeted = greet()
     mail = Mail(send_sem, recv_sem)
     lane = lax.broadcasted_iota(jnp.int32, (8, 128), 1)
@@ -586,6 +574,13 @@
     greeted()
     for t, _ in beside():
         mail.send(t, part_ref.at[t], got_ref.at[8 - t])
+
+    def prepare(b, _):
+        for pair in range(4):
+            onehot_ref[b, :, 256 * pair:256 * pair + 256] = onehot_of(slot_ref, pl.multiple_of(b * 8, 8), pair)
+        return 0
+
+    lax.fori_loop(0, CHUNKS // 2, prepare, 0)
     total = part_ref[4]
     mail.wait()
     for t in range(9):
@@ -597,27 +592,40 @@
     new_ref[...] = motion_ref[...] + jnp.where(row < 3, total / mass, total / inertia)
     for t, _ in beside():
         mail.send(t, new_ref, back_ref.at[8 - t])
+    lax.fori_loop(CHUNKS // 2, CHUNKS, prepare, 0)
     mail.wait()
     write_table(table_ref, lambda t: new_ref[...] if t == 4 else back_ref[t])
-
-
-VM = pl.BlockSpec(memory_space=pltpu.VMEM)
-
-
-def update(sums, motion):
+    table = split(table_ref[...])[:, 0:SLOTS]
+
+    def group(b, _):
+        rows = pl.ds(pl.multiple_of(b * 8, 8), 8)
+        for pair in range(4):
+            found_at(table, onehot_ref[b, :, 256 * pair:256 * pair + 256], pair, at_ref)
+        value = pop_ref[rows, :]
+        for i in range(6):
+            value = value - gain_ref[i, rows, :] * at_ref[pl.ds(i, 8, stride=8), :]
+        out_ref[rows, :] = value
+        return 0
+
+    lax.fori_loop(0, CHUNKS, group, 0)
+
+
+def update(sums, motion, slot, pop, gain):
     return pl.pallas_call(
         update_kernel,
-        out_shape=(jax.ShapeDtypeStruct((8, 128), jnp.float32), jax.ShapeDtypeStruct((8, SLOTS_PAD), jnp.float32)),
-        in_specs=[VM, VM],
+        out_shape=(jax.ShapeDtypeStruct((8, 128), jnp.float32), jax.ShapeDtypeStruct((LINKS // 128, 128), jnp.float32)),
+        in_specs=[VM] * 5,
         out_specs=(VM, VM),
         scratch_shapes=[
             pltpu.VMEM((9, 8, 128), jnp.float32), pltpu.VMEM((9, 8, 128), jnp.float32),
             pltpu.VMEM((8, 128), jnp.float32), pltpu.VMEM((9, 8, 128), jnp.float32),
+            pltpu.VMEM((8, SLOTS_PAD), jnp.float32), pltpu.VMEM((CHUNKS, SLOTS, CHUNK), jnp.bfloat16),
+            pltpu.VMEM((64, 128), jnp.float32),
             pltpu.SemaphoreType.DMA((16,)), pltpu.SemaphoreType.DMA((16,)),
         ],
         name="update",
-        compiler_params=pltpu.CompilerParams(collective_id=1, has_side_effects=True),
-    )(sums, motion)
+        compiler_params=pltpu.CompilerParams(vmem_limit_bytes=40 * 2**20, collective_id=1, has_side_effects=True),
+    )(sums, motion, slot, pop, gain)
 
 
 def shards(
@@ -629,11 +637,11 @@
     potential, q, table = relax(eps_field, charge, potential_start, motion)
     row = link_depth.reshape(-1) * TX + (link_site.reshape(-1) >> 7)
     rb = link_rb.reshape(3, LINKS // 128, 128)
-    slot, sums = link_sums(
+    slot, gain, sums = link_sums(
         row, flat(link_site), flat(link_dir), flat(link_colloid), flat(link_pop), rb, q.reshape(NZ * TX, TY), table
     )
-    report, table = update(sums, motion)
-    link_out = reflect(flat(link_dir), slot, flat(link_pop), rb, table).reshape(link_pop.shape)
+    report, link_out = update(sums, motion, slot, flat(link_pop), gain)
+    link_out = link_out.reshape(link_pop.shape)
     return potential, report[0:6, 0:NC_DEV], link_out
 
 

time: 128 us -> 120 us (0.938)
  Pallas kernels: 120 us -> 112 us
    pallas_call x2 -> x1, Pallas kernels: 46.6 us -> 32.8 us  [link_sums(): pl.pallas_call(links_kernel, in_specs=[pl.BlockSpec(memory_space=pl.ANY)]...]
    pallas_call x1, Pallas kernels: 12.4 us -> 18.4 us  [update(): pl.pallas_call(update_kernel, out_shape=(jax.ShapeDtypeStruct((8, 128), j...]
    unnamed x28 -> x25, local copies, waits for them, and re-layouts: 5.21 us -> 4.54 us
where the time goes in v4:
time: 120 us; the launch traced here: 119 us
  Pallas kernels  112 us (93%)
  local copies, waits for them, and re-layouts  4.54 us (4%)
  other arithmetic  1.51 us (1%)
    pallas_call x1, Pallas kernels, relax(): pl.pallas_call(relax_kernel, out_shape=(jax.ShapeDtypeStruct((NZ, TX, TY)...  60.6 us
    pallas_call x1, Pallas kernels, link_sums(): pl.pallas_call(links_kernel, in_specs=[pl.BlockSpec(memory_space=pl.ANY)]...  32.8 us
    pallas_call x1, Pallas kernels, update(): pl.pallas_call(update_kernel, out_shape=(jax.ShapeDtypeStruct((8, 128), j...  18.4 us
    unnamed x25, local copies, waits for them, and re-layouts  4.54 us

profile of v4, /device:TPU:0, one launch (start us, length us, event | category | flops | bytes accessed | tf_op | source)
XLA Modules:
  0.0 118.5 jit_solution(435976723534330724)
XLA Ops:
  0.6 1.3 %select_maximum_fusion.motion_ref = f32[8,128]{1,0:T(8,128)} fusion(f32[3,32]{1,0:T(4,128)} %param.16, f32[3,32]{1,0:T(4,128)} %param.15), kind=kLoop, calls=%fused_computation.1 | loop fusion | flops 8192 | bytes 4864 | tf_op jit(solution)/shard_map/concatenate | solution.py:636
  1.9 0.0 copy-start.4
  2.0 0.0 copy-start.5
  2.0 0.0 copy-start.7
  2.0 60.6 %relax.1 = (f32[48,64,128]{2,1,0:T(8,128)}, f32[48,64,128]{2,1,0:T(8,128)}, f32[8,384]{1,0:T(8,128)}) custom-call(bf16[48,64,128]{2,1,0:T(8,128)(2,1)} %eps_ref.1, f32[48,64,128]{2,1,0:T(8,128)} %charge_ref.1, f32[48,64,128]{2,1,0:T(8,128)} %phi_ref.1, f32[8,128]{1,0:T(8,128)} %select_maximum_fusion.motion_ref), custom_call_target="tpu_custom_call" | custom-call | tf_op jit(solution)/shard_map/relax/pallas_call | solution.py:381
  62.6 0.0 copy-start.6
  62.6 0.0 copy-done.1
  62.6 0.0 copy-done.10
  62.6 0.2 shift-right-arithmetic_add_fusion
  62.8 0.0 copy-done.2
  62.8 0.0 copy-done.3
  62.8 0.0 copy-done.4
  62.8 0.0 copy-done.5
  62.8 0.0 copy-done.7
  62.8 0.0 copy-start
  62.9 1.4 %copy-done = f32[48,64,128]{2,1,0:T(8,128)S(1)} copy-done((f32[48,64,128]{2,1,0:T(8,128)S(1)}, f32[48,64,128]{2,1,0:T(8,128)}, u32[]{:S(2)}) %copy-start) | copy-done | bytes 1572888
  64.3 0.7 copy-done.8
  65.0 32.8 %link_sums.1 = (s32[256,128]{1,0:T(8,128)S(1)}, f32[6,256,128]{2,1,0:T(8,128)S(1)}, f32[8,384]{1,0:T(8,128)S(1)}) custom-call(s32[32768]{0:T(1024)S(1)} %bitcast.11, s32[256,128]{1,0:T(8,128)S(1)} %bitcast.10, s32[256,128]{1,0:T(8,128)S(1)} %bitcast.16, s32[256,128]{1,0:T(8,128)S(1)} %bitcast.17, f32[256,128]{1,0:T(8,128)S(1)} %bitcast.12, ...), custom_call_target="tpu_custom_call" | custom-call | tf_op jit(solution)/shard_map/link_sums/pallas_call | solution.py:543
  97.7 0.0 copy-done.6
  97.7 18.4 %update.1 = (f32[8,128]{1,0:T(8,128)S(1)}, f32[256,128]{1,0:T(8,128)S(1)}) custom-call(f32[8,384]{1,0:T(8,128)S(1)} %get-tuple-element.14.sums_ref, f32[8,128]{1,0:T(8,128)S(1)} %copy-done.6, s32[256,128]{1,0:T(8,128)S(1)} %get-tuple-element.15.slot_ref, f32[256,128]{1,0:T(8,128)S(1)} %bitcast.13, f32[6,256,128]{2,1,0:T(8,128)S(1)} %get-tuple-element.16.gain_ref), custom_call_target="tpu_custom_call" | custom-call | tf_op jit(solution)/shard_map/update/pallas_call | solution.py:614
  116.1 0.0 copy-done.9
  116.1 1.1 copy.18
  117.3 0.6 copy.19
  117.9 0.7 copy.20
  (6 shorter events, 0.0 us)
Async XLA Ops:
  1.9 60.6 %copy-start.1 = (s32[1,1,32768]{2,1,0:T(1,128)S(1)}, s32[1,1,32768]{2,1,0:T(1,128)}, u32[]{:S(2)}) copy-start(s32[1,1,32768]{2,1,0:T(1,128)} %param.19) | copy-start | bytes 393220
  1.9 60.6 %copy-start.10 = (s32[1,1,32768]{2,1,0:T(1,128)S(1)}, s32[1,1,32768]{2,1,0:T(1,128)}, u32[]{:S(2)}) copy-start(s32[1,1,32768]{2,1,0:T(1,128)} %param.20) | copy-start | bytes 393220
  1.9 60.9 %copy-start.2 = (f32[1,1,32768]{2,1,0:T(1,128)S(1)}, f32[1,1,32768]{2,1,0:T(1,128)}, u32[]{:S(2)}) copy-start(f32[1,1,32768]{2,1,0:T(1,128)} %param.21) | copy-start | bytes 393220
  1.9 60.9 %copy-start.3 = (f32[3,1,1,32768]{3,2,1,0:T(1,128)S(1)}, f32[3,1,1,32768]{3,2,1,0:T(1,128)}, u32[]{:S(2)}) copy-start(f32[3,1,1,32768]{3,2,1,0:T(1,128)} %param.22) | copy-start | bytes 1179652
  1.9 60.9 %copy-start.4 = (s32[1,1,32768]{2,1,0:T(1,128)S(1)}, s32[1,1,32768]{2,1,0:T(1,128)}, u32[]{:S(2)}) copy-start(s32[1,1,32768]{2,1,0:T(1,128)} %param.17) | copy-start | bytes 393220
  2.0 60.9 %copy-start.5 = (s32[1,1,32768]{2,1,0:T(1,128)S(1)}, s32[1,1,32768]{2,1,0:T(1,128)}, u32[]{:S(2)}) copy-start(s32[1,1,32768]{2,1,0:T(1,128)} %param.18) | copy-start | bytes 393220
  2.0 60.9 %copy-start.7 = (f32[32,128]{1,0:T(8,128)S(1)}, f32[32,128]{1,0:T(8,128)}, u32[]{:S(2)}) copy-start(f32[32,128]{1,0:T(8,128)} %constant.9.clone.lat_ref) | copy-start | bytes 49156
  62.6 35.2 %copy-start.6 = (f32[8,128]{1,0:T(8,128)S(1)}, f32[8,128]{1,0:T(8,128)}, u32[]{:S(2)}) copy-start(f32[8,128]{1,0:T(8,128)} %select_maximum_fusion.motion_ref) | copy-start | bytes 12292
  62.8 1.4 %copy-start = (f32[48,64,128]{2,1,0:T(8,128)S(1)}, f32[48,64,128]{2,1,0:T(8,128)}, u32[]{:S(2)}) copy-start(f32[48,64,128]{2,1,0:T(8,128)} %get-tuple-element.12) | copy-start | bytes 4718596
  64.3 0.7 copy-start.8
  65.0 51.2 %copy-start.9 = (f32[48,64,128]{2,1,0:T(8,128)S(1)}, f32[48,64,128]{2,1,0:T(8,128)}, u32[]{:S(2)}) copy-start(f32[48,64,128]{2,1,0:T(8,128)} %get-tuple-element.22) | copy-start | bytes 4718596

commit v5 on v4

--- a/solution.py
+++ b/solution.py
@@ -328,15 +328,19 @@
         return 0
     lax.fori_loop(0, 3, three, 0)
     step(0, False)
+
+    def send_rows2(c):
+        mail.send(1, p_refs[c].at[pl.ds(1, HALF), pl.ds(TOP, 8), :], x2_refs[c].at[1])
+        mail.send(7, p_refs[c].at[pl.ds(1, HALF), pl.ds(TOP + TX - 8, 8), :], x2_refs[c].at[0])
+
+    send_rows2(0)
     step(1, True)
 
     def coloured(g, k, r):
         value = p_refs[k % 2][8 * g + k // 2 + 1, TOP + r:TOP + r + 16, :]
         return value[0:8], value[8:16]
 
-    for c in (0, 1):
-        mail.send(1, p_refs[c].at[pl.ds(1, HALF), pl.ds(TOP, 8), :], x2_refs[c].at[1])
-        mail.send(7, p_refs[c].at[pl.ds(1, HALF), pl.ds(TOP + TX - 8, 8), :], x2_refs[c].at[0])
+    send_rows2(1)
     pack(coloured, to2_low, to2_high, 0)
     send_sides(to2_low, to2_high, from2_low, from2_high, 0)
     mail.wait()
@@ -414,7 +418,6 @@
 
 CHUNK = 1024
 CHUNKS = LINKS // CHUNK
-RING = 2
 SLOTS = 9 * NC_DEV
 SLOTS_PAD = 384
 VELOCITY = np.array(
@@ -449,9 +452,9 @@
     return [jnp.take_along_axis(lat_ref[8 * i:8 * i + 8, :], direction, axis=1) for i in range(4)]
 
 
-def onehot_of(slot_ref, base, pair):
+def onehot_of(slot_ref, pair):
     ids = lax.broadcasted_iota(jnp.int32, (SLOTS, 128), 0)
-    halves = [ids == slot_ref[pl.ds(base + 2 * pair + h, 1), :] for h in (0, 1)]
+    halves = [ids == slot_ref[2 * pair + h:2 * pair + h + 1, :] for h in (0, 1)]
     return jnp.concatenate([half.astype(jnp.float32) for half in halves], axis=1).astype(jnp.bfloat16)
 
 
@@ -463,9 +466,12 @@
 
 
 def links_kernel(
-    row_ref, site_ref, dir_ref, ids_ref, pop_ref, rb_ref, q_ref, table_ref, lat_ref, slot_ref, gain_ref, sums_ref,
-    onehot_ref, at_ref, term_ref, index_refs, index_sem,
+    row_ref, site_ref, dir_ref, ids_ref, pop_ref, rb_ref, q_ref, table_ref, lat_ref, motion_ref, report_ref, out_ref,
+    slot_ref, gain_ref, sums_ref, onehot_ref, at_ref, term_ref, press_refs, index_refs,
+    part_ref, got_ref, new_ref, back_ref, moved_ref, index_sem, send_sem, recv_sem,
 ):
+    greeted = greet()
+    mail = Mail(send_sem, recv_sem)
     home_x = lax.axis_index("gx")
     home_y = lax.axis_index("gy")
     lane = lax.broadcasted_iota(jnp.int32, (8, 128), 1)
@@ -475,44 +481,38 @@
         rows = row_ref.at[pl.ds(pl.multiple_of(b * CHUNK, CHUNK), CHUNK)]
         return pltpu.make_async_copy(rows, index_refs[k], index_sem.at[k])
 
-    for k in range(RING):
-        fetch(k, k).start()
-    sums_ref[...] = jnp.zeros_like(sums_ref)
-    term_ref[...] = jnp.zeros_like(term_ref)
-    table = split(table_ref[...])[:, 0:SLOTS]
-
-    def group(b, k):
-        base = pl.multiple_of(b * 8, 8)
-        rows = pl.ds(base, 8)
-        ids = ids_ref[rows, :]
-        owner = ids >> 5
-        near_x = ((owner >> 4) - home_x + 1) & (TILES_X - 1)
-        near_y = ((owner & (TILES_Y - 1)) - home_y + 1) & (TILES_Y - 1)
-        slot_ref[rows, :] = jnp.where(ids >= 0, (near_x * 3 + near_y) * NC_DEV + (ids & (NC_DEV - 1)), -1)
-        column = site_ref[rows, :] & 127
+    def gather(b, k):
+        column = site_ref[pl.ds(pl.multiple_of(b * 8, 8), 8), :] & 127
         pressure = jnp.zeros((8, 128), jnp.float32)
-        fetch(b, k).wait()
         for j in range(128):
             at = lambda s: jnp.broadcast_to(q_ref[pl.ds(index_refs[k][s * 128 + j], 1), :], (8, 128))
             picked = at(0)
             for s in range(1, 8):
                 picked = jnp.where(sub == s, at(s), picked)
             pressure = jnp.where(lane == j, jnp.take_along_axis(picked, column, axis=1), pressure)
-
-        @pl.when(b + RING < CHUNKS)
-        def _():
-            fetch(b + RING, k).start()
-
+        press_refs[k][...] = pressure
+
+    sums_ref[...] = jnp.zeros_like(sums_ref)
+    term_ref[...] = jnp.zeros_like(term_ref)
+    table = split(table_ref[...])[:, 0:SLOTS]
+
+    def add(b, k):
+        rows = pl.ds(pl.multiple_of(b * 8, 8), 8)
+        ids = ids_ref[rows, :]
+        owner = ids >> 5
+        near_x = ((owner >> 4) - home_x + 1) & (TILES_X - 1)
+        near_y = ((owner & (TILES_Y - 1)) - home_y + 1) & (TILES_Y - 1)
+        slot_ref[...] = jnp.where(ids >= 0, (near_x * 3 + near_y) * NC_DEV + (ids & (NC_DEV - 1)), -1)
         *velocity, weight = decode(lat_ref, dir_ref[rows, :])
         offsets = [rb_ref[i, rows, :] for i in range(3)]
         arms = (*velocity, *cross(offsets, velocity))
+        onehots = [onehot_of(slot_ref, pair) for pair in range(4)]
         for pair in range(4):
-            onehot = onehot_of(slot_ref, base, pair)
-            onehot_ref[:, 256 * pair:256 * pair + 256] = onehot
-            found_at(table, onehot, pair, at_ref)
+            onehot_ref[b, :, 256 * pair:256 * pair + 256] = onehots[pair]
+            found_at(table, onehots[pair], pair, at_ref)
         live = ids >= 0
         scale = jnp.where(live, 6.0 * weight, 0.0)
-        source = jnp.where(live, 2.0 * pop_ref[rows, :] + weight * pressure, 0.0)
+        source = jnp.where(live, 2.0 * pop_ref[rows, :] + weight * press_refs[k][...], 0.0)
         for i, arm in enumerate(arms):
             gain = scale * arm
             gain_ref[i, rows, :] = gain
@@ -523,48 +523,34 @@
         for pair in range(4):
             terms = jnp.concatenate([term_ref[16 * pair:16 * pair + 8, :], term_ref[16 * pair + 8:16 * pair + 16, :]], axis=1)
             total = total + lax.dot_general(
-                split(terms), onehot_ref[:, 256 * pair:256 * pair + 256], (((1,), (1,)), ((), ())),
+                split(terms), onehot_ref[b, :, 256 * pair:256 * pair + 256], (((1,), (1,)), ((), ())),
                 preferred_element_type=jnp.float32,
             )
         sums_ref[:, 0:SLOTS] += total[0:8] + total[8:16]
 
+    fetch(0, 0).start()
+    fetch(1, 1).start()
+    fetch(0, 0).wait()
+    gather(0, 0)
+
     def ring(i, _):
-        for k in range(RING):
-            group(i * RING + k, k)
-        return 0
-
-    lax.fori_loop(0, CHUNKS // RING, ring, 0)
-
-
-VM = pl.BlockSpec(memory_space=pltpu.VMEM)
-
-
-def link_sums(row, site, direction, ids, pop, rb, q, table):
-    return pl.pallas_call(
-        links_kernel,
-        in_specs=[pl.BlockSpec(memory_space=pl.ANY)] + [VM] * 8,
-        out_specs=(VM, VM, VM),
-        out_shape=(
-            jax.ShapeDtypeStruct((LINKS // 128, 128), jnp.int32),
-            jax.ShapeDtypeStruct((6, LINKS // 128, 128), jnp.float32),
-            jax.ShapeDtypeStruct((8, SLOTS_PAD), jnp.float32),
-        ),
-        scratch_shapes=[
-            pltpu.VMEM((SLOTS, CHUNK), jnp.bfloat16), pltpu.VMEM((64, 128), jnp.float32), pltpu.VMEM((64, 128), jnp.float32),
-            [pltpu.SMEM((CHUNK,), jnp.int32)] * RING, pltpu.SemaphoreType.DMA((RING,)),
-        ],
-        name="link_sums",
-        compiler_params=pltpu.CompilerParams(vmem_limit_bytes=40 * 2**20),
-    )(row, site, direction, ids, pop, rb, q, table, lattice_table())
-
-
-def update_kernel(
-    sums_ref, motion_ref, slot_ref, pop_ref, gain_ref, report_ref, out_ref,
-    part_ref, got_ref, new_ref, back_ref, table_ref, onehot_ref, at_ref, send_sem, recv_sem,
-):
-    greeted = greet()
-    mail = Mail(send_sem, recv_sem)
-    lane = lax.broadcasted_iota(jnp.int32, (8, 128), 1)
+        @pl.when(i < CHUNKS // 2 - 1)
+        def _():
+            fetch(2 * i + 2, 0).start()
+        fetch(2 * i + 1, 1).wait()
+        gather(2 * i + 1, 1)
+        add(2 * i, 0)
+
+        @pl.when(i < CHUNKS // 2 - 1)
+        def _():
+            fetch(2 * i + 3, 1).start()
+            fetch(2 * i + 2, 0).wait()
+        gather(lax.rem(2 * i + 2, CHUNKS), 0)
+        add(2 * i + 1, 1)
+        return 0
+
+    lax.fori_loop(0, CHUNKS // 2, ring, 0)
+
     row = lax.broadcasted_iota(jnp.int32, (8, 128), 0)
     for t in range(9):
         value = sums_ref[:, 128 * (t // 4):128 * (t // 4) + 128]
@@ -574,13 +560,6 @@
     greeted()
     for t, _ in beside():
         mail.send(t, part_ref.at[t], got_ref.at[8 - t])
-
-    def prepare(b, _):
-        for pair in range(4):
-            onehot_ref[b, :, 256 * pair:256 * pair + 256] = onehot_of(slot_ref, pl.multiple_of(b * 8, 8), pair)
-        return 0
-
-    lax.fori_loop(0, CHUNKS // 2, prepare, 0)
     total = part_ref[4]
     mail.wait()
     for t in range(9):
@@ -588,19 +567,18 @@
             total = total + got_ref[t]
     mass = 4.0 / 3.0 * math.pi * RADIUS**3
     inertia = 0.4 * mass * RADIUS**2
-    report_ref[...] = jnp.where(row < 3, total, total / RADIUS)
     new_ref[...] = motion_ref[...] + jnp.where(row < 3, total / mass, total / inertia)
     for t, _ in beside():
         mail.send(t, new_ref, back_ref.at[8 - t])
-    lax.fori_loop(CHUNKS // 2, CHUNKS, prepare, 0)
+    report_ref[...] = jnp.where(row < 3, total, total / RADIUS)
     mail.wait()
-    write_table(table_ref, lambda t: new_ref[...] if t == 4 else back_ref[t])
-    table = split(table_ref[...])[:, 0:SLOTS]
+    write_table(moved_ref, lambda t: new_ref[...] if t == 4 else back_ref[t])
+    moved = split(moved_ref[...])[:, 0:SLOTS]
 
     def group(b, _):
         rows = pl.ds(pl.multiple_of(b * 8, 8), 8)
         for pair in range(4):
-            found_at(table, onehot_ref[b, :, 256 * pair:256 * pair + 256], pair, at_ref)
+            found_at(moved, onehot_ref[b, :, 256 * pair:256 * pair + 256], pair, at_ref)
         value = pop_ref[rows, :]
         for i in range(6):
             value = value - gain_ref[i, rows, :] * at_ref[pl.ds(i, 8, stride=8), :]
@@ -610,22 +588,28 @@
     lax.fori_loop(0, CHUNKS, group, 0)
 
 
-def update(sums, motion, slot, pop, gain):
+VM = pl.BlockSpec(memory_space=pltpu.VMEM)
+
+
+def links(row, site, direction, ids, pop, rb, q, table, motion):
+    small = pltpu.VMEM((9, 8, 128), jnp.float32)
+    wide = pltpu.VMEM((8, SLOTS_PAD), jnp.float32)
+    column = pltpu.VMEM((64, 128), jnp.float32)
     return pl.pallas_call(
-        update_kernel,
+        links_kernel,
+        in_specs=[pl.BlockSpec(memory_space=pl.ANY)] + [VM] * 9,
+        out_specs=(VM, VM),
         out_shape=(jax.ShapeDtypeStruct((8, 128), jnp.float32), jax.ShapeDtypeStruct((LINKS // 128, 128), jnp.float32)),
-        in_specs=[VM] * 5,
-        out_specs=(VM, VM),
         scratch_shapes=[
-            pltpu.VMEM((9, 8, 128), jnp.float32), pltpu.VMEM((9, 8, 128), jnp.float32),
-            pltpu.VMEM((8, 128), jnp.float32), pltpu.VMEM((9, 8, 128), jnp.float32),
-            pltpu.VMEM((8, SLOTS_PAD), jnp.float32), pltpu.VMEM((CHUNKS, SLOTS, CHUNK), jnp.bfloat16),
-            pltpu.VMEM((64, 128), jnp.float32),
-            pltpu.SemaphoreType.DMA((16,)), pltpu.SemaphoreType.DMA((16,)),
+            pltpu.VMEM((8, 128), jnp.int32), pltpu.VMEM((6, LINKS // 128, 128), jnp.float32), wide,
+            pltpu.VMEM((CHUNKS, SLOTS, CHUNK), jnp.bfloat16), column, column,
+            [pltpu.VMEM((8, 128), jnp.float32)] * 2, [pltpu.SMEM((CHUNK,), jnp.int32)] * 2,
+            small, small, pltpu.VMEM((8, 128), jnp.float32), small, wide,
+            pltpu.SemaphoreType.DMA((2,)), pltpu.SemaphoreType.DMA((16,)), pltpu.SemaphoreType.DMA((16,)),
         ],
-        name="update",
+        name="links",
         compiler_params=pltpu.CompilerParams(vmem_limit_bytes=40 * 2**20, collective_id=1, has_side_effects=True),
-    )(sums, motion, slot, pop, gain)
+    )(row, site, direction, ids, pop, rb, q, table, lattice_table(), motion)
 
 
 def shards(
@@ -637,10 +621,9 @@
     potential, q, table = relax(eps_field, charge, potential_start, motion)
     row = link_depth.reshape(-1) * TX + (link_site.reshape(-1) >> 7)
     rb = link_rb.reshape(3, LINKS // 128, 128)
-    slot, gain, sums = link_sums(
-        row, flat(link_site), flat(link_dir), flat(link_colloid), flat(link_pop), rb, q.reshape(NZ * TX, TY), table
+    report, link_out = links(
+        row, flat(link_site), flat(link_dir), flat(link_colloid), flat(link_pop), rb, q.reshape(NZ * TX, TY), table, motion
     )
-    report, link_out = update(sums, motion, slot, flat(link_pop), gain)
     link_out = link_out.reshape(link_pop.shape)
     return potential, report[0:6, 0:NC_DEV], link_out
 

time: 120 us -> 120 us (level); the launches traced: 119 us -> 120 us
    pallas_call x2 -> x1, Pallas kernels: 51.1 us -> 52.7 us  [links(): pl.pallas_call(links_kernel, in_specs=[pl.BlockSpec(memory_space=pl.ANY)]...]
where the time goes in v5:
time: 120 us
  Pallas kernels  113 us (94%)
  local copies, waits for them, and re-layouts  4.54 us (4%)
  other arithmetic  1.51 us (1%)
    pallas_call x1, Pallas kernels, relax(): pl.pallas_call(relax_kernel, out_shape=(jax.ShapeDtypeStruct((NZ, TX, TY)...  60.5 us
    pallas_call x1, Pallas kernels, links(): pl.pallas_call(links_kernel, in_specs=[pl.BlockSpec(memory_space=pl.ANY)]...  52.7 us
    unnamed x25, local copies, waits for them, and re-layouts  4.54 us

profile of v5, /device:TPU:0, one launch (start us, length us, event | category | flops | bytes accessed | tf_op | source)
XLA Modules:
  0.0 120.1 jit_solution(15262305365356734532)
XLA Ops:
  0.6 1.3 %select_maximum_fusion.motion_ref = f32[8,128]{1,0:T(8,128)} fusion(f32[3,32]{1,0:T(4,128)} %param.16, f32[3,32]{1,0:T(4,128)} %param.15), kind=kLoop, calls=%fused_computation.1 | loop fusion | flops 8192 | bytes 4864 | tf_op jit(solution)/shard_map/concatenate | solution.py:620
  1.9 0.0 copy-start.1
  1.9 0.0 copy-start.4
  2.0 0.0 copy-start.5
  2.0 0.0 copy-start.6
  2.0 0.0 copy-start.7
  2.0 60.5 %relax.1 = (f32[48,64,128]{2,1,0:T(8,128)}, f32[48,64,128]{2,1,0:T(8,128)}, f32[8,384]{1,0:T(8,128)}) custom-call(bf16[48,64,128]{2,1,0:T(8,128)(2,1)} %eps_ref.1, f32[48,64,128]{2,1,0:T(8,128)} %charge_ref.1, f32[48,64,128]{2,1,0:T(8,128)} %phi_ref.1, f32[8,128]{1,0:T(8,128)} %select_maximum_fusion.motion_ref), custom_call_target="tpu_custom_call" | custom-call | tf_op jit(solution)/shard_map/relax/pallas_call | solution.py:385
  62.5 0.0 copy-done.1
  62.5 0.0 copy-done.10
  62.5 0.2 shift-right-arithmetic_add_fusion
  62.8 0.0 copy-done.2
  62.8 0.0 copy-done.3
  62.8 0.0 copy-done.4
  62.8 0.0 copy-done.5
  62.8 0.0 copy-done.6
  62.8 0.0 copy-done.7
  62.8 0.0 copy-start
  62.8 1.4 %copy-done = f32[48,64,128]{2,1,0:T(8,128)S(1)} copy-done((f32[48,64,128]{2,1,0:T(8,128)S(1)}, f32[48,64,128]{2,1,0:T(8,128)}, u32[]{:S(2)}) %copy-start) | copy-done | bytes 1572888
  64.2 0.7 copy-done.8
  64.9 52.7 %links.1 = (f32[8,128]{1,0:T(8,128)S(1)}, f32[256,128]{1,0:T(8,128)S(1)}) custom-call(s32[32768]{0:T(1024)S(1)} %bitcast.11, s32[256,128]{1,0:T(8,128)S(1)} %bitcast.10, s32[256,128]{1,0:T(8,128)S(1)} %bitcast.14, s32[256,128]{1,0:T(8,128)S(1)} %bitcast.15, f32[256,128]{1,0:T(8,128)S(1)} %bitcast.16, f32[3,256,128]{2,1,0:T(8,128)S(1)} %bitcast.12, ...), custom_call_target="tpu_custom_call" | custom-call | tf_op jit(solution)/shard_map/links/pallas_call | solution.py:598
  117.7 0.0 copy-done.9
  117.7 1.1 copy.18
  118.8 0.6 copy.19
  119.4 0.7 copy.20
  (5 shorter events, 0.0 us)
Async XLA Ops:
  1.9 60.6 %copy-start.1 = (s32[1,1,32768]{2,1,0:T(1,128)S(1)}, s32[1,1,32768]{2,1,0:T(1,128)}, u32[]{:S(2)}) copy-start(s32[1,1,32768]{2,1,0:T(1,128)} %param.19) | copy-start | bytes 393220
  1.9 60.6 %copy-start.10 = (s32[1,1,32768]{2,1,0:T(1,128)S(1)}, s32[1,1,32768]{2,1,0:T(1,128)}, u32[]{:S(2)}) copy-start(s32[1,1,32768]{2,1,0:T(1,128)} %param.20) | copy-start | bytes 393220
  1.9 60.8 %copy-start.2 = (f32[3,1,1,32768]{3,2,1,0:T(1,128)S(1)}, f32[3,1,1,32768]{3,2,1,0:T(1,128)}, u32[]{:S(2)}) copy-start(f32[3,1,1,32768]{3,2,1,0:T(1,128)} %param.22) | copy-start | bytes 1179652
  1.9 60.8 %copy-start.3 = (s32[1,1,32768]{2,1,0:T(1,128)S(1)}, s32[1,1,32768]{2,1,0:T(1,128)}, u32[]{:S(2)}) copy-start(s32[1,1,32768]{2,1,0:T(1,128)} %param.17) | copy-start | bytes 393220
  1.9 60.8 %copy-start.4 = (s32[1,1,32768]{2,1,0:T(1,128)S(1)}, s32[1,1,32768]{2,1,0:T(1,128)}, u32[]{:S(2)}) copy-start(s32[1,1,32768]{2,1,0:T(1,128)} %param.18) | copy-start | bytes 393220
  2.0 60.8 %copy-start.5 = (f32[1,1,32768]{2,1,0:T(1,128)S(1)}, f32[1,1,32768]{2,1,0:T(1,128)}, u32[]{:S(2)}) copy-start(f32[1,1,32768]{2,1,0:T(1,128)} %param.21) | copy-start | bytes 393220
  2.0 60.8 %copy-start.6 = (f32[8,128]{1,0:T(8,128)S(1)}, f32[8,128]{1,0:T(8,128)}, u32[]{:S(2)}) copy-start(f32[8,128]{1,0:T(8,128)} %select_maximum_fusion.motion_ref) | copy-start | bytes 12292
  2.0 60.8 %copy-start.7 = (f32[32,128]{1,0:T(8,128)S(1)}, f32[32,128]{1,0:T(8,128)}, u32[]{:S(2)}) copy-start(f32[32,128]{1,0:T(8,128)} %constant.9.clone.lat_ref) | copy-start | bytes 49156
  62.8 1.4 %copy-start = (f32[48,64,128]{2,1,0:T(8,128)S(1)}, f32[48,64,128]{2,1,0:T(8,128)}, u32[]{:S(2)}) copy-start(f32[48,64,128]{2,1,0:T(8,128)} %get-tuple-element.9) | copy-start | bytes 4718596
  64.2 0.7 copy-start.8
  64.9 52.7 %copy-start.9 = (f32[48,64,128]{2,1,0:T(8,128)S(1)}, f32[48,64,128]{2,1,0:T(8,128)}, u32[]{:S(2)}) copy-start(f32[48,64,128]{2,1,0:T(8,128)} %get-tuple-element.16) | copy-start | bytes 4718596

commit v6 on v5

--- a/solution.py
+++ b/solution.py
@@ -56,14 +56,9 @@
         self.copies = []
 
 
-def write_table(table_ref, block):
-    for tile in range(3):
-        total = jnp.zeros((8, 128), jnp.float32)
-        for i in range(4):
-            if 4 * tile + i < 9:
-                value = block(4 * tile + i)
-                total = total + (pltpu.roll(value, NC_DEV * i, 1) if i else value)
-        table_ref[:, 128 * tile:128 * tile + 128] = total
+def write_blocks(blocks_ref, block):
+    for t in range(9):
+        blocks_ref[8 * t:8 * t + 8, :] = block(t)
 
 
 def relax_kernel(
@@ -307,7 +302,7 @@
         lax.fori_loop(0, GROUPS, strip_step, 0)
 
     mail.wait()
-    write_table(table_ref, lambda t: motion_ref[...] if t == 4 else got_ref[t])
+    write_blocks(table_ref, lambda t: motion_ref[...] if t == 4 else got_ref[t])
 
     def edges1(m, _):
         for side, g in ((0, 8), (1, TOP + TX)):
@@ -387,7 +382,7 @@
         out_shape=(
             jax.ShapeDtypeStruct((NZ, TX, TY), jnp.float32),
             jax.ShapeDtypeStruct((NZ, TX, TY), jnp.float32),
-            jax.ShapeDtypeStruct((8, SLOTS_PAD), jnp.float32),
+            jax.ShapeDtypeStruct((72, 128), jnp.float32),
         ),
         in_specs=[spec] * 4,
         out_specs=(spec,) * 3,
@@ -418,8 +413,8 @@
 
 CHUNK = 1024
 CHUNKS = LINKS // CHUNK
-SLOTS = 9 * NC_DEV
-SLOTS_PAD = 384
+RING = 4
+FINAL = 8
 VELOCITY = np.array(
     [[1, 0, 0], [-1, 0, 0], [0, 1, 0], [0, -1, 0], [0, 0, 1], [0, 0, -1], [1, 1, 0], [1, -1, 0], [-1, 1, 0],
      [-1, -1, 0], [1, 0, 1], [1, 0, -1], [-1, 0, 1], [-1, 0, -1], [0, 1, 1], [0, 1, -1], [0, -1, 1], [0, -1, -1]],
@@ -435,11 +430,6 @@
     return jnp.asarray(rows.reshape(32, 128))
 
 
-def split(values):
-    high = values.astype(jnp.bfloat16).astype(jnp.float32)
-    return jnp.concatenate([high, values - high], axis=0).astype(jnp.bfloat16)
-
-
 def cross(first, second):
     return (
         first[1] * second[2] - first[2] * second[1],
@@ -452,23 +442,38 @@
     return [jnp.take_along_axis(lat_ref[8 * i:8 * i + 8, :], direction, axis=1) for i in range(4)]
 
 
-def onehot_of(slot_ref, pair):
-    ids = lax.broadcasted_iota(jnp.int32, (SLOTS, 128), 0)
-    halves = [ids == slot_ref[2 * pair + h:2 * pair + h + 1, :] for h in (0, 1)]
-    return jnp.concatenate([half.astype(jnp.float32) for half in halves], axis=1).astype(jnp.bfloat16)
-
-
-def found_at(table, onehot, pair, at_ref):
-    found = jnp.dot(table, onehot, preferred_element_type=jnp.float32)
-    found = found[0:8] + found[8:16]
-    at_ref[16 * pair:16 * pair + 8, :] = found[:, 0:128]
-    at_ref[16 * pair + 8:16 * pair + 16, :] = found[:, 128:256]
+def pair_of(slot_ref, base, pair):
+    slots = jnp.concatenate([slot_ref[pl.ds(base + 2 * pair + h, 1), :] for h in (0, 1)], axis=1)
+    colloid = lax.broadcasted_iota(jnp.int32, (NC_DEV, 256), 0) == (slots & (NC_DEV - 1))
+    return slots >> 5, colloid.astype(jnp.float32)
+
+
+def block_table(block):
+    rows = []
+    for t in range(9):
+        value = block(t)
+        high = value.astype(jnp.bfloat16).astype(jnp.float32)
+        rows.append(high + pltpu.roll(value - high, NC_DEV, 1))
+    rows.append(jnp.zeros((8, 128), jnp.float32))
+    return jnp.concatenate(rows, axis=0).astype(jnp.bfloat16)[:, 0:2 * NC_DEV]
+
+
+def found_at(table, slot_ref, base, at_ref):
+    for pair in range(4):
+        near, colloid = pair_of(slot_ref, base, pair)
+        onehot = jnp.concatenate([colloid, colloid], axis=0).astype(jnp.bfloat16)
+        every = jnp.dot(table, onehot, preferred_element_type=jnp.float32)
+        found = jnp.zeros((8, 256), jnp.float32)
+        for t in range(9):
+            found = jnp.where(near == t, every[8 * t:8 * t + 8], found)
+        at_ref[16 * pair:16 * pair + 8, :] = found[:, 0:128]
+        at_ref[16 * pair + 8:16 * pair + 16, :] = found[:, 128:256]
 
 
 def links_kernel(
     row_ref, site_ref, dir_ref, ids_ref, pop_ref, rb_ref, q_ref, table_ref, lat_ref, motion_ref, report_ref, out_ref,
-    slot_ref, gain_ref, sums_ref, onehot_ref, at_ref, term_ref, press_refs, index_refs,
-    part_ref, got_ref, new_ref, back_ref, moved_ref, index_sem, send_sem, recv_sem,
+    slot_ref, slots_refs, gain_ref, sums_ref, at_refs, term_refs, press_refs, index_refs,
+    part_ref, got_ref, new_ref, back_ref, index_sem, send_sem, recv_sem,
 ):
     greeted = greet()
     mail = Mail(send_sem, recv_sem)
@@ -493,70 +498,79 @@
         press_refs[k][...] = pressure
 
     sums_ref[...] = jnp.zeros_like(sums_ref)
-    term_ref[...] = jnp.zeros_like(term_ref)
-    table = split(table_ref[...])[:, 0:SLOTS]
-
-    def add(b, k):
+    for term_ref in term_refs:
+        term_ref[...] = jnp.zeros_like(term_ref)
+    table = block_table(lambda t: table_ref[8 * t:8 * t + 8, :])
+
+    def place(b, k):
         rows = pl.ds(pl.multiple_of(b * 8, 8), 8)
         ids = ids_ref[rows, :]
         owner = ids >> 5
         near_x = ((owner >> 4) - home_x + 1) & (TILES_X - 1)
         near_y = ((owner & (TILES_Y - 1)) - home_y + 1) & (TILES_Y - 1)
-        slot_ref[...] = jnp.where(ids >= 0, (near_x * 3 + near_y) * NC_DEV + (ids & (NC_DEV - 1)), -1)
+        slots = jnp.where(ids >= 0, (near_x * 3 + near_y) * NC_DEV + (ids & (NC_DEV - 1)), -1)
+        slot_ref[rows, :] = slots
+        slots_refs[k][...] = slots
+
+    def terms_of(b, k):
+        rows = pl.ds(pl.multiple_of(b * 8, 8), 8)
         *velocity, weight = decode(lat_ref, dir_ref[rows, :])
         offsets = [rb_ref[i, rows, :] for i in range(3)]
         arms = (*velocity, *cross(offsets, velocity))
-        onehots = [onehot_of(slot_ref, pair) for pair in range(4)]
-        for pair in range(4):
-            onehot_ref[b, :, 256 * pair:256 * pair + 256] = onehots[pair]
-            found_at(table, onehots[pair], pair, at_ref)
-        live = ids >= 0
+        live = slots_refs[k][...] >= 0
         scale = jnp.where(live, 6.0 * weight, 0.0)
         source = jnp.where(live, 2.0 * pop_ref[rows, :] + weight * press_refs[k][...], 0.0)
         for i, arm in enumerate(arms):
             gain = scale * arm
             gain_ref[i, rows, :] = gain
-            source = source - gain * at_ref[pl.ds(i, 8, stride=8), :]
+            source = source - gain * at_refs[k][pl.ds(i, 8, stride=8), :]
         for i, arm in enumerate(arms):
-            term_ref[pl.ds(i, 8, stride=8), :] = arm * source
-        total = jnp.zeros((16, SLOTS), jnp.float32)
+            term_refs[k][pl.ds(i, 8, stride=8), :] = arm * source
+
+    def summed(k, total):
         for pair in range(4):
-            terms = jnp.concatenate([term_ref[16 * pair:16 * pair + 8, :], term_ref[16 * pair + 8:16 * pair + 16, :]], axis=1)
+            near, colloid = pair_of(slots_refs[k], 0, pair)
+            terms = [term_refs[k][16 * pair + 8 * h:16 * pair + 8 * h + 8, :] for h in (0, 1)]
+            terms = jnp.concatenate(terms, axis=1)
+            high = terms.astype(jnp.bfloat16).astype(jnp.float32)
+            both = jnp.concatenate([high, terms - high], axis=0)
+            spread = jnp.concatenate([jnp.where(near == t, both, 0.0) for t in range(9)], axis=0).astype(jnp.bfloat16)
             total = total + lax.dot_general(
-                split(terms), onehot_ref[b, :, 256 * pair:256 * pair + 256], (((1,), (1,)), ((), ())),
-                preferred_element_type=jnp.float32,
+                spread, colloid.astype(jnp.bfloat16), (((1,), (1,)), ((), ())), preferred_element_type=jnp.float32
             )
-        sums_ref[:, 0:SLOTS] += total[0:8] + total[8:16]
-
-    fetch(0, 0).start()
-    fetch(1, 1).start()
-    fetch(0, 0).wait()
-    gather(0, 0)
+        return total
+
+    for k in range(RING):
+        fetch(k, k).start()
 
     def ring(i, _):
-        @pl.when(i < CHUNKS // 2 - 1)
+        first = i * RING
+        for k in range(RING):
+            fetch(first + k, k).wait()
+        for k in range(RING):
+            gather(first + k, k)
+
+        @pl.when(i < CHUNKS // RING - 1)
         def _():
-            fetch(2 * i + 2, 0).start()
-        fetch(2 * i + 1, 1).wait()
-        gather(2 * i + 1, 1)
-        add(2 * i, 0)
-
-        @pl.when(i < CHUNKS // 2 - 1)
-        def _():
-            fetch(2 * i + 3, 1).start()
-            fetch(2 * i + 2, 0).wait()
-        gather(lax.rem(2 * i + 2, CHUNKS), 0)
-        add(2 * i + 1, 1)
-        return 0
-
-    lax.fori_loop(0, CHUNKS // 2, ring, 0)
+            for k in range(RING):
+                fetch(first + RING + k, k).start()
+        for k in range(RING):
+            place(first + k, k)
+        for k in range(RING):
+            found_at(table, slots_refs[k], 0, at_refs[k])
+        for k in range(RING):
+            terms_of(first + k, k)
+        total = jnp.zeros((144, NC_DEV), jnp.float32)
+        for k in range(RING):
+            total = summed(k, total)
+        sums_ref[:, 0:NC_DEV] += total
+        return 0
+
+    lax.fori_loop(0, CHUNKS // RING, ring, 0)
 
     row = lax.broadcasted_iota(jnp.int32, (8, 128), 0)
     for t in range(9):
-        value = sums_ref[:, 128 * (t // 4):128 * (t // 4) + 128]
-        if t % 4:
-            value = pltpu.roll(value, 128 - NC_DEV * (t % 4), 1)
-        part_ref[t] = jnp.where(lane < NC_DEV, value, 0.0)
+        part_ref[t] = sums_ref[16 * t:16 * t + 8, :] + sums_ref[16 * t + 8:16 * t + 16, :]
     greeted()
     for t, _ in beside():
         mail.send(t, part_ref.at[t], got_ref.at[8 - t])
@@ -572,20 +586,20 @@
         mail.send(t, new_ref, back_ref.at[8 - t])
     report_ref[...] = jnp.where(row < 3, total, total / RADIUS)
     mail.wait()
-    write_table(moved_ref, lambda t: new_ref[...] if t == 4 else back_ref[t])
-    moved = split(moved_ref[...])[:, 0:SLOTS]
-
-    def group(b, _):
-        rows = pl.ds(pl.multiple_of(b * 8, 8), 8)
-        for pair in range(4):
-            found_at(moved, onehot_ref[b, :, 256 * pair:256 * pair + 256], pair, at_ref)
-        value = pop_ref[rows, :]
-        for i in range(6):
-            value = value - gain_ref[i, rows, :] * at_ref[pl.ds(i, 8, stride=8), :]
-        out_ref[rows, :] = value
-        return 0
-
-    lax.fori_loop(0, CHUNKS, group, 0)
+    moved = block_table(lambda t: new_ref[...] if t == 4 else back_ref[t])
+
+    def group(i, _):
+        for k in range(FINAL):
+            found_at(moved, slot_ref, pl.multiple_of((i * FINAL + k) * 8, 8), at_refs[k])
+        for k in range(FINAL):
+            rows = pl.ds(pl.multiple_of((i * FINAL + k) * 8, 8), 8)
+            value = pop_ref[rows, :]
+            for j in range(6):
+                value = value - gain_ref[j, rows, :] * at_refs[k][pl.ds(j, 8, stride=8), :]
+            out_ref[rows, :] = value
+        return 0
+
+    lax.fori_loop(0, CHUNKS // FINAL, group, 0)
 
 
 VM = pl.BlockSpec(memory_space=pltpu.VMEM)
@@ -593,7 +607,6 @@
 
 def links(row, site, direction, ids, pop, rb, q, table, motion):
     small = pltpu.VMEM((9, 8, 128), jnp.float32)
-    wide = pltpu.VMEM((8, SLOTS_PAD), jnp.float32)
     column = pltpu.VMEM((64, 128), jnp.float32)
     return pl.pallas_call(
         links_kernel,
@@ -601,11 +614,11 @@
         out_specs=(VM, VM),
         out_shape=(jax.ShapeDtypeStruct((8, 128), jnp.float32), jax.ShapeDtypeStruct((LINKS // 128, 128), jnp.float32)),
         scratch_shapes=[
-            pltpu.VMEM((8, 128), jnp.int32), pltpu.VMEM((6, LINKS // 128, 128), jnp.float32), wide,
-            pltpu.VMEM((CHUNKS, SLOTS, CHUNK), jnp.bfloat16), column, column,
-            [pltpu.VMEM((8, 128), jnp.float32)] * 2, [pltpu.SMEM((CHUNK,), jnp.int32)] * 2,
-            small, small, pltpu.VMEM((8, 128), jnp.float32), small, wide,
-            pltpu.SemaphoreType.DMA((2,)), pltpu.SemaphoreType.DMA((16,)), pltpu.SemaphoreType.DMA((16,)),
+            pltpu.VMEM((LINKS // 128, 128), jnp.int32), [pltpu.VMEM((8, 128), jnp.int32)] * RING, pltpu.VMEM((6, LINKS // 128, 128), jnp.float32),
+            pltpu.VMEM((144, 128), jnp.float32), [column] * max(RING, FINAL), [column] * RING,
+            [pltpu.VMEM((8, 128), jnp.float32)] * RING, [pltpu.SMEM((CHUNK,), jnp.int32)] * RING,
+            small, small, pltpu.VMEM((8, 128), jnp.float32), small,
+            pltpu.SemaphoreType.DMA((RING,)), pltpu.SemaphoreType.DMA((16,)), pltpu.SemaphoreType.DMA((16,)),
         ],
         name="links",
         compiler_params=pltpu.CompilerParams(vmem_limit_bytes=40 * 2**20, collective_id=1, has_side_effects=True),

time: 120 us -> 107 us (0.89)
  Pallas kernels: 113 us -> 100 us
    pallas_call x1, Pallas kernels: 52.7 us -> 39.5 us  [links(): pl.pallas_call(links_kernel, in_specs=[pl.BlockSpec(memory_space=pl.ANY)]...]
where the time goes in v6:
time: 107 us
  Pallas kernels  100 us (93%)
  local copies, waits for them, and re-layouts  4.6 us (4%)
  other arithmetic  1.51 us (1%)
    pallas_call x1, Pallas kernels, relax(): pl.pallas_call(relax_kernel, out_shape=(jax.ShapeDtypeStruct((NZ, TX, TY)...  60.5 us
    pallas_call x1, Pallas kernels, links(): pl.pallas_call(links_kernel, in_specs=[pl.BlockSpec(memory_space=pl.ANY)]...  39.5 us
    unnamed x25, local copies, waits for them, and re-layouts  4.6 us

profile of v6, /device:TPU:0, one launch (start us, length us, event | category | flops | bytes accessed | tf_op | source)
XLA Modules:
  0.0 107.0 jit_solution(15299558501283194494)
XLA Ops:
  0.6 1.3 %select_maximum_fusion.motion_ref = f32[8,128]{1,0:T(8,128)} fusion(f32[3,32]{1,0:T(4,128)} %param.16, f32[3,32]{1,0:T(4,128)} %param.15), kind=kLoop, calls=%fused_computation.1 | loop fusion | flops 8192 | bytes 4864 | tf_op jit(solution)/shard_map/concatenate | solution.py:633
  1.9 0.0 copy-start.1
  1.9 0.0 copy-start.4
  2.0 0.0 copy-start.5
  2.0 0.0 copy-start.6
  2.0 0.0 copy-start.8
  2.0 60.5 %relax.1 = (f32[48,64,128]{2,1,0:T(8,128)}, f32[48,64,128]{2,1,0:T(8,128)}, f32[72,128]{1,0:T(8,128)}) custom-call(bf16[48,64,128]{2,1,0:T(8,128)(2,1)} %eps_ref.1, f32[48,64,128]{2,1,0:T(8,128)} %charge_ref.1, f32[48,64,128]{2,1,0:T(8,128)} %phi_ref.1, f32[8,128]{1,0:T(8,128)} %select_maximum_fusion.motion_ref), custom_call_target="tpu_custom_call" | custom-call | tf_op jit(solution)/shard_map/relax/pallas_call | solution.py:380
  62.5 0.0 copy-done.1
  62.6 0.0 copy-done.10
  62.6 0.2 shift-right-arithmetic_add_fusion
  62.8 0.0 copy-done.2
  62.8 0.0 copy-done.3
  62.8 0.0 copy-done.4
  62.8 0.0 copy-done.5
  62.8 0.0 copy-done.6
  62.8 0.0 copy-done.8
  62.8 0.0 copy-start
  62.8 1.4 %copy-done = f32[48,64,128]{2,1,0:T(8,128)S(1)} copy-done((f32[48,64,128]{2,1,0:T(8,128)S(1)}, f32[48,64,128]{2,1,0:T(8,128)}, u32[]{:S(2)}) %copy-start) | copy-done | bytes 1572888
  64.2 0.8 copy-done.7
  65.0 39.5 %links.1 = (f32[8,128]{1,0:T(8,128)S(1)}, f32[256,128]{1,0:T(8,128)S(1)}) custom-call(s32[32768]{0:T(1024)S(1)} %bitcast.11, s32[256,128]{1,0:T(8,128)S(1)} %bitcast.10, s32[256,128]{1,0:T(8,128)S(1)} %bitcast.14, s32[256,128]{1,0:T(8,128)S(1)} %bitcast.15, f32[256,128]{1,0:T(8,128)S(1)} %bitcast.16, f32[3,256,128]{2,1,0:T(8,128)S(1)} %bitcast.12, ...), custom_call_target="tpu_custom_call" | custom-call | tf_op jit(solution)/shard_map/links/pallas_call | solution.py:611
  104.6 0.0 copy-done.9
  104.6 1.1 %copy.18 = f32[48,64,128]{2,1,0:T(8,128)} copy(f32[48,64,128]{2,1,0:T(8,128)S(1)} %copy-done.9) | data formatting | bytes 3145728
  105.7 0.6 copy.19
  106.3 0.7 copy.20
  (5 shorter events, 0.0 us)
Async XLA Ops:
  1.9 60.6 %copy-start.1 = (s32[1,1,32768]{2,1,0:T(1,128)S(1)}, s32[1,1,32768]{2,1,0:T(1,128)}, u32[]{:S(2)}) copy-start(s32[1,1,32768]{2,1,0:T(1,128)} %param.19) | copy-start | bytes 393220
  1.9 60.6 %copy-start.10 = (s32[1,1,32768]{2,1,0:T(1,128)S(1)}, s32[1,1,32768]{2,1,0:T(1,128)}, u32[]{:S(2)}) copy-start(s32[1,1,32768]{2,1,0:T(1,128)} %param.20) | copy-start | bytes 393220
  1.9 60.8 %copy-start.2 = (f32[3,1,1,32768]{3,2,1,0:T(1,128)S(1)}, f32[3,1,1,32768]{3,2,1,0:T(1,128)}, u32[]{:S(2)}) copy-start(f32[3,1,1,32768]{3,2,1,0:T(1,128)} %param.22) | copy-start | bytes 1179652
  1.9 60.9 %copy-start.3 = (s32[1,1,32768]{2,1,0:T(1,128)S(1)}, s32[1,1,32768]{2,1,0:T(1,128)}, u32[]{:S(2)}) copy-start(s32[1,1,32768]{2,1,0:T(1,128)} %param.17) | copy-start | bytes 393220
  1.9 60.9 %copy-start.4 = (s32[1,1,32768]{2,1,0:T(1,128)S(1)}, s32[1,1,32768]{2,1,0:T(1,128)}, u32[]{:S(2)}) copy-start(s32[1,1,32768]{2,1,0:T(1,128)} %param.18) | copy-start | bytes 393220
  2.0 60.9 %copy-start.5 = (f32[1,1,32768]{2,1,0:T(1,128)S(1)}, f32[1,1,32768]{2,1,0:T(1,128)}, u32[]{:S(2)}) copy-start(f32[1,1,32768]{2,1,0:T(1,128)} %param.21) | copy-start | bytes 393220
  2.0 60.9 %copy-start.6 = (f32[8,128]{1,0:T(8,128)S(1)}, f32[8,128]{1,0:T(8,128)}, u32[]{:S(2)}) copy-start(f32[8,128]{1,0:T(8,128)} %select_maximum_fusion.motion_ref) | copy-start | bytes 12292
  2.0 60.9 %copy-start.8 = (f32[32,128]{1,0:T(8,128)S(1)}, f32[32,128]{1,0:T(8,128)}, u32[]{:S(2)}) copy-start(f32[32,128]{1,0:T(8,128)} %constant.9.clone.lat_ref) | copy-start | bytes 49156
  62.8 1.4 %copy-start = (f32[48,64,128]{2,1,0:T(8,128)S(1)}, f32[48,64,128]{2,1,0:T(8,128)}, u32[]{:S(2)}) copy-start(f32[48,64,128]{2,1,0:T(8,128)} %get-tuple-element.9) | copy-start | bytes 4718596
  64.2 0.8 copy-start.7
  65.0 39.6 %copy-start.9 = (f32[48,64,128]{2,1,0:T(8,128)S(1)}, f32[48,64,128]{2,1,0:T(8,128)}, u32[]{:S(2)}) copy-start(f32[48,64,128]{2,1,0:T(8,128)} %get-tuple-element.16) | copy-start | bytes 4718596

commit v7 on v6

--- a/solution.py
+++ b/solution.py
@@ -62,10 +62,10 @@
 
 
 def relax_kernel(
-    eps_ref, charge_ref, phi_ref, motion_ref, pot_ref, q_ref, table_ref,
+    eps_ref, charge_ref, phi_ref, vel_ref, spin_ref, pot_ref, q_ref, table_ref,
     p_refs, e_refs, ps_refs, es_refs, gs_refs, seam_refs, c_refs, coef_refs, cs_refs, coefs_refs,
     to_low, to_high, from_low, from_high, x_eps, x_charge, x_phi, to2_low, to2_high, from2_low, from2_high, x2_refs,
-    got_ref, send_sem, recv_sem,
+    motion_ref, got_ref, send_sem, recv_sem,
 ):
     sub = lax.broadcasted_iota(jnp.int32, (8, 128), 0)
     lane = lax.broadcasted_iota(jnp.int32, (8, 128), 1)
@@ -111,6 +111,9 @@
         mail.send(1, ref.at[:, pl.ds(0, rows), :], target.at[1])
         mail.send(7, ref.at[:, pl.ds(TX - rows, rows), :], target.at[0])
 
+    motion_ref[...] = zero
+    motion_ref[0:3, 0:NC_DEV] = vel_ref[...]
+    motion_ref[3:6, 0:NC_DEV] = spin_ref[...]
     pack(natural(eps_ref), to_low, to_high, GROUPS)
     greeted()
     send_sides(to_low, to_high, from_low, from_high, GROUPS)
@@ -374,7 +377,7 @@
     lax.fori_loop(0, HALF, out, 0)
 
 
-def relax(eps, charge, phi, motion):
+def relax(eps, charge, phi, vel, spin):
     vm = lambda *s: pltpu.VMEM(s, jnp.float32)
     spec = pl.BlockSpec(memory_space=pltpu.VMEM)
     return pl.pallas_call(
@@ -384,7 +387,7 @@
             jax.ShapeDtypeStruct((NZ, TX, TY), jnp.float32),
             jax.ShapeDtypeStruct((72, 128), jnp.float32),
         ),
-        in_specs=[spec] * 4,
+        in_specs=[spec] * 5,
         out_specs=(spec,) * 3,
         scratch_shapes=[
             [vm(HALF + 2, ROWS, 128)] * 2,
@@ -403,17 +406,17 @@
             vm(GROUPS, TX, 128), vm(GROUPS, TX, 128),
             vm(GROUPS, TX + 16, 128), vm(GROUPS, TX + 16, 128),
             [vm(2, HALF, 8, 128)] * 2,
-            vm(9, 8, 128),
+            vm(8, 128), vm(9, 8, 128),
             pltpu.SemaphoreType.DMA((42,)), pltpu.SemaphoreType.DMA((42,)),
         ],
         name="relax",
         compiler_params=pltpu.CompilerParams(vmem_limit_bytes=58 * 2**20, collective_id=0, has_side_effects=True),
-    )(eps, charge, phi, motion)
+    )(eps, charge, phi, vel, spin)
 
 
 CHUNK = 1024
 CHUNKS = LINKS // CHUNK
-RING = 4
+RING = 8
 FINAL = 8
 VELOCITY = np.array(
     [[1, 0, 0], [-1, 0, 0], [0, 1, 0], [0, -1, 0], [0, 0, 1], [0, 0, -1], [1, 1, 0], [1, -1, 0], [-1, 1, 0],
@@ -471,7 +474,7 @@
 
 
 def links_kernel(
-    row_ref, site_ref, dir_ref, ids_ref, pop_ref, rb_ref, q_ref, table_ref, lat_ref, motion_ref, report_ref, out_ref,
+    row_ref, site_ref, dir_ref, ids_ref, pop_ref, rb_ref, q_ref, table_ref, lat_ref, report_ref, out_ref,
     slot_ref, slots_refs, gain_ref, sums_ref, at_refs, term_refs, press_refs, index_refs,
     part_ref, got_ref, new_ref, back_ref, index_sem, send_sem, recv_sem,
 ):
@@ -581,7 +584,7 @@
             total = total + got_ref[t]
     mass = 4.0 / 3.0 * math.pi * RADIUS**3
     inertia = 0.4 * mass * RADIUS**2
-    new_ref[...] = motion_ref[...] + jnp.where(row < 3, total / mass, total / inertia)
+    new_ref[...] = table_ref[32:40, :] + jnp.where(row < 3, total / mass, total / inertia)
     for t, _ in beside():
         mail.send(t, new_ref, back_ref.at[8 - t])
     report_ref[...] = jnp.where(row < 3, total, total / RADIUS)
@@ -605,12 +608,12 @@
 VM = pl.BlockSpec(memory_space=pltpu.VMEM)
 
 
-def links(row, site, direction, ids, pop, rb, q, table, motion):
+def links(row, site, direction, ids, pop, rb, q, table):
     small = pltpu.VMEM((9, 8, 128), jnp.float32)
     column = pltpu.VMEM((64, 128), jnp.float32)
     return pl.pallas_call(
         links_kernel,
-        in_specs=[pl.BlockSpec(memory_space=pl.ANY)] + [VM] * 9,
+        in_specs=[pl.BlockSpec(memory_space=pl.ANY)] + [VM] * 8,
         out_specs=(VM, VM),
         out_shape=(jax.ShapeDtypeStruct((8, 128), jnp.float32), jax.ShapeDtypeStruct((LINKS // 128, 128), jnp.float32)),
         scratch_shapes=[
@@ -622,7 +625,7 @@
         ],
         name="links",
         compiler_params=pltpu.CompilerParams(vmem_limit_bytes=40 * 2**20, collective_id=1, has_side_effects=True),
-    )(row, site, direction, ids, pop, rb, q, table, lattice_table(), motion)
+    )(row, site, direction, ids, pop, rb, q, table, lattice_table())
 
 
 def shards(
@@ -630,12 +633,11 @@
     link_pop, link_rb,
 ):
     flat = lambda a: a.reshape(LINKS // 128, 128)
-    motion = jnp.pad(jnp.concatenate([colloid_vel, colloid_spin], axis=0), ((0, 2), (0, 128 - NC_DEV)))
-    potential, q, table = relax(eps_field, charge, potential_start, motion)
+    potential, q, table = relax(eps_field, charge, potential_start, colloid_vel, colloid_spin)
     row = link_depth.reshape(-1) * TX + (link_site.reshape(-1) >> 7)
     rb = link_rb.reshape(3, LINKS // 128, 128)
     report, link_out = links(
-        row, flat(link_site), flat(link_dir), flat(link_colloid), flat(link_pop), rb, q.reshape(NZ * TX, TY), table, motion
+        row, flat(link_site), flat(link_dir), flat(link_colloid), flat(link_pop), rb, q.reshape(NZ * TX, TY), table
     )
     link_out = link_out.reshape(link_pop.shape)
     return potential, report[0:6, 0:NC_DEV], link_out

time: 107 us -> 104 us (0.972)
  Pallas kernels: 100 us -> 97.7 us
  other arithmetic: 1.51 us -> 0.21 us
    pallas_call x1, Pallas kernels: 39.5 us -> 37.1 us  [links(): pl.pallas_call(links_kernel, in_specs=[pl.BlockSpec(memory_space=pl.ANY)]...]
    concatenate x1 -> x0, other arithmetic: 1.3 us -> none  [shards(): jnp.concatenate([colloid_vel, colloid_spin], axis=0)]
    unnamed x25 -> x23, local copies, waits for them, and re-layouts: 4.6 us -> 4.6 us
where the time goes in v7:
time: 104 us; the launch traced here: 103 us
  Pallas kernels  97.7 us (94%)
  local copies, waits for them, and re-layouts  4.6 us (4%)
    pallas_call x1, Pallas kernels, relax(): pl.pallas_call(relax_kernel, out_shape=(jax.ShapeDtypeStruct((NZ, TX, TY)...  60.6 us
    pallas_call x1, Pallas kernels, links(): pl.pallas_call(links_kernel, in_specs=[pl.BlockSpec(memory_space=pl.ANY)]...  37.1 us
    unnamed x23, local copies, waits for them, and re-layouts  4.6 us

profile of v7, /device:TPU:0, one launch (start us, length us, event | category | flops | bytes accessed | tf_op | source)
XLA Modules:
  0.0 103.3 jit_solution(11330159517305857528)
XLA Ops:
  0.6 0.0 copy-start.7
  0.6 0.0 copy-start.1
  0.7 0.0 copy-start.9
  0.7 0.0 copy-start.3
  0.7 0.0 copy-start.4
  0.7 0.0 copy-start.5
  0.7 0.0 copy-start.2
  0.7 60.6 %relax.1 = (f32[48,64,128]{2,1,0:T(8,128)}, f32[48,64,128]{2,1,0:T(8,128)}, f32[72,128]{1,0:T(8,128)}) custom-call(bf16[48,64,128]{2,1,0:T(8,128)(2,1)} %eps_ref.1, f32[48,64,128]{2,1,0:T(8,128)} %charge_ref.1, f32[48,64,128]{2,1,0:T(8,128)} %phi_ref.1, f32[3,32]{1,0:T(4,128)} %vel_ref.1, f32[3,32]{1,0:T(4,128)} %spin_ref.1), custom_call_target="tpu_custom_call" | custom-call | tf_op jit(solution)/shard_map/relax/pallas_call | solution.py:383
  61.4 0.0 copy-done.1
  61.4 0.0 copy-done.9
  61.4 0.2 shift-right-arithmetic_add_fusion
  61.6 0.0 copy-done.7
  61.6 0.0 copy-done.3
  61.6 0.0 copy-done.4
  61.6 0.0 copy-done.5
  61.6 0.0 copy-done.2
  61.6 0.0 copy-start
  61.7 1.4 %copy-done = f32[48,64,128]{2,1,0:T(8,128)S(1)} copy-done((f32[48,64,128]{2,1,0:T(8,128)S(1)}, f32[48,64,128]{2,1,0:T(8,128)}, u32[]{:S(2)}) %copy-start) | copy-done | bytes 1572888
  63.1 0.8 copy-done.6
  63.8 37.1 %links.1 = (f32[8,128]{1,0:T(8,128)S(1)}, f32[256,128]{1,0:T(8,128)S(1)}) custom-call(s32[32768]{0:T(1024)S(1)} %bitcast.11, s32[256,128]{1,0:T(8,128)S(1)} %bitcast.10, s32[256,128]{1,0:T(8,128)S(1)} %bitcast.14, s32[256,128]{1,0:T(8,128)S(1)} %bitcast.15, f32[256,128]{1,0:T(8,128)S(1)} %bitcast.16, f32[3,256,128]{2,1,0:T(8,128)S(1)} %bitcast.12, ...), custom_call_target="tpu_custom_call" | custom-call | tf_op jit(solution)/shard_map/links/pallas_call | solution.py:614
  100.9 0.0 copy-done.8
  100.9 1.1 %copy.18 = f32[48,64,128]{2,1,0:T(8,128)} copy(f32[48,64,128]{2,1,0:T(8,128)S(1)} %copy-done.8) | data formatting | bytes 3145728
  102.0 0.6 copy.19
  102.6 0.7 copy.20
  (2 shorter events, 0.0 us)
Async XLA Ops:
  0.6 61.0 %copy-start.7 = (f32[32,128]{1,0:T(8,128)S(1)}, f32[32,128]{1,0:T(8,128)}, u32[]{:S(2)}) copy-start(f32[32,128]{1,0:T(8,128)} %constant.6.clone.lat_ref) | copy-start | bytes 49156
  0.6 60.7 %copy-start.1 = (s32[1,1,32768]{2,1,0:T(1,128)S(1)}, s32[1,1,32768]{2,1,0:T(1,128)}, u32[]{:S(2)}) copy-start(s32[1,1,32768]{2,1,0:T(1,128)} %param.19) | copy-start | bytes 393220
  0.7 60.7 %copy-start.9 = (s32[1,1,32768]{2,1,0:T(1,128)S(1)}, s32[1,1,32768]{2,1,0:T(1,128)}, u32[]{:S(2)}) copy-start(s32[1,1,32768]{2,1,0:T(1,128)} %param.20) | copy-start | bytes 393220
  0.7 60.9 %copy-start.3 = (s32[1,1,32768]{2,1,0:T(1,128)S(1)}, s32[1,1,32768]{2,1,0:T(1,128)}, u32[]{:S(2)}) copy-start(s32[1,1,32768]{2,1,0:T(1,128)} %param.17) | copy-start | bytes 393220
  0.7 60.9 %copy-start.4 = (s32[1,1,32768]{2,1,0:T(1,128)S(1)}, s32[1,1,32768]{2,1,0:T(1,128)}, u32[]{:S(2)}) copy-start(s32[1,1,32768]{2,1,0:T(1,128)} %param.18) | copy-start | bytes 393220
  0.7 60.9 %copy-start.5 = (f32[1,1,32768]{2,1,0:T(1,128)S(1)}, f32[1,1,32768]{2,1,0:T(1,128)}, u32[]{:S(2)}) copy-start(f32[1,1,32768]{2,1,0:T(1,128)} %param.21) | copy-start | bytes 393220
  0.7 60.9 %copy-start.2 = (f32[3,1,1,32768]{3,2,1,0:T(1,128)S(1)}, f32[3,1,1,32768]{3,2,1,0:T(1,128)}, u32[]{:S(2)}) copy-start(f32[3,1,1,32768]{3,2,1,0:T(1,128)} %param.22) | copy-start | bytes 1179652
  61.6 1.4 %copy-start = (f32[48,64,128]{2,1,0:T(8,128)S(1)}, f32[48,64,128]{2,1,0:T(8,128)}, u32[]{:S(2)}) copy-start(f32[48,64,128]{2,1,0:T(8,128)} %get-tuple-element.9) | copy-start | bytes 4718596
  63.1 0.8 copy-start.6
  63.8 37.1 %copy-start.8 = (f32[48,64,128]{2,1,0:T(8,128)S(1)}, f32[48,64,128]{2,1,0:T(8,128)}, u32[]{:S(2)}) copy-start(f32[48,64,128]{2,1,0:T(8,128)} %get-tuple-element.16) | copy-start | bytes 4718596
